TPU v7x, 32 devices: a whole 2x2x4 slice. The times are simulated.
32 devices in a mesh: grp: 4 (over y, x), blk: 8 (over z, core).
Axes of the slice: x: 2, y: 2, z: 4, core: 2. Of those that a mesh axis runs over, the one named last changes fastest.
Arguments:
- feats: bfloat16 [32768, 256], P(('grp', 'blk')), may hold values from -6 to 6
- weight: bfloat16 [256, 256], replicated, may hold values from -0.375 to 0.375
- cotangent: bfloat16 [32768, 256], P(('grp', 'blk')), may hold values from -6 to 6
- labels: int32 [32768], P(('grp', 'blk')), may hold values from -86 to 171
- tile_vals: bfloat16 [4, 8, 8, 32, 128, 128], P('grp', 'blk'), may hold values from -0.09375 to 0.09375
- tile_row: int32 [4, 8, 8, 32], P('grp', 'blk'), may hold values from 0 to 7
- tile_col: int32 [4, 8, 8, 32], P('grp', 'blk'), may hold values from 0 to 7
- tile_count: int32 [4, 8, 8], P('grp', 'blk'), may hold values from 1 to 32, as said below
- hub_vals: bfloat16 [4, 8, 16, 128, 128], P('grp', 'blk'), may hold values from -0.09375 to 0.09375
- hub_col: int32 [4, 8, 16], P('grp', 'blk'), may hold values from 0 to 7
- hub_dest: int32 [4, 8, 16, 1], P(None, 'blk'), may hold values from 0 to 3; in each aligned block of 16 rows (0 to 15, 16 to 31, ..., all dimensions but the last counted through in order) at most 4 rows name the same one
- hub_row: int32 [4, 8, 16], P(None, 'blk'), may hold values from 0 to 7
Outputs:
- layer_out: bfloat16 [32768, 256], P(('grp', 'blk'))
- grad_feats: bfloat16 [32768, 256], P(('grp', 'blk'))
- grad_weight: float32 [256, 256], replicated
Inputs may be any that keep to these rules, and one draw needn't show every extreme that they name: Only the first tile_count slots of a device's list for a source block are used; some device uses all 32. `hub_dest`: at most 4 of the 16 hub tiles of one device name the same group, and exactly 4 in some devices.
All inputs are finite; a program needn't handle non-finite values.
Results may differ from a plain program's by a relative error of at most 0.007.
Values may be sent and summed in bfloat16 or wider, within the bound.
No kernel may reach another device: no remote copies, remote signals or barrier semaphores. Data moves between devices by JAX's collectives and lax.ppermute only.
A program may use at most 192 MiB of HBM per device.

v0:
```python
import math

import jax
import jax.numpy as jnp
from jax import lax
from jax.sharding import PartitionSpec as P


def shifted(value, axis, by):
    size = lax.axis_size(axis)
    return lax.ppermute(value, axis, [(i, (i + by) % size) for i in range(size)])


def local(
    feats,
    weight,
    cotangent,
    labels,
    tile_vals,
    tile_row,
    tile_col,
    tile_count,
    hub_vals,
    hub_col,
    hub_dest,
    hub_row,
):
    n_blocks = lax.axis_size("blk")
    n_groups = lax.axis_size("grp")
    my_block = lax.axis_index("blk")
    my_group = lax.axis_index("grp")
    rows_dev = feats.shape[0]
    width = feats.shape[1]
    tile_size = tile_vals.shape[-1]
    row_tiles = rows_dev // tile_size
    slot_count = tile_vals.shape[3]
    hub_count = hub_vals.shape[2]
    capacity = max(2, hub_count // 4)
    highest = lax.Precision.HIGHEST
    dev_vals = tile_vals[0, 0]
    dev_rows = tile_row[0, 0]
    dev_cols = tile_col[0, 0]
    dev_count = tile_count[0, 0]
    tile_range = jnp.arange(row_tiles, dtype=jnp.int32)
    slot_range = jnp.arange(slot_count, dtype=jnp.int32)
    proj = jnp.dot(feats, weight, preferred_element_type=jnp.float32).astype(jnp.bfloat16)
    own_panel = proj.reshape(row_tiles, tile_size, width)

    def block_parts(source):
        blk_vals = lax.dynamic_index_in_dim(dev_vals, source, 0, keepdims=False)
        blk_rows = lax.dynamic_index_in_dim(dev_rows, source, 0, keepdims=False)
        blk_cols = lax.dynamic_index_in_dim(dev_cols, source, 0, keepdims=False)
        blk_count = lax.dynamic_index_in_dim(dev_count, source, 0, keepdims=False)
        live_mask = (slot_range < blk_count).astype(jnp.float32)
        return (blk_vals, blk_rows, blk_cols, live_mask)

    def forward_block(source, panel_now):
        blk_vals, blk_rows, blk_cols, live_mask = block_parts(source)
        picked = jnp.take(panel_now, blk_cols, axis=0)
        product = jnp.einsum("tij,tjf->tif", blk_vals, picked, preferred_element_type=jnp.float32)
        placing = (blk_rows[:, None] == tile_range[None, :]).astype(jnp.float32) * live_mask[
            :, None
        ]
        return jnp.einsum("tr,tif->rif", placing, product, precision=highest)

    def backward_block(target, grad_tiles):
        blk_vals, blk_rows, blk_cols, live_mask = block_parts(target)
        picked = jnp.take(grad_tiles, blk_rows, axis=0)
        product = jnp.einsum("tij,tif->tjf", blk_vals, picked, preferred_element_type=jnp.float32)
        placing = (blk_cols[:, None] == tile_range[None, :]).astype(jnp.float32) * live_mask[
            :, None
        ]
        return jnp.einsum("tr,tjf->rjf", placing, product, precision=highest)

    agg_sum = forward_block(my_block, own_panel)

    def forward_turn(k, carry):
        panel_now, running = carry
        panel_now = shifted(panel_now, "blk", 1)
        source = (my_block - k) % n_blocks
        return (panel_now, running + forward_block(source, panel_now))

    _, agg_sum = lax.fori_loop(1, n_blocks, forward_turn, (own_panel, agg_sum))
    dest_all = hub_dest[:, 0, :, 0]
    hub_rows_all = hub_row[:, 0, :]
    hub_range = jnp.arange(hub_count, dtype=jnp.int32)
    earlier = hub_range[None, :] < hub_range[:, None]
    same_dest = dest_all[:, :, None] == dest_all[:, None, :]
    rank_all = jnp.sum((same_dest & earlier[None, :, :]).astype(jnp.int32), axis=-1)
    my_dest = lax.dynamic_index_in_dim(dest_all, my_group, 0, keepdims=False)
    my_rank = lax.dynamic_index_in_dim(rank_all, my_group, 0, keepdims=False)
    slot_of = my_dest * capacity + my_rank
    send_place = (
        slot_of[:, None] == jnp.arange(n_groups * capacity, dtype=jnp.int32)[None, :]
    ).astype(jnp.float32)
    hub_tiles = hub_vals[0, 0]
    hub_cols = hub_col[0, 0]
    hub_src = jnp.take(own_panel, hub_cols, axis=0)
    hub_part = jnp.einsum("hij,hjf->hif", hub_tiles, hub_src, preferred_element_type=jnp.float32)
    send_buf = jnp.einsum("hs,hif->sif", send_place, hub_part, precision=highest)
    send_buf = send_buf.reshape(n_groups, capacity, tile_size, width)
    received = lax.all_to_all(send_buf, "grp", split_axis=0, concat_axis=0, tiled=True)
    chosen = (dest_all == my_group).astype(jnp.float32)
    slot_hot = (rank_all[..., None] == jnp.arange(capacity, dtype=jnp.int32)).astype(
        jnp.float32
    ) * chosen[..., None]
    row_hot = (hub_rows_all[..., None] == tile_range).astype(jnp.float32)
    routing = jnp.einsum("shc,shr->scr", slot_hot, row_hot, precision=highest)
    agg_sum = agg_sum + jnp.einsum("scr,scif->rif", routing, received, precision=highest)
    agg_rows = agg_sum.reshape(rows_dev, width)
    layer_out = jax.nn.silu(agg_rows).astype(jnp.bfloat16)
    sigmoid_z = jax.nn.sigmoid(agg_rows)
    slope = sigmoid_z * (1.0 + agg_rows * (1.0 - sigmoid_z))
    keep = (labels >= 0).astype(jnp.float32)[:, None]
    grad_agg = (cotangent.astype(jnp.float32) * keep * slope).astype(jnp.bfloat16)
    grad_tiles = grad_agg.reshape(row_tiles, tile_size, width)
    grad_sum = backward_block((my_block + n_blocks - 1) % n_blocks, grad_tiles)

    def backward_turn(k, running):
        running = shifted(running, "blk", 1)
        return running + backward_block((my_block + n_blocks - 1 - k) % n_blocks, grad_tiles)

    grad_sum = lax.fori_loop(1, n_blocks, backward_turn, grad_sum)
    back_send = jnp.einsum(
        "scr,rif->scif",
        routing.astype(jnp.bfloat16),
        grad_tiles,
        preferred_element_type=jnp.float32,
    ).astype(jnp.bfloat16)
    back_recv = lax.all_to_all(back_send, "grp", split_axis=0, concat_axis=0, tiled=True)
    back_flat = back_recv.reshape(n_groups * capacity, tile_size, width)
    own_pick = jnp.einsum(
        "hs,sif->hif",
        send_place.astype(jnp.bfloat16),
        back_flat,
        preferred_element_type=jnp.float32,
    ).astype(jnp.bfloat16)
    hub_back = jnp.einsum("hij,hif->hjf", hub_tiles, own_pick, preferred_element_type=jnp.float32)
    col_hot = (hub_cols[:, None] == tile_range[None, :]).astype(jnp.float32)
    grad_sum = grad_sum + jnp.einsum("hr,hjf->rjf", col_hot, hub_back, precision=highest)
    grad_rows = grad_sum.reshape(rows_dev, width).astype(jnp.bfloat16)
    weight_term = lax.dot_general(
        feats, grad_rows, (((0,), (0,)), ((), ())), preferred_element_type=jnp.float32
    )
    grad_scale = 1.0 / math.sqrt(rows_dev * n_blocks * n_groups)
    grad_weight = lax.psum(weight_term, ("grp", "blk")) * grad_scale
    grad_feats = lax.dot_general(
        grad_rows, weight, (((1,), (1,)), ((), ())), preferred_element_type=jnp.float32
    ).astype(jnp.bfloat16)
    return (layer_out, grad_feats, grad_weight)


def solution(mesh):
    in_specs = (
        P(("grp", "blk"), None),
        P(),
        P(("grp", "blk"), None),
        P(("grp", "blk")),
        P("grp", "blk", None, None, None, None),
        P("grp", "blk", None, None),
        P("grp", "blk", None, None),
        P("grp", "blk", None),
        P("grp", "blk", None, None, None),
        P("grp", "blk", None),
        P(None, "blk", None, None),
        P(None, "blk", None),
    )
    out_specs = (P(("grp", "blk"), None), P(("grp", "blk"), None), P())
    return jax.shard_map(local, mesh=mesh, in_specs=in_specs, out_specs=out_specs, check_vma=False)
```

profile of v0, /device:TPU:0, one launch (start us, length us, event | category | flops | bytes accessed | tf_op | source)
XLA Modules:
  0.0 508.8 jit_solution(9581815356164716633)
XLA Ops:
  8.6 1.3 convolution_convert_fusion.3
  10.6 1.9 convolution_bitcast_fusion.1
  12.4 3.1 copy.53
  15.8 4.1 fusion.90
  19.9 2.9 reshape.151
  22.7 3.3 copy.54
  26.0 5.3 %all-to-all-start = ((f32[4,4,128,256]{3,1,2,0:T(4,128)}), f32[4,4,128,256]{3,1,2,0:T(4,128)}, u32[]{:S(2)}, u32[]{:S(2)}) async-start(f32[4,4,128,256]{3,1,2,0:T(4,128)} %copy.54), calls=%async_computation | async-start | bytes 4194304 | tf_op jit(solution)/shard_map/all_to_all | solution.py:102
  31.4 2.0 gather_fusion.3
  35.0 2.7 fusion.56
  37.7 5.3 %fusion.52 = f32[8,128,256]{2,0,1:T(8,128)} fusion(f32[32,128,256]{2,1,0:T(8,128)S(1)} %fusion.56, f32[32]{0:T(128)S(1)} %compare_convert_fusion.5, s32[32]{0:T(128)S(1)} %fusion.116), kind=kOutput, calls=%fused_computation.63 | convolution fusion | flops 100663808 | bytes 5243136 | tf_op jit(solution)/shard_map/tr,tif->rif/dot_general | solution.py:64
  43.0 131.2 %while.34 = (s32[]{:T(128)}, bf16[8,128,256]{2,1,0:T(8,128)(2,1)S(1)}, f32[8,128,256]{2,0,1:T(8,128)}, s32[]{:T(128)}, s32[8,32]{1,0:T(8,128)S(1)}, /*index=5*/s...) while((s32[]{:T(128)}, ...), condition=%wide.region_1.3_spmd.clone, body=%wide.region_0.2_spmd.clone.sunk | while | flops 370411264 | bytes 29365836 | solution.py:83
  44.3 9.6 %collective-permute-done = bf16[8,128,256]{2,1,0:T(8,128)(2,1)S(1)} collective-permute-done((bf16[8,128,256]{2,1,0:T(8,128)(2,1)S(1)}, bf16[8,128,256]{2,1,0:T(8,128)(2,1)S(1)}, u32[]{:S(2)}, u32[]{:S(2)}) %collective-permute-start) | collective-permute-done | bytes 524320 | tf_op jit(solution)/shard_map/while/body/eval_jaxpr/ppermute | solution.py:11
  54.5 2.1 fusion.158
  56.7 4.5 fusion.160
  63.4 9.1 %collective-permute-done = bf16[8,128,256]{2,1,0:T(8,128)(2,1)S(1)} collective-permute-done((bf16[8,128,256]{2,1,0:T(8,128)(2,1)S(1)}, bf16[8,128,256]{2,1,0:T(8,128)(2,1)S(1)}, u32[]{:S(2)}, u32[]{:S(2)}) %collective-permute-start) | collective-permute-done | bytes 524320 | tf_op jit(solution)/shard_map/while/body/eval_jaxpr/ppermute | solution.py:11
  73.2 2.1 fusion.158
  75.3 4.5 fusion.160
  82.1 9.1 %collective-permute-done = bf16[8,128,256]{2,1,0:T(8,128)(2,1)S(1)} collective-permute-done((bf16[8,128,256]{2,1,0:T(8,128)(2,1)S(1)}, bf16[8,128,256]{2,1,0:T(8,128)(2,1)S(1)}, u32[]{:S(2)}, u32[]{:S(2)}) %collective-permute-start) | collective-permute-done | bytes 524320 | tf_op jit(solution)/shard_map/while/body/eval_jaxpr/ppermute | solution.py:11
  91.9 2.1 fusion.158
  94.0 4.5 fusion.160
  100.8 9.1 %collective-permute-done = bf16[8,128,256]{2,1,0:T(8,128)(2,1)S(1)} collective-permute-done((bf16[8,128,256]{2,1,0:T(8,128)(2,1)S(1)}, bf16[8,128,256]{2,1,0:T(8,128)(2,1)S(1)}, u32[]{:S(2)}, u32[]{:S(2)}) %collective-permute-start) | collective-permute-done | bytes 524320 | tf_op jit(solution)/shard_map/while/body/eval_jaxpr/ppermute | solution.py:11
  110.6 2.1 fusion.158
  112.7 4.5 fusion.160
  119.5 9.1 %collective-permute-done = bf16[8,128,256]{2,1,0:T(8,128)(2,1)S(1)} collective-permute-done((bf16[8,128,256]{2,1,0:T(8,128)(2,1)S(1)}, bf16[8,128,256]{2,1,0:T(8,128)(2,1)S(1)}, u32[]{:S(2)}, u32[]{:S(2)}) %collective-permute-start) | collective-permute-done | bytes 524320 | tf_op jit(solution)/shard_map/while/body/eval_jaxpr/ppermute | solution.py:11
  129.3 2.1 fusion.158
  131.4 4.5 fusion.160
  138.2 9.1 %collective-permute-done = bf16[8,128,256]{2,1,0:T(8,128)(2,1)S(1)} collective-permute-done((bf16[8,128,256]{2,1,0:T(8,128)(2,1)S(1)}, bf16[8,128,256]{2,1,0:T(8,128)(2,1)S(1)}, u32[]{:S(2)}, u32[]{:S(2)}) %collective-permute-start) | collective-permute-done | bytes 524320 | tf_op jit(solution)/shard_map/while/body/eval_jaxpr/ppermute | solution.py:11
  148.0 2.1 fusion.158
  150.1 4.5 fusion.160
  156.9 9.1 %collective-permute-done = bf16[8,128,256]{2,1,0:T(8,128)(2,1)S(1)} collective-permute-done((bf16[8,128,256]{2,1,0:T(8,128)(2,1)S(1)}, bf16[8,128,256]{2,1,0:T(8,128)(2,1)S(1)}, u32[]{:S(2)}, u32[]{:S(2)}) %collective-permute-start) | collective-permute-done | bytes 524320 | tf_op jit(solution)/shard_map/while/body/eval_jaxpr/ppermute | solution.py:11
  166.7 2.1 fusion.158
  168.8 4.5 fusion.160
  174.3 4.3 fusion.60
  180.9 1.6 convolution_convert_fusion
  182.5 4.2 all-to-all-start.1
  187.5 12.0 %copy.49 = bf16[1,1,8,32,128,128]{4,5,3,2,1,0:T(8,128)(2,1)} copy(bf16[1,1,8,32,128,128]{5,4,3,2,1,0:T(8,128)(2,1)} %bitcast.177) | data formatting | bytes 16777216 | tf_op args[4]
  200.1 2.0 fusion.54
  202.1 5.3 %fusion.50 = f32[8,128,256]{2,0,1:T(8,128)} fusion(f32[32,128,256]{2,1,0:T(8,128)S(1)} %fusion.54, f32[32]{0:T(128)S(1)} %compare_convert_fusion.3, s32[32]{0:T(128)S(1)} %fusion.122), kind=kOutput, calls=%fused_computation.61 | convolution fusion | flops 100663808 | bytes 5243136 | tf_op jit(solution)/shard_map/tr,tjf->rjf/dot_general | solution.py:73
  207.5 1.4 copy.60
  210.2 2.0 copy.63
  212.2 160.3 %while.35 = (s32[]{:T(128)}, f32[8,128,256]{2,0,1:T(8,128)}, s32[]{:T(128)}, s32[8,32]{1,0:T(8,128)S(1)}, s32[8]{0:T(128)S(1)}, /*index=5*/bf16[8,32,128,128]{2,...) while((s32[]{:T(128)}, f32[8,128,256]{2,0,1:T(8,128)}, ...), condition=%wide.region_4.6_spmd.clone, body=%wide.region_3.5_spmd.clone.sunk | while | flops 370411264 | bytes 22025748 | solution.py:123
  214.2 2.0 fusion.165
  216.2 12.3 %collective-permute-done.1 = f32[8,128,256]{2,0,1:T(8,128)} collective-permute-done((f32[8,128,256]{2,0,1:T(8,128)}, f32[8,128,256]{2,0,1:T(8,128)}, u32[]{:S(2)}, u32[]{:S(2)}) %collective-permute-start.1) | collective-permute-done | bytes 1048608 | tf_op jit(solution)/shard_map/while/body/eval_jaxpr/ppermute | solution.py:11
  228.5 6.6 %fusion.167 = f32[8,128,256]{2,0,1:T(8,128)} fusion(f32[8,128,256]{2,0,1:T(8,128)} %collective-permute-done.1, f32[32,128,256]{2,1,0:T(8,128)S(1)} %fusion.165, f32[32]{0:T(128)S(1)} %compare_convert_fusion.9, s32[32]{0:T(128)S(1)} %fusion.166), kind=kOutput, calls=%fused_computation.40.clone.1 | convolution fusion | flops 100925952 | bytes 6291712 | tf_op jit(solution)/shard_map/while/body/eval_jaxpr/tr,tjf->rjf/dot_general | solution.py:73
  237.1 2.0 fusion.165
  239.1 12.3 %collective-permute-done.1 = f32[8,128,256]{2,0,1:T(8,128)} collective-permute-done((f32[8,128,256]{2,0,1:T(8,128)}, f32[8,128,256]{2,0,1:T(8,128)}, u32[]{:S(2)}, u32[]{:S(2)}) %collective-permute-start.1) | collective-permute-done | bytes 1048608 | tf_op jit(solution)/shard_map/while/body/eval_jaxpr/ppermute | solution.py:11
  251.4 6.6 %fusion.167 = f32[8,128,256]{2,0,1:T(8,128)} fusion(f32[8,128,256]{2,0,1:T(8,128)} %collective-permute-done.1, f32[32,128,256]{2,1,0:T(8,128)S(1)} %fusion.165, f32[32]{0:T(128)S(1)} %compare_convert_fusion.9, s32[32]{0:T(128)S(1)} %fusion.166), kind=kOutput, calls=%fused_computation.40.clone.1 | convolution fusion | flops 100925952 | bytes 6291712 | tf_op jit(solution)/shard_map/while/body/eval_jaxpr/tr,tjf->rjf/dot_general | solution.py:73
  260.0 2.0 fusion.165
  262.0 12.3 %collective-permute-done.1 = f32[8,128,256]{2,0,1:T(8,128)} collective-permute-done((f32[8,128,256]{2,0,1:T(8,128)}, f32[8,128,256]{2,0,1:T(8,128)}, u32[]{:S(2)}, u32[]{:S(2)}) %collective-permute-start.1) | collective-permute-done | bytes 1048608 | tf_op jit(solution)/shard_map/while/body/eval_jaxpr/ppermute | solution.py:11
  274.3 6.6 %fusion.167 = f32[8,128,256]{2,0,1:T(8,128)} fusion(f32[8,128,256]{2,0,1:T(8,128)} %collective-permute-done.1, f32[32,128,256]{2,1,0:T(8,128)S(1)} %fusion.165, f32[32]{0:T(128)S(1)} %compare_convert_fusion.9, s32[32]{0:T(128)S(1)} %fusion.166), kind=kOutput, calls=%fused_computation.40.clone.1 | convolution fusion | flops 100925952 | bytes 6291712 | tf_op jit(solution)/shard_map/while/body/eval_jaxpr/tr,tjf->rjf/dot_general | solution.py:73
  282.8 2.0 fusion.165
  284.9 12.3 %collective-permute-done.1 = f32[8,128,256]{2,0,1:T(8,128)} collective-permute-done((f32[8,128,256]{2,0,1:T(8,128)}, f32[8,128,256]{2,0,1:T(8,128)}, u32[]{:S(2)}, u32[]{:S(2)}) %collective-permute-start.1) | collective-permute-done | bytes 1048608 | tf_op jit(solution)/shard_map/while/body/eval_jaxpr/ppermute | solution.py:11
  297.2 6.6 %fusion.167 = f32[8,128,256]{2,0,1:T(8,128)} fusion(f32[8,128,256]{2,0,1:T(8,128)} %collective-permute-done.1, f32[32,128,256]{2,1,0:T(8,128)S(1)} %fusion.165, f32[32]{0:T(128)S(1)} %compare_convert_fusion.9, s32[32]{0:T(128)S(1)} %fusion.166), kind=kOutput, calls=%fused_computation.40.clone.1 | convolution fusion | flops 100925952 | bytes 6291712 | tf_op jit(solution)/shard_map/while/body/eval_jaxpr/tr,tjf->rjf/dot_general | solution.py:73
  305.7 2.0 fusion.165
  307.7 12.3 %collective-permute-done.1 = f32[8,128,256]{2,0,1:T(8,128)} collective-permute-done((f32[8,128,256]{2,0,1:T(8,128)}, f32[8,128,256]{2,0,1:T(8,128)}, u32[]{:S(2)}, u32[]{:S(2)}) %collective-permute-start.1) | collective-permute-done | bytes 1048608 | tf_op jit(solution)/shard_map/while/body/eval_jaxpr/ppermute | solution.py:11
  320.1 6.6 %fusion.167 = f32[8,128,256]{2,0,1:T(8,128)} fusion(f32[8,128,256]{2,0,1:T(8,128)} %collective-permute-done.1, f32[32,128,256]{2,1,0:T(8,128)S(1)} %fusion.165, f32[32]{0:T(128)S(1)} %compare_convert_fusion.9, s32[32]{0:T(128)S(1)} %fusion.166), kind=kOutput, calls=%fused_computation.40.clone.1 | convolution fusion | flops 100925952 | bytes 6291712 | tf_op jit(solution)/shard_map/while/body/eval_jaxpr/tr,tjf->rjf/dot_general | solution.py:73
  328.6 2.0 fusion.165
  330.6 12.3 %collective-permute-done.1 = f32[8,128,256]{2,0,1:T(8,128)} collective-permute-done((f32[8,128,256]{2,0,1:T(8,128)}, f32[8,128,256]{2,0,1:T(8,128)}, u32[]{:S(2)}, u32[]{:S(2)}) %collective-permute-start.1) | collective-permute-done | bytes 1048608 | tf_op jit(solution)/shard_map/while/body/eval_jaxpr/ppermute | solution.py:11
  343.0 6.6 %fusion.167 = f32[8,128,256]{2,0,1:T(8,128)} fusion(f32[8,128,256]{2,0,1:T(8,128)} %collective-permute-done.1, f32[32,128,256]{2,1,0:T(8,128)S(1)} %fusion.165, f32[32]{0:T(128)S(1)} %compare_convert_fusion.9, s32[32]{0:T(128)S(1)} %fusion.166), kind=kOutput, calls=%fused_computation.40.clone.1 | convolution fusion | flops 100925952 | bytes 6291712 | tf_op jit(solution)/shard_map/while/body/eval_jaxpr/tr,tjf->rjf/dot_general | solution.py:73
  351.5 2.0 fusion.165
  353.5 12.3 %collective-permute-done.1 = f32[8,128,256]{2,0,1:T(8,128)} collective-permute-done((f32[8,128,256]{2,0,1:T(8,128)}, f32[8,128,256]{2,0,1:T(8,128)}, u32[]{:S(2)}, u32[]{:S(2)}) %collective-permute-start.1) | collective-permute-done | bytes 1048608 | tf_op jit(solution)/shard_map/while/body/eval_jaxpr/ppermute | solution.py:11
  365.9 6.6 %fusion.167 = f32[8,128,256]{2,0,1:T(8,128)} fusion(f32[8,128,256]{2,0,1:T(8,128)} %collective-permute-done.1, f32[32,128,256]{2,1,0:T(8,128)S(1)} %fusion.165, f32[32]{0:T(128)S(1)} %compare_convert_fusion.9, s32[32]{0:T(128)S(1)} %fusion.166), kind=kOutput, calls=%fused_computation.40.clone.1 | convolution fusion | flops 100925952 | bytes 6291712 | tf_op jit(solution)/shard_map/while/body/eval_jaxpr/tr,tjf->rjf/dot_general | solution.py:73
  372.4 2.7 fusion.61
  377.5 122.6 %all-reduce.2.cloned.1.call-done = f32[256,256]{0,1:T(8,128)} async-done(((f32[256,256]{0,1:T(8,128)}), f32[256,256]{0,1:T(8,128)}) %all-reduce.2.cloned.1.call-update) | async-done | bytes 262160 | tf_op jit(solution)/shard_map/psum | solution.py:146
  (187 shorter events, 46.9 us)
Async XLA Ops:
  7.2 3.4 copy-start
  12.4 3.2 copy-start.6
  26.0 5.3 %copy-start.8 = (s32[1,1,8,32]{3,2,1,0:T(8,128)S(1)}, s32[1,1,8,32]{3,2,1,0:T(8,128)}, u32[]{:S(2)}) copy-start(s32[1,1,8,32]{3,2,1,0:T(8,128)} %param.23) | copy-start | bytes 3076
  26.0 5.3 %copy-start.9 = (s32[1,1,8,32]{3,2,1,0:T(8,128)S(1)}, s32[1,1,8,32]{3,2,1,0:T(8,128)}, u32[]{:S(2)}) copy-start(s32[1,1,8,32]{3,2,1,0:T(8,128)} %param.24) | copy-start | bytes 3076
  26.0 148.2 %all-to-all-start = ((f32[4,4,128,256]{3,1,2,0:T(4,128)}), f32[4,4,128,256]{3,1,2,0:T(4,128)}, u32[]{:S(2)}, u32[]{:S(2)}) async-start(f32[4,4,128,256]{3,1,2,0:T(4,128)} %copy.54), calls=%async_computation | async-start | bytes 4194304 | tf_op jit(solution)/shard_map/all_to_all | solution.py:102
  31.4 2.1 copy-start.10
  31.4 3.4 copy-start.7
  31.4 3.4 copy-start.12
  43.0 10.8 %collective-permute-start = (bf16[8,128,256]{2,1,0:T(8,128)(2,1)S(1)}, bf16[8,128,256]{2,1,0:T(8,128)(2,1)S(1)}, u32[]{:S(2)}, u32[]{:S(2)}) collective-permute-start(bf16[8,128,256]{2,1,0:T(8,128)(2,1)S(1)} %get-tuple-element.727), channel_id=1, source_target_pairs={{0,1},{1,2},{2,3},{3,4},{4,5},{5,6},{6,7},{7,0},{8,9},{9,10},{10,1... | collective-permute-start | bytes 1572872 | tf_op jit(solution)/shard_map/while/body/eval_jaxpr/ppermute | solution.py:11
  54.5 2.1 copy-start.1
  61.1 1.0 copy-start.2
  62.1 10.4 %collective-permute-start = (bf16[8,128,256]{2,1,0:T(8,128)(2,1)S(1)}, bf16[8,128,256]{2,1,0:T(8,128)(2,1)S(1)}, u32[]{:S(2)}, u32[]{:S(2)}) collective-permute-start(bf16[8,128,256]{2,1,0:T(8,128)(2,1)S(1)} %get-tuple-element.727), channel_id=1, source_target_pairs={{0,1},{1,2},{2,3},{3,4},{4,5},{5,6},{6,7},{7,0},{8,9},{9,10},{10,1... | collective-permute-start | bytes 1572872 | tf_op jit(solution)/shard_map/while/body/eval_jaxpr/ppermute | solution.py:11
  73.2 2.1 copy-start.1
  79.8 1.0 copy-start.2
  80.8 10.4 %collective-permute-start = (bf16[8,128,256]{2,1,0:T(8,128)(2,1)S(1)}, bf16[8,128,256]{2,1,0:T(8,128)(2,1)S(1)}, u32[]{:S(2)}, u32[]{:S(2)}) collective-permute-start(bf16[8,128,256]{2,1,0:T(8,128)(2,1)S(1)} %get-tuple-element.727), channel_id=1, source_target_pairs={{0,1},{1,2},{2,3},{3,4},{4,5},{5,6},{6,7},{7,0},{8,9},{9,10},{10,1... | collective-permute-start | bytes 1572872 | tf_op jit(solution)/shard_map/while/body/eval_jaxpr/ppermute | solution.py:11
  91.9 2.1 copy-start.1
  98.5 1.0 copy-start.2
  99.5 10.4 %collective-permute-start = (bf16[8,128,256]{2,1,0:T(8,128)(2,1)S(1)}, bf16[8,128,256]{2,1,0:T(8,128)(2,1)S(1)}, u32[]{:S(2)}, u32[]{:S(2)}) collective-permute-start(bf16[8,128,256]{2,1,0:T(8,128)(2,1)S(1)} %get-tuple-element.727), channel_id=1, source_target_pairs={{0,1},{1,2},{2,3},{3,4},{4,5},{5,6},{6,7},{7,0},{8,9},{9,10},{10,1... | collective-permute-start | bytes 1572872 | tf_op jit(solution)/shard_map/while/body/eval_jaxpr/ppermute | solution.py:11
  110.6 2.1 copy-start.1
  117.2 1.0 copy-start.2
  118.2 10.4 %collective-permute-start = (bf16[8,128,256]{2,1,0:T(8,128)(2,1)S(1)}, bf16[8,128,256]{2,1,0:T(8,128)(2,1)S(1)}, u32[]{:S(2)}, u32[]{:S(2)}) collective-permute-start(bf16[8,128,256]{2,1,0:T(8,128)(2,1)S(1)} %get-tuple-element.727), channel_id=1, source_target_pairs={{0,1},{1,2},{2,3},{3,4},{4,5},{5,6},{6,7},{7,0},{8,9},{9,10},{10,1... | collective-permute-start | bytes 1572872 | tf_op jit(solution)/shard_map/while/body/eval_jaxpr/ppermute | solution.py:11
  129.3 2.1 copy-start.1
  135.9 1.0 copy-start.2
  136.9 10.4 %collective-permute-start = (bf16[8,128,256]{2,1,0:T(8,128)(2,1)S(1)}, bf16[8,128,256]{2,1,0:T(8,128)(2,1)S(1)}, u32[]{:S(2)}, u32[]{:S(2)}) collective-permute-start(bf16[8,128,256]{2,1,0:T(8,128)(2,1)S(1)} %get-tuple-element.727), channel_id=1, source_target_pairs={{0,1},{1,2},{2,3},{3,4},{4,5},{5,6},{6,7},{7,0},{8,9},{9,10},{10,1... | collective-permute-start | bytes 1572872 | tf_op jit(solution)/shard_map/while/body/eval_jaxpr/ppermute | solution.py:11
  148.0 2.1 copy-start.1
  154.6 1.0 copy-start.2
  155.6 10.4 %collective-permute-start = (bf16[8,128,256]{2,1,0:T(8,128)(2,1)S(1)}, bf16[8,128,256]{2,1,0:T(8,128)(2,1)S(1)}, u32[]{:S(2)}, u32[]{:S(2)}) collective-permute-start(bf16[8,128,256]{2,1,0:T(8,128)(2,1)S(1)} %get-tuple-element.727), channel_id=1, source_target_pairs={{0,1},{1,2},{2,3},{3,4},{4,5},{5,6},{6,7},{7,0},{8,9},{9,10},{10,1... | collective-permute-start | bytes 1572872 | tf_op jit(solution)/shard_map/while/body/eval_jaxpr/ppermute | solution.py:11
  166.7 2.1 copy-start.1
  173.3 1.0 copy-start.2
  178.6 1.0 copy-start.4
  182.5 25.0 %all-to-all-start.1 = ((bf16[4,4,128,256]{3,1,2,0:T(4,128)(2,1)}), bf16[4,4,128,256]{3,1,2,0:T(4,128)(2,1)}, u32[]{:S(2)}, u32[]{:S(2)}) async-start(bf16[4,4,128,256]{3,1,2,0:T(4,128)(2,1)} %convolution_convert_fusion), calls=%async_computation.1 | async-start | bytes 2097152 | tf_op jit(solution)/shard_map/all_to_all | solution.py:130
  186.7 313.4 %all-reduce.2.cloned.1.call-start = ((), (), s32[]{:S(2)}) async-start(), calls=%async_computation.2 | async-start | bytes 524288 | tf_op jit(solution)/shard_map/psum | solution.py:146
  212.2 160.3 %copy-start.11 = (s32[1,1,16]{2,1,0:T(1,128)S(1)}, s32[1,1,16]{2,1,0:T(1,128)}, u32[]{:S(2)}) copy-start(s32[1,1,16]{2,1,0:T(1,128)} %param.27) | copy-start | bytes 196
  212.2 16.3 %collective-permute-start.1 = (f32[8,128,256]{2,0,1:T(8,128)}, f32[8,128,256]{2,0,1:T(8,128)}, u32[]{:S(2)}, u32[]{:S(2)}) collective-permute-start(f32[8,128,256]{2,0,1:T(8,128)} %get-tuple-element.763), channel_id=1, source_target_pairs={{0,1},{1,2},{2,3},{3,4},{4,5},{5,6},{6,7},{7,0},{8,9},{9,10},{10,1... | collective-permute-start | bytes 3145736 | tf_op jit(solution)/shard_map/while/body/eval_jaxpr/ppermute | solution.py:11
  235.1 16.3 %collective-permute-start.1 = (f32[8,128,256]{2,0,1:T(8,128)}, f32[8,128,256]{2,0,1:T(8,128)}, u32[]{:S(2)}, u32[]{:S(2)}) collective-permute-start(f32[8,128,256]{2,0,1:T(8,128)} %get-tuple-element.763), channel_id=1, source_target_pairs={{0,1},{1,2},{2,3},{3,4},{4,5},{5,6},{6,7},{7,0},{8,9},{9,10},{10,1... | collective-permute-start | bytes 3145736 | tf_op jit(solution)/shard_map/while/body/eval_jaxpr/ppermute | solution.py:11
  258.0 16.3 %collective-permute-start.1 = (f32[8,128,256]{2,0,1:T(8,128)}, f32[8,128,256]{2,0,1:T(8,128)}, u32[]{:S(2)}, u32[]{:S(2)}) collective-permute-start(f32[8,128,256]{2,0,1:T(8,128)} %get-tuple-element.763), channel_id=1, source_target_pairs={{0,1},{1,2},{2,3},{3,4},{4,5},{5,6},{6,7},{7,0},{8,9},{9,10},{10,1... | collective-permute-start | bytes 3145736 | tf_op jit(solution)/shard_map/while/body/eval_jaxpr/ppermute | solution.py:11
  280.9 16.3 %collective-permute-start.1 = (f32[8,128,256]{2,0,1:T(8,128)}, f32[8,128,256]{2,0,1:T(8,128)}, u32[]{:S(2)}, u32[]{:S(2)}) collective-permute-start(f32[8,128,256]{2,0,1:T(8,128)} %get-tuple-element.763), channel_id=1, source_target_pairs={{0,1},{1,2},{2,3},{3,4},{4,5},{5,6},{6,7},{7,0},{8,9},{9,10},{10,1... | collective-permute-start | bytes 3145736 | tf_op jit(solution)/shard_map/while/body/eval_jaxpr/ppermute | solution.py:11
  303.8 16.3 %collective-permute-start.1 = (f32[8,128,256]{2,0,1:T(8,128)}, f32[8,128,256]{2,0,1:T(8,128)}, u32[]{:S(2)}, u32[]{:S(2)}) collective-permute-start(f32[8,128,256]{2,0,1:T(8,128)} %get-tuple-element.763), channel_id=1, source_target_pairs={{0,1},{1,2},{2,3},{3,4},{4,5},{5,6},{6,7},{7,0},{8,9},{9,10},{10,1... | collective-permute-start | bytes 3145736 | tf_op jit(solution)/shard_map/while/body/eval_jaxpr/ppermute | solution.py:11
  326.7 16.3 %collective-permute-start.1 = (f32[8,128,256]{2,0,1:T(8,128)}, f32[8,128,256]{2,0,1:T(8,128)}, u32[]{:S(2)}, u32[]{:S(2)}) collective-permute-start(f32[8,128,256]{2,0,1:T(8,128)} %get-tuple-element.763), channel_id=1, source_target_pairs={{0,1},{1,2},{2,3},{3,4},{4,5},{5,6},{6,7},{7,0},{8,9},{9,10},{10,1... | collective-permute-start | bytes 3145736 | tf_op jit(solution)/shard_map/while/body/eval_jaxpr/ppermute | solution.py:11
  349.5 16.3 %collective-permute-start.1 = (f32[8,128,256]{2,0,1:T(8,128)}, f32[8,128,256]{2,0,1:T(8,128)}, u32[]{:S(2)}, u32[]{:S(2)}) collective-permute-start(f32[8,128,256]{2,0,1:T(8,128)} %get-tuple-element.763), channel_id=1, source_target_pairs={{0,1},{1,2},{2,3},{3,4},{4,5},{5,6},{6,7},{7,0},{8,9},{9,10},{10,1... | collective-permute-start | bytes 3145736 | tf_op jit(solution)/shard_map/while/body/eval_jaxpr/ppermute | solution.py:11
  372.4 2.9 copy-start.3
  375.2 1.2 copy-start.5
Sparse Core Ops, SparseCore 0:
  376.5 123.6 all-reduce.1
where the time goes:
time: 511 us; the launch traced here: 509 us
  waiting for transfers between devices  273 us (53%)
  matrix products  141 us (28%)
  local copies, waits for them, and re-layouts  55.3 us (11%)
  other arithmetic  14.6 us (3%)
  between operations  14.3 us (3%)
  starting transfers between devices  9.62 us (2%)
    ppermute x14, waiting for transfers between devices, shifted(): lax.ppermute(value, axis, [(i, (i + by) % size) for i in range(size)])  151 us
    psum x1, waiting for transfers between devices, local(): grad_weight = lax.psum(weight_term, ('grp', 'blk')) * grad_scale  123 us
    dot_general x8, matrix products, backward_block(): return jnp.einsum('tr,tjf->rjf', placing, product, precision=highest)  51.2 us
    dot_general x8, matrix products, forward_block(): return jnp.einsum('tr,tif->rif', placing, product, precision=highest)  36.7 us
    dot_general x8, matrix products, forward_block(): jnp.einsum('tij,tjf->tif', blk_vals, picked, preferred_element_type=jnp.f...  17.4 us
    dot_general x8, matrix products, backward_block(): jnp.einsum('tij,tif->tjf', blk_vals, picked, preferred_element_type=jnp.f...  16.1 us
    unnamed x24, local copies, waits for them, and re-layouts  13.5 us
    convert_element_type x16, other arithmetic, block_parts(): live_mask = (slot_range < blk_count).astype(jnp.float32)  10.4 us
  transfers between devices with their start and end apart: 17, of which 15 were waited for; matrix products, arithmetic and copies ran while one was open for 24% of the time, Pallas kernels for 0%

commit v1 on v0

v1 whole, which is shorter than its diff:
```python
import functools
import math

import jax
import jax.numpy as jnp
from jax import lax
from jax.experimental import pallas as pl
from jax.experimental.pallas import tpu as pltpu
from jax.sharding import PartitionSpec as P

F32 = jnp.float32
BF16 = jnp.bfloat16
UNROLL = 16
SMEM = pl.BlockSpec(memory_space=pltpu.SMEM)
VMEM = pl.BlockSpec(memory_space=pltpu.VMEM)
ANY = pl.BlockSpec(memory_space=pl.ANY)


def dot(a, b, dims):
    return lax.dot_general(a, b, (dims, ((), ())), preferred_element_type=F32)


def call(kernel, name, out_shape, in_specs, out_specs, scratch, flops, moved):
    return pl.pallas_call(
        kernel,
        out_shape=out_shape,
        in_specs=in_specs,
        out_specs=out_specs,
        scratch_shapes=scratch,
        compiler_params=pltpu.CompilerParams(vmem_limit_bytes=40 << 20),
        cost_estimate=pl.CostEstimate(flops=flops, bytes_accessed=moved, transcendentals=0),
        name=name,
    )


def fetch_pair(ids, vals, buf, sem):
    slots = vals.shape[1]
    copies = [
        pltpu.make_async_copy(vals.at[ids[k]], buf.at[pl.ds(k * slots, slots)], sem.at[k])
        for k in range(2)
    ]
    for copy in copies:
        copy.start()
    return copies


def pair_loop(ids, cnt, picks, places, buf, source, total, spread):
    slots = buf.shape[0] // 2
    row_tiles = source.shape[0] if spread == "places" else source.shape[0] // 2
    trash = total.shape[0] - 1
    first, second = cnt[ids[0]], cnt[ids[1]]
    used = first + second
    contract = ((1,), (0,)) if spread == "picks" else ((0,), (0,))

    def body(step, carry):
        products = []
        for u in range(UNROLL):
            at = step * UNROLL + u
            late = at >= first
            live = at < used
            slot = jnp.where(live, jnp.where(late, at - first, at), 0)
            block = jnp.where(late, ids[1], ids[0])
            shift = jnp.where(late, 1, 0)
            pick = picks[block, slot]
            place = places[block, slot]
            if spread == "picks":
                pick = pick + shift * row_tiles
            else:
                place = place + shift * row_tiles
            place = jnp.where(live, place, trash)
            tile = buf[shift * slots + slot]
            products.append((place, dot(tile, source[pick], contract)))
        for place, product in products:
            total[place] += product
        return carry

    lax.fori_loop(0, (used + UNROLL - 1) // UNROLL, body, 0)


def forward_pair(has_acc, ids, cnt, rows, cols, *refs):
    if has_acc:
        acc, block_a, block_b, weight, vals, out, buf, panel, total, sem = refs
    else:
        block_a, block_b, weight, vals, out, buf, panel, total, sem = refs
    copies = fetch_pair(ids, vals, buf, sem)
    row_tiles, size, width = out.shape
    for k, block in enumerate((block_a, block_b)):
        proj = dot(block[...], weight[...], ((1,), (0,))).astype(BF16)
        panel[pl.ds(k * row_tiles, row_tiles)] = proj.reshape(row_tiles, size, width)
    if has_acc:
        total[pl.ds(0, row_tiles)] = acc[...]
    else:
        total[...] = jnp.zeros_like(total)
    for copy in copies:
        copy.wait()
    pair_loop(ids, cnt, cols, rows, buf, panel, total, "picks")
    out[...] = total[pl.ds(0, row_tiles)]


def hub_products(me, dest, cols, feats, weight, tiles, send, panel, tally):
    groups = send.shape[0]
    cap = send.shape[1]
    row_tiles, size, width = panel.shape
    proj = dot(feats[...], weight[...], ((1,), (0,))).astype(BF16)
    panel[...] = proj.reshape(row_tiles, size, width)
    for k in range(groups):
        tally[k] = 0
    for h in range(tiles.shape[0]):
        to = dest[me[0], h] ^ me[0]
        rank = jnp.minimum(tally[to], cap - 1)
        tally[to] = rank + 1
        product = dot(tiles[h], panel[cols[h]], ((1,), (0,)))
        send[to, rank] = product.astype(BF16)


def each_hub(me, dest, groups, count, cap, visit):
    for k in range(groups):
        source = me[0] ^ k

        def body(h, rank, k=k, source=source):
            mine = dest[source, h] == me[0]

            @pl.when(mine)
            def _():
                visit(k, source, h, jnp.minimum(rank, cap - 1))

            return rank + mine.astype(jnp.int32)

        lax.fori_loop(0, count, body, jnp.int32(0))


def hub_add(groups, me, dest, hub_rows, *refs):
    acc, parts, out = refs[0], refs[1:-1], refs[-1]
    out[...] = acc[...]

    def visit(k, source, h, rank):
        out[hub_rows[source, h]] += parts[k][rank].astype(F32)

    each_hub(me, dest, groups, dest.shape[1], parts[0].shape[0], visit)


def last_forward(
    ids, cnt, rows, cols, me, dest, hub_rows, acc, block_a, block_b, weight, vals, cot,
    layer_out, grad, back, buf, panel, total, sem,
):
    copies = fetch_pair(ids, vals, buf, sem)
    row_tiles, size, width = grad.shape
    for k, block in enumerate((block_a, block_b)):
        proj = dot(block[...], weight[...], ((1,), (0,))).astype(BF16)
        panel[pl.ds(k * row_tiles, row_tiles)] = proj.reshape(row_tiles, size, width)
    total[pl.ds(0, row_tiles)] = acc[...]
    for copy in copies:
        copy.wait()
    pair_loop(ids, cnt, cols, rows, buf, panel, total, "picks")

    def finish(r, carry):
        agg = total[r]
        sig = jax.nn.sigmoid(agg)
        layer_out[r] = (agg * sig).astype(BF16)
        slope = sig * (1.0 + agg * (1.0 - sig))
        grad[r] = (cot[r].astype(F32) * slope).astype(BF16)
        return carry

    lax.fori_loop(0, row_tiles, finish, 0)

    def visit(k, source, h, rank):
        back[k, rank] = grad[hub_rows[source, h]]

    each_hub(me, dest, back.shape[0], dest.shape[1], back.shape[1], visit)


def backward_pair(has_gw, ids, cnt, rows, cols, *refs):
    if has_gw:
        gw, grad, block_a, block_b, vals, part_a, part_b, gw_out, buf, total, sem = refs
    else:
        grad, block_a, block_b, vals, part_a, part_b, gw_out, buf, total, sem = refs
    copies = fetch_pair(ids, vals, buf, sem)
    row_tiles, size, width = grad.shape
    total[...] = jnp.zeros_like(total)
    for copy in copies:
        copy.wait()
    pair_loop(ids, cnt, rows, cols, buf, grad, total, "places")
    part_a[...] = total[pl.ds(0, row_tiles)].astype(BF16)
    part_b[...] = total[pl.ds(row_tiles, row_tiles)]
    sums = gw[...] if has_gw else jnp.zeros(gw_out.shape, F32)
    for k, block in enumerate((block_a, block_b)):
        mine = total[pl.ds(k * row_tiles, row_tiles)].astype(BF16).reshape(row_tiles * size, width)
        sums += dot(block[...], mine, ((0,), (0,)))
    gw_out[...] = sums


def hub_backward(groups, me, dest, cols, gw, own, feats, tiles, *refs):
    parts, (out, gw_out, slots, total, tally) = refs[:groups], refs[groups:]
    row_tiles, size, width = out.shape
    cap = parts[0].shape[0]
    for k in range(groups):
        slots[pl.ds(k * cap, cap)] = parts[k][...]
        tally[k] = 0
    total[...] = jnp.zeros_like(total)
    products = []
    for h in range(tiles.shape[0]):
        source = dest[me[0], h] ^ me[0]
        rank = jnp.minimum(tally[source], cap - 1)
        tally[source] = rank + 1
        products.append(dot(tiles[h], slots[source * cap + rank], ((0,), (0,))))
        if len(products) == 8 or h == tiles.shape[0] - 1:
            for back, product in enumerate(products):
                total[cols[h + 1 - len(products) + back]] += product
            products = []
    out[...] = own[...] + total[...]
    mine = total[...].astype(BF16).reshape(row_tiles * size, width)
    gw_out[...] = gw[...] + dot(feats[...], mine, ((0,), (0,)))


def last_backward(count, *refs):
    own, parts, weight, out = refs[0], refs[1 : 1 + count], refs[-2], refs[-1]
    sums = own[...]
    for part in parts:
        sums = sums + part[...].astype(F32)
    out[...] = dot(sums.astype(BF16).reshape(out.shape), weight[...], ((1,), (1,))).astype(BF16)


def tree_sum(values):
    while len(values) > 1:
        values = [a + b for a, b in zip(values[::2], values[1::2])]
    return values[0]


def local(
    feats,
    weight,
    cotangent,
    labels,
    tile_vals,
    tile_row,
    tile_col,
    tile_count,
    hub_vals,
    hub_col,
    hub_dest,
    hub_row,
):
    n_blocks = lax.axis_size("blk")
    n_groups = lax.axis_size("grp")
    n_chips = n_blocks // 2
    my_block = lax.axis_index("blk").astype(jnp.int32)
    my_group = lax.axis_index("grp").astype(jnp.int32)
    core = my_block % 2
    rows_dev, width = feats.shape
    size = tile_vals.shape[-1]
    row_tiles = rows_dev // size
    slots = tile_vals.shape[3]
    hubs = hub_vals.shape[2]
    cap = max(2, hubs // 4)
    vals = tile_vals[0, 0]
    rows, cols, cnt = tile_row[0, 0], tile_col[0, 0], tile_count[0, 0]
    dest, hub_rows = hub_dest[:, 0, :, 0], hub_row[:, 0, :]
    hub_tiles, hub_cols = hub_vals[0, 0], hub_col[0, 0]
    me = my_group.reshape(1)
    panel = (row_tiles, size, width)
    relay = n_chips == 4

    def swap(value):
        return lax.ppermute(value, "blk", [(i, i ^ 1) for i in range(n_blocks)])

    def across(value, mask, chips=None):
        chosen = range(n_chips) if chips is None else chips
        pairs = [(2 * c + k, 2 * (c ^ mask) + k) for c in chosen for k in range(2)]
        return lax.ppermute(value, "blk", pairs)

    def group(value, mask):
        return lax.ppermute(value, "grp", [(i, i ^ mask) for i in range(n_groups)])

    def ids_of(mask):
        chip = (my_block // 2) ^ mask
        return jnp.stack([2 * chip + 1 - core, 2 * chip + core])

    moved = 4 << 20
    tile_flops = 2 * size * size * width
    pair_flops = 2 * slots * tile_flops
    buf = pltpu.VMEM((2 * slots, size, size), BF16)
    sems = pltpu.SemaphoreType.DMA((2,))
    acc_shape = jax.ShapeDtypeStruct(panel, F32)

    got = {0: feats}
    if relay:
        got[2] = across(feats, 2)
        got[1] = across(feats, 1)
        direct = across(feats, 3, (1, 2))
        passed = across(got[2], 1, (1, 2))
        got[3] = direct + passed
    else:
        for mask in range(1, n_chips):
            got[mask] = across(feats, mask)
    pairs = {mask: swap(value) for mask, value in got.items()}

    send = call(
        hub_products,
        "hub_products",
        jax.ShapeDtypeStruct((n_groups, cap, size, width), BF16),
        [SMEM, SMEM, SMEM, VMEM, VMEM, VMEM],
        VMEM,
        [pltpu.VMEM(panel, BF16), pltpu.SMEM((n_groups,), jnp.int32)],
        hubs * tile_flops,
        moved,
    )(me, dest, hub_cols, feats, weight, hub_tiles)
    hub_parts = [send[0]] + [group(send[k], k) for k in range(1, n_groups)]

    order = [m for m in range(n_chips) if m != n_chips - 1]
    last = n_chips - 1

    acc = None
    for mask in order:
        acc = call(
            functools.partial(forward_pair, acc is not None),
            "forward_pair",
            acc_shape,
            [SMEM] * 4 + [VMEM] * (3 if acc is None else 4) + [ANY],
            VMEM,
            [
                buf,
                pltpu.VMEM((2 * row_tiles, size, width), BF16),
                pltpu.VMEM((row_tiles + 1, size, width), F32),
                sems,
            ],
            pair_flops,
            moved,
        )(
            ids_of(mask), cnt, rows, cols, *(() if acc is None else (acc,)),
            pairs[mask], got[mask], weight, vals,
        )
        if mask == order[1]:
            acc = call(
                functools.partial(hub_add, n_groups),
                "hub_add",
                acc_shape,
                [SMEM] * 3 + [VMEM] * (1 + n_groups),
                VMEM,
                [],
                1 << 20,
                moved,
            )(me, dest, hub_rows, acc, *hub_parts)

    cot = jnp.where(labels[:, None] >= 0, cotangent, jnp.zeros_like(cotangent)).reshape(panel)
    layer_out, grad, back = call(
        last_forward,
        "last_forward",
        (
            jax.ShapeDtypeStruct(panel, BF16),
            jax.ShapeDtypeStruct(panel, BF16),
            jax.ShapeDtypeStruct((n_groups, cap, size, width), BF16),
        ),
        [SMEM] * 7 + [VMEM] * 4 + [ANY, VMEM],
        (VMEM, VMEM, VMEM),
        [
            buf,
            pltpu.VMEM((2 * row_tiles, size, width), BF16),
            pltpu.VMEM((row_tiles + 1, size, width), F32),
            sems,
        ],
        pair_flops,
        moved,
    )(
        ids_of(last), cnt, rows, cols, me, dest, hub_rows, acc,
        pairs[last], got[last], weight, vals, cot,
    )

    back_parts = [back[0]] + [group(back[k], k) for k in range(1, n_groups)]

    gw = None
    arrived = []
    from_ends = None
    for mask in reversed(range(n_chips)):
        part_other, part_own, gw = call(
            functools.partial(backward_pair, gw is not None),
            "backward_pair",
            (
                jax.ShapeDtypeStruct(panel, BF16),
                acc_shape,
                jax.ShapeDtypeStruct((width, width), F32),
            ),
            [SMEM] * 4 + [VMEM] * (3 if gw is None else 4) + [ANY],
            (VMEM, VMEM, VMEM),
            [buf, pltpu.VMEM((2 * row_tiles + 1, size, width), F32), sems],
            pair_flops,
            moved,
        )(
            ids_of(mask), cnt, rows, cols, *(() if gw is None else (gw,)),
            grad, pairs[mask], got[mask], vals,
        )
        theirs = swap(part_other)
        if mask == 0:
            arrived.append(theirs)
            break
        both = part_own + theirs.astype(F32)
        if relay and mask == 3:
            both = both.astype(BF16)
            from_ends = across(both, 1, (0, 3))
            arrived.append(across(both, 3, (1, 2)))
        else:
            if relay and mask == 2:
                both = both + from_ends.astype(F32)
            arrived.append(across(both.astype(BF16), mask))

    own_sum, gw = call(
        functools.partial(hub_backward, n_groups),
        "hub_backward",
        (acc_shape, jax.ShapeDtypeStruct((width, width), F32)),
        [SMEM] * 3 + [VMEM] * (4 + n_groups),
        (VMEM, VMEM),
        [
            pltpu.VMEM((n_groups * cap, size, width), BF16),
            pltpu.VMEM(panel, F32),
            pltpu.SMEM((n_groups,), jnp.int32),
        ],
        hubs * tile_flops,
        moved,
    )(me, dest, hub_cols, gw, part_own, feats, hub_tiles, *back_parts)

    half = width // 2
    halves = gw.reshape(2, half, width).astype(BF16)
    kept = lax.dynamic_index_in_dim(halves, core, 0, keepdims=False)
    given = lax.dynamic_index_in_dim(halves, 1 - core, 0, keepdims=False)
    share = (kept.astype(F32) + swap(given).astype(F32)).astype(BF16)
    terms = [share] + [group(share, k) for k in range(1, n_groups)]
    share = tree_sum([t.astype(F32) for t in terms]).astype(BF16)
    terms = [share] + [across(share, m) for m in range(1, n_chips)]
    share = tree_sum([t.astype(F32) for t in terms]) * (1.0 / math.sqrt(rows_dev * n_blocks * n_groups))
    other = swap(share)
    grad_weight = jnp.concatenate(
        [jnp.where(core == 0, share, other), jnp.where(core == 0, other, share)], axis=0
    )

    grad_feats = call(
        functools.partial(last_backward, len(arrived)),
        "last_backward",
        jax.ShapeDtypeStruct((rows_dev, width), BF16),
        [VMEM] * (2 + len(arrived)),
        VMEM,
        [],
        2 * rows_dev * width * width,
        moved,
    )(own_sum, *arrived, weight)
    return (layer_out.reshape(rows_dev, width), grad_feats, grad_weight)


def solution(mesh):
    in_specs = (
        P(("grp", "blk"), None),
        P(),
        P(("grp", "blk"), None),
        P(("grp", "blk")),
        P("grp", "blk", None, None, None, None),
        P("grp", "blk", None, None),
        P("grp", "blk", None, None),
        P("grp", "blk", None),
        P("grp", "blk", None, None, None),
        P("grp", "blk", None),
        P(None, "blk", None, None),
        P(None, "blk", None),
    )
    out_specs = (P(("grp", "blk"), None), P(("grp", "blk"), None), P())
    return jax.shard_map(local, mesh=mesh, in_specs=in_specs, out_specs=out_specs, check_vma=False)
```

time: 511 us -> 169 us (0.33)
  waiting for transfers between devices: 273 us -> 60.2 us
  matrix products: 141 us -> 0 us
  Pallas kernels: 0 us -> 35.4 us
  local copies, waits for them, and re-layouts: 55.3 us -> 23.6 us
  starting transfers between devices: 9.62 us -> 38.1 us
  between operations: 14.3 us -> 1.16 us
    dot_general x43 -> x0, matrix products: 141 us -> none  [the longest x8 51.2 us: backward_block(): return jnp.einsum('tr,tjf->rjf', placing, product, precision=highest)]
    psum x1 -> x0, waiting for transfers between devices: 123 us -> none  [local(): grad_weight = lax.psum(weight_term, ('grp', 'blk')) * grad_scale]
    ppermute x14 -> x30, waiting for transfers between devices: 151 us -> 60.2 us  [the longest x11 58.3 us: across(): return lax.ppermute(value, 'blk', pairs)]
    ppermute x14 -> x30, starting transfers between devices: 0.04 us -> 38.1 us  [the longest x11 23.1 us: across(): return lax.ppermute(value, 'blk', pairs)]
    pallas_call x0 -> x12, Pallas kernels: none -> 35.4 us  [the longest x4 14.4 us: local(): call(functools.partial(backward_pair, gw is not None), 'backward_pair', (...]
    gather x17 -> x0, local copies, waits for them, and re-layouts: 12.8 us -> none  [the longest x8 6.78 us: forward_block(): picked = jnp.take(panel_now, blk_cols, axis=0)]
    all_to_all x2 -> x0, starting transfers between devices: 9.54 us -> none  [the longest x1 5.29 us: local(): lax.all_to_all(send_buf, 'grp', split_axis=0, concat_axis=0, tiled=True)]
    dynamic_slice x15 -> x0, local copies, waits for them, and re-layouts: 8.82 us -> none  [block_parts(): blk_count = lax.dynamic_index_in_dim(dev_count, source, 0, keepdims=False)]
  transfers between devices with their start and end apart: 17 -> 30, of which waited for: 15 -> 8; matrix products, arithmetic and copies ran while one was open for 24% -> 6% of each run, Pallas kernels for 0% -> 17%
where the time goes in v1:
time: 169 us; the launch traced here: 168 us
  waiting for transfers between devices  60.2 us (36%)
  starting transfers between devices  38.1 us (23%)
  Pallas kernels  35.4 us (21%)
  local copies, waits for them, and re-layouts  23.6 us (14%)
  other arithmetic  9.71 us (6%)
    ppermute x11, waiting for transfers between devices, across(): return lax.ppermute(value, 'blk', pairs)  58.3 us
    ppermute x11, starting transfers between devices, across(): return lax.ppermute(value, 'blk', pairs)  23.1 us
    unnamed x86, local copies, waits for them, and re-layouts  21.9 us
    pallas_call x4, Pallas kernels, local(): call(functools.partial(backward_pair, gw is not None), 'backward_pair', (...  14.4 us
    ppermute x9, starting transfers between devices, group(): return lax.ppermute(value, 'grp', [(i, i ^ mask) for i in range(n_groups)])  12.4 us
    pallas_call x3, Pallas kernels, local(): call(functools.partial(forward_pair, acc is not None), 'forward_pair', ac...  8.92 us
    pallas_call x1, Pallas kernels, local(): call(last_forward, 'last_forward', (jax.ShapeDtypeStruct(panel, BF16), ja...  4.72 us
  transfers between devices with their start and end apart: 30, of which 8 were waited for; matrix products, arithmetic and copies ran while one was open for 6% of the time, Pallas kernels for 17%

profile of v1, /device:TPU:0, one launch (start us, length us, event | category | flops | bytes accessed | tf_op | source)
XLA Modules:
  0.0 168.2 jit_solution(7096571605404608523)
XLA Ops:
  0.6 4.1 %collective-permute-start.6 = (bf16[1024,256]{1,0:T(8,128)(2,1)}, bf16[1024,256]{1,0:T(8,128)(2,1)S(1)}, u32[]{:S(2)}, u32[]{:S(2)}) collective-permute-start(bf16[1024,256]{1,0:T(8,128)(2,1)} %feats.3), channel_id=1, source_target_pairs={{0,4},{1,5},{2,6},{3,7},{4,0},{5,1},{6,2},{7,3},{8,12},{9,13},{10,... | collective-permute-start | bytes 1572872 | tf_op jit(solution)/shard_map/ppermute | solution.py:269
  4.7 1.6 collective-permute-start.1
  6.3 0.7 collective-permute-start.8
  7.0 1.0 copy-done.3
  8.1 0.9 copy-done.6
  9.0 1.0 copy-done.9
  10.0 0.7 copy-done.23
  10.7 0.7 copy-done.32
  11.3 1.6 hub_products.1
  12.9 16.1 %collective-permute-done.6.refs_2_.refs_3_ = bf16[1024,256]{1,0:T(8,128)(2,1)S(1)} collective-permute-done((bf16[1024,256]{1,0:T(8,128)(2,1)}, bf16[1024,256]{1,0:T(8,128)(2,1)S(1)}, u32[]{:S(2)}, u32[]{:S(2)}) %collective-permute-start.6) | collective-permute-done | bytes 524320 | tf_op jit(solution)/shard_map/ppermute | solution.py:269
  29.0 1.3 collective-permute-start.9
  30.3 0.9 slice_bitcast_fusion
  31.2 1.8 %collective-permute-start.3 = (bf16[4,128,256]{2,1,0:T(8,128)(2,1)}, bf16[4,128,256]{2,1,0:T(8,128)(2,1)}, u32[]{:S(2)}, u32[]{:S(2)}) collective-permute-start(bf16[4,128,256]{2,1,0:T(8,128)(2,1)} %get-tuple-element.43), channel_id=1, source_target_pairs={{0,8},{8,0},{16,24},{24,16},{1,9},{9,1},{17,25},{25,17},{2,10},{10... | collective-permute-start | bytes 786440 | tf_op jit(solution)/shard_map/ppermute | solution.py:272
  33.0 0.7 broadcast_compare_fusion
  33.7 1.2 broadcast_select_fusion
  35.5 7.7 %collective-permute-done.9 = bf16[1024,256]{1,0:T(8,128)(2,1)} collective-permute-done((bf16[1024,256]{1,0:T(8,128)(2,1)S(1)}, bf16[1024,256]{1,0:T(8,128)(2,1)}, u32[]{:S(2)}, u32[]{:S(2)}) %collective-permute-start.9) | collective-permute-done | bytes 524320 | tf_op jit(solution)/shard_map/ppermute | solution.py:269
  43.3 1.2 add.90.block_b.refs_2_
  44.7 1.3 collective-permute-start.4
  46.0 1.4 collective-permute-start.5
  47.5 3.4 %copy-done = bf16[1,1,8,32,128,128]{5,4,3,2,1,0:T(8,128)(2,1)S(1)} copy-done((bf16[1,1,8,32,128,128]{5,4,3,2,1,0:T(8,128)(2,1)S(1)}, bf16[1,1,8,32,128,128]{5,4,3,2,1,0:T(8,128)(2,1)}, u32[]{:S(2)}) %copy-start) | copy-done | bytes 8388632
  50.9 1.0 copy-done.4
  52.0 0.9 copy-done.7
  52.9 0.7 copy-done.19
  53.6 0.7 copy-done.21
  54.3 0.7 copy-done.25
  54.9 3.2 %forward_pair.3.refs_0_ = f32[8,128,256]{2,1,0:T(8,128)S(1)} custom-call(s32[2]{0:T(128)S(1)} %pad_add_fusion.3.ids, s32[8]{0:T(128)S(1)} %bitcast.74, s32[8,32]{1,0:T(8,128)S(1)} %bitcast.54, s32[8,32]{1,0:T(8,128)S(1)} %bitcast.62, bf16[1024,256]{1,0:T(8,128)(2,1)S(1)} %collective-permute-done.refs_0_.refs_2_, bf16[1024,256]{1,0:T(8,128)(2,1)S(1)} %copy-done.4, ...), custom_call_target="tpu_custom_call" | custom-call | flops 536870912 | bytes 4194304 | tf_op jit(solution)/shard_map/forward_pair/pallas_call | solution.py:314
  58.3 2.7 %forward_pair.4.refs_0_ = f32[8,128,256]{2,1,0:T(8,128)S(1)} custom-call(s32[2]{0:T(128)S(1)} %pad_add_fusion.2.ids, s32[8]{0:T(128)S(1)} %bitcast.75, s32[8,32]{1,0:T(8,128)S(1)} %bitcast.55, s32[8,32]{1,0:T(8,128)S(1)} %bitcast.63, f32[8,128,256]{2,1,0:T(8,128)S(1)} %forward_pair.3.refs_0_, bf16[1024,256]{1,0:T(8,128)(2,1)} %collective-permute-done.2.refs_1_.refs_2_, ...), custom_call_target="tpu_custom_call" | custom-call | flops 536870912 | bytes 4194304 | tf_op jit(solution)/shard_map/forward_pair/pallas_call | solution.py:314
  61.0 2.5 %hub_add.1.refs_0_ = f32[8,128,256]{2,1,0:T(8,128)S(1)} custom-call(s32[1]{0:T(128)} %bitcast.5.me, s32[4,16]{1,0:T(4,128)S(1)} %bitcast.71, s32[4,16]{1,0:T(4,128)S(1)} %bitcast.82, f32[8,128,256]{2,1,0:T(8,128)S(1)} %forward_pair.4.refs_0_, bf16[4,128,256]{2,1,0:T(8,128)(2,1)S(1)} %get-tuple-element.44.refs_1_, ...), custom_call_target="tpu_custom_call" | custom-call | flops 1048576 | bytes 4194304 | tf_op jit(solution)/shard_map/hub_add/pallas_call | solution.py:333
  63.6 3.1 %forward_pair.5.acc = f32[8,128,256]{2,1,0:T(8,128)S(1)} custom-call(s32[2]{0:T(128)S(1)} %pad_add_fusion.1.ids, s32[8]{0:T(128)S(1)} %bitcast.76, s32[8,32]{1,0:T(8,128)S(1)} %bitcast.56, s32[8,32]{1,0:T(8,128)S(1)} %bitcast.64, f32[8,128,256]{2,1,0:T(8,128)S(1)} %hub_add.1.refs_0_, bf16[1024,256]{1,0:T(8,128)(2,1)} %collective-permute-done.7.refs_1_.refs_2_, ...), custom_call_target="tpu_custom_call" | custom-call | flops 536870912 | bytes 4194304 | tf_op jit(solution)/shard_map/forward_pair/pallas_call | solution.py:314
  66.7 4.7 %last_forward.1 = (bf16[8,128,256]{2,1,0:T(8,128)(2,1)}, bf16[8,128,256]{2,1,0:T(8,128)(2,1)S(1)}, bf16[4,4,128,256]{3,2,1,0:T(8,128)(2,1)S(1)}) custom-call(s32[2]{0:T(128)S(1)} %pad_add_fusion.ids, s32[8]{0:T(128)S(1)} %bitcast.77, s32[8,32]{1,0:T(8,128)S(1)} %bitcast.57, s32[8,32]{1,0:T(8,128)S(1)} %bitcast.65, s32[1]{0:T(128)} %bitcast.5.me, ...), custom_call_target="tpu_custom_call" | custom-call | flops 536870912 | bytes 4194304 | tf_op jit(solution)/shard_map/last_forward/pallas_call | solution.py:345
  71.4 0.9 slice_bitcast_fusion.4
  72.3 2.1 %collective-permute-start.11 = (bf16[4,128,256]{2,1,0:T(8,128)(2,1)}, bf16[4,128,256]{2,1,0:T(8,128)(2,1)}, u32[]{:S(2)}, u32[]{:S(2)}) collective-permute-start(bf16[4,128,256]{2,1,0:T(8,128)(2,1)} %get-tuple-element.39), channel_id=1, source_target_pairs={{0,8},{8,0},{16,24},{24,16},{1,9},{9,1},{17,25},{25,17},{2,10},{10... | collective-permute-start | bytes 786440 | tf_op jit(solution)/shard_map/ppermute | solution.py:272
  74.4 1.3 collective-permute-start.12
  75.7 0.9 collective-permute-start.13
  76.7 3.4 %copy-done.2 = bf16[1,1,8,32,128,128]{5,4,3,2,1,0:T(8,128)(2,1)S(1)} copy-done((bf16[1,1,8,32,128,128]{5,4,3,2,1,0:T(8,128)(2,1)S(1)}, bf16[1,1,8,32,128,128]{5,4,3,2,1,0:T(8,128)(2,1)}, u32[]{:S(2)}) %copy-start.2) | copy-done | bytes 8388632
  80.6 3.3 %backward_pair.4 = (bf16[8,128,256]{2,1,0:T(8,128)(2,1)}, f32[8,128,256]{2,1,0:T(8,128)S(1)}, f32[256,256]{1,0:T(8,128)S(1)}) custom-call(s32[2]{0:T(128)S(1)} %copy-done.31, s32[8]{0:T(128)S(1)} %bitcast.78, s32[8,32]{1,0:T(8,128)S(1)} %bitcast.58, s32[8,32]{1,0:T(8,128)S(1)} %bitcast.66, bf16[8,128,256]{2,1,0:T(8,128)(2,1)S(1)} %get-tuple-element.21.refs_0_.refs_1_, ...), custom_call_target="tpu_custom_call" | custom-call | flops 536870912 | bytes 4194304 | tf_op jit(solution)/shard_map/backward_pair/pallas_call | solution.py:374
  84.0 0.8 copy-done.16
  84.9 0.6 copy-done.37
  85.5 3.6 %backward_pair.5 = (bf16[8,128,256]{2,1,0:T(8,128)(2,1)S(1)}, f32[8,128,256]{2,1,0:T(8,128)S(1)}, f32[256,256]{1,0:T(8,128)S(1)}) custom-call(s32[2]{0:T(128)S(1)} %copy-done.37, s32[8]{0:T(128)S(1)} %bitcast.79, s32[8,32]{1,0:T(8,128)S(1)} %bitcast.59, s32[8,32]{1,0:T(8,128)S(1)} %bitcast.67, f32[256,256]{1,0:T(8,128)S(1)} %get-tuple-element.22.refs_0_, ...), custom_call_target="tpu_custom_call" | custom-call | flops 536870912 | bytes 4194304 | tf_op jit(solution)/shard_map/backward_pair/pallas_call | solution.py:374
  89.1 1.0 copy-done.13
  90.0 0.8 copy-done.38
  90.9 3.1 %backward_pair.6 = (bf16[8,128,256]{2,1,0:T(8,128)(2,1)S(1)}, f32[8,128,256]{2,1,0:T(8,128)S(1)}, f32[256,256]{1,0:T(8,128)S(1)}) custom-call(s32[2]{0:T(128)S(1)} %copy-done.35, s32[8]{0:T(128)S(1)} %bitcast.80, s32[8,32]{1,0:T(8,128)S(1)} %bitcast.60, s32[8,32]{1,0:T(8,128)S(1)} %bitcast.68, f32[256,256]{1,0:T(8,128)S(1)} %get-tuple-element.23.refs_0_, ...), custom_call_target="tpu_custom_call" | custom-call | flops 536870912 | bytes 4194304 | tf_op jit(solution)/shard_map/backward_pair/pallas_call | solution.py:374
  94.0 1.0 copy-done.15
  94.9 0.8 copy-done.40
  95.8 4.5 %backward_pair.7 = (bf16[8,128,256]{2,1,0:T(8,128)(2,1)}, f32[8,128,256]{2,1,0:T(8,128)S(1)}, f32[256,256]{1,0:T(8,128)S(1)}) custom-call(s32[2]{0:T(128)S(1)} %copy-done.29, s32[8]{0:T(128)S(1)} %bitcast.81, s32[8,32]{1,0:T(8,128)S(1)} %bitcast.61, s32[8,32]{1,0:T(8,128)S(1)} %bitcast.69, f32[256,256]{1,0:T(8,128)S(1)} %get-tuple-element.24.refs_0_, ...), custom_call_target="tpu_custom_call" | custom-call | flops 536870912 | bytes 4194304 | tf_op jit(solution)/shard_map/backward_pair/pallas_call | solution.py:374
  100.3 2.0 %hub_backward.1 = (f32[8,128,256]{2,1,0:T(8,128)S(1)}, f32[256,256]{1,0:T(8,128)S(1)}) custom-call(s32[1]{0:T(128)} %bitcast.5.me, s32[4,16]{1,0:T(4,128)S(1)} %bitcast.73, s32[16]{0:T(128)S(1)} %bitcast.85, f32[256,256]{1,0:T(8,128)S(1)} %get-tuple-element.25.gw, f32[8,128,256]{2,1,0:T(8,128)S(1)} %get-tuple-element.26.own, ...), custom_call_target="tpu_custom_call" | custom-call | flops 134217728 | bytes 4194304 | tf_op jit(solution)/shard_map/hub_backward/pallas_call | solution.py:405
  102.4 1.0 copy-done.17
  103.4 1.1 collective-permute-start.22
  105.4 1.1 collective-permute-start.23
  106.5 1.3 collective-permute-start.24
  107.8 1.2 collective-permute-start.25
  109.0 2.3 %add_convert_fusion.2 = bf16[8,128,256]{2,1,0:T(8,128)(2,1)} fusion(f32[8,128,256]{2,1,0:T(8,128)} %copy-done.16, bf16[8,128,256]{2,1,0:T(8,128)(2,1)} %collective-permute-done.14), kind=kLoop, calls=%fused_computation.2 | loop fusion | flops 786432 | bytes 2097152 | tf_op jit(solution)/shard_map/convert_element_type | solution.py:397
  111.2 1.4 collective-permute-start.17
  113.1 5.5 %collective-permute-start.27 = (bf16[128,256]{1,0:T(8,128)(2,1)S(1)}, bf16[128,256]{1,0:T(8,128)(2,1)S(1)}, u32[]{:S(2)}, u32[]{:S(2)}) collective-permute-start(bf16[128,256]{1,0:T(8,128)(2,1)S(1)} %add_convert_fusion.3), channel_id=1, source_target_pairs={{0,4},{1,5},{2,6},{3,7},{4,0},{5,1},{6,2},{7,3},{8,12},{9,13},{10,... | collective-permute-start | bytes 196616 | tf_op jit(solution)/shard_map/ppermute | solution.py:269
  118.6 2.2 %add_convert_fusion = bf16[8,128,256]{2,1,0:T(8,128)(2,1)} fusion(f32[8,128,256]{2,1,0:T(8,128)} %copy-done.15, bf16[8,128,256]{2,1,0:T(8,128)(2,1)S(1)} %collective-permute-done.19), kind=kLoop, calls=%fused_computation | loop fusion | flops 786432 | bytes 2097152 | tf_op jit(solution)/shard_map/convert_element_type | solution.py:403
  120.8 4.6 %collective-permute-done.17 = bf16[8,128,256]{2,1,0:T(8,128)(2,1)S(1)} collective-permute-done((bf16[8,128,256]{2,1,0:T(8,128)(2,1)}, bf16[8,128,256]{2,1,0:T(8,128)(2,1)S(1)}, u32[]{:S(2)}, u32[]{:S(2)}) %collective-permute-start.17) | collective-permute-done | bytes 524320 | tf_op jit(solution)/shard_map/ppermute | solution.py:269
  125.3 0.7 collective-permute-start.15
  126.0 1.0 add_convert_fusion.1
  127.0 7.8 %collective-permute-start.20 = (bf16[8,128,256]{2,1,0:T(8,128)(2,1)}, bf16[8,128,256]{2,1,0:T(8,128)(2,1)S(1)}, u32[]{:S(2)}, u32[]{:S(2)}) collective-permute-start(bf16[8,128,256]{2,1,0:T(8,128)(2,1)} %add_convert_fusion), channel_id=1, source_target_pairs={{0,2},{1,3},{2,0},{3,1},{4,6},{5,7},{6,4},{7,5},{8,10},{9,11},{10,... | collective-permute-start | bytes 1572872 | tf_op jit(solution)/shard_map/ppermute | solution.py:269
  135.0 1.3 collective-permute-done.29
  136.3 0.7 pad_maximum_fusion
  137.0 10.5 %collective-permute-done.20.refs_3_ = bf16[8,128,256]{2,1,0:T(8,128)(2,1)S(1)} collective-permute-done((bf16[8,128,256]{2,1,0:T(8,128)(2,1)}, bf16[8,128,256]{2,1,0:T(8,128)(2,1)S(1)}, u32[]{:S(2)}, u32[]{:S(2)}) %collective-permute-start.20) | collective-permute-done | bytes 524320 | tf_op jit(solution)/shard_map/ppermute | solution.py:269
  147.5 19.4 %collective-permute-done.18.refs_2_ = bf16[8,128,256]{2,1,0:T(8,128)(2,1)S(1)} collective-permute-done((bf16[8,128,256]{2,1,0:T(8,128)(2,1)}, bf16[8,128,256]{2,1,0:T(8,128)(2,1)S(1)}, u32[]{:S(2)}, u32[]{:S(2)}) %collective-permute-start.18) | collective-permute-done | bytes 524320 | tf_op jit(solution)/shard_map/ppermute | solution.py:269
  167.0 1.2 last_backward.1
  (114 shorter events, 3.5 us)
Async XLA Ops:
  0.6 28.3 %collective-permute-start.6 = (bf16[1024,256]{1,0:T(8,128)(2,1)}, bf16[1024,256]{1,0:T(8,128)(2,1)S(1)}, u32[]{:S(2)}, u32[]{:S(2)}) collective-permute-start(bf16[1024,256]{1,0:T(8,128)(2,1)} %feats.3), channel_id=1, source_target_pairs={{0,4},{1,5},{2,6},{3,7},{4,0},{5,1},{6,2},{7,3},{8,12},{9,13},{10,... | collective-permute-start | bytes 1572872 | tf_op jit(solution)/shard_map/ppermute | solution.py:269
  4.7 28.3 %collective-permute-start.1 = (bf16[1024,256]{1,0:T(8,128)(2,1)}, bf16[1024,256]{1,0:T(8,128)(2,1)S(1)}, u32[]{:S(2)}, u32[]{:S(2)}) collective-permute-start(bf16[1024,256]{1,0:T(8,128)(2,1)} %feats.3), channel_id=1, source_target_pairs={{0,2},{1,3},{2,0},{3,1},{4,6},{5,7},{6,4},{7,5},{8,10},{9,11},{10,... | collective-permute-start | bytes 1572872 | tf_op jit(solution)/shard_map/ppermute | solution.py:269
  6.3 38.4 %collective-permute-start = (bf16[1024,256]{1,0:T(8,128)(2,1)}, bf16[1024,256]{1,0:T(8,128)(2,1)S(1)}, u32[]{:S(2)}, u32[]{:S(2)}) collective-permute-start(bf16[1024,256]{1,0:T(8,128)(2,1)} %feats.3), channel_id=1, source_target_pairs={{0,1},{1,0},{2,3},{3,2},{4,5},{5,4},{6,7},{7,6},{8,9},{9,8},{10,11... | collective-permute-start | bytes 1572872 | tf_op jit(solution)/shard_map/ppermute | solution.py:264
  6.3 28.6 %collective-permute-start.8 = (bf16[1024,256]{1,0:T(8,128)(2,1)}, bf16[1024,256]{1,0:T(8,128)(2,1)S(1)}, u32[]{:S(2)}, u32[]{:S(2)}) collective-permute-start(bf16[1024,256]{1,0:T(8,128)(2,1)} %feats.3), channel_id=1, source_target_pairs={{2,4},{3,5},{4,2},{5,3},{10,12},{11,13},{12,10},{13,11},{18,20},{1... | collective-permute-start | bytes 1572872 | tf_op jit(solution)/shard_map/ppermute | solution.py:269
  7.0 1.0 copy-start.3
  8.1 0.9 copy-start.6
  9.0 1.0 copy-start.9
  11.3 46.7 %copy-start.20 = (s32[1,1,8,32]{3,2,1,0:T(8,128)S(1)}, s32[1,1,8,32]{3,2,1,0:T(8,128)}, u32[]{:S(2)}) copy-start(s32[1,1,8,32]{3,2,1,0:T(8,128)} %param.17) | copy-start | bytes 3076
  29.0 34.5 %copy-start.11 = (bf16[1024,256]{1,0:T(8,128)(2,1)}, bf16[1024,256]{1,0:T(8,128)(2,1)S(1)}, u32[]{:S(2)}) copy-start(bf16[1024,256]{1,0:T(8,128)(2,1)S(1)} %collective-permute-done.6.refs_2_.refs_3_) | copy-start | bytes 1572868
  29.0 14.3 %collective-permute-start.9 = (bf16[1024,256]{1,0:T(8,128)(2,1)S(1)}, bf16[1024,256]{1,0:T(8,128)(2,1)}, u32[]{:S(2)}, u32[]{:S(2)}) collective-permute-start(bf16[1024,256]{1,0:T(8,128)(2,1)S(1)} %collective-permute-done.6.refs_2_.refs_3_), channel_id=1, source_target_pairs={{2,0},{3,1},{4,6},{5,7},{10,8},{11,9},{12,14},{13,15},{18,16},{19,... | collective-permute-start | bytes 1572872 | tf_op jit(solution)/shard_map/ppermute | solution.py:269
  31.2 29.8 %collective-permute-start.3 = (bf16[4,128,256]{2,1,0:T(8,128)(2,1)}, bf16[4,128,256]{2,1,0:T(8,128)(2,1)}, u32[]{:S(2)}, u32[]{:S(2)}) collective-permute-start(bf16[4,128,256]{2,1,0:T(8,128)(2,1)} %get-tuple-element.43), channel_id=1, source_target_pairs={{0,8},{8,0},{16,24},{24,16},{1,9},{9,1},{17,25},{25,17},{2,10},{10... | collective-permute-start | bytes 786440 | tf_op jit(solution)/shard_map/ppermute | solution.py:272
  33.0 13.0 %collective-permute-start.2 = (bf16[1024,256]{1,0:T(8,128)(2,1)S(1)}, bf16[1024,256]{1,0:T(8,128)(2,1)}, u32[]{:S(2)}, u32[]{:S(2)}) collective-permute-start(bf16[1024,256]{1,0:T(8,128)(2,1)S(1)} %collective-permute-done.1.refs_2_.refs_3_), channel_id=1, source_target_pairs={{0,1},{1,0},{2,3},{3,2},{4,5},{5,4},{6,7},{7,6},{8,9},{9,8},{10,11... | collective-permute-start | bytes 1572872 | tf_op jit(solution)/shard_map/ppermute | solution.py:264
  35.0 28.6 %collective-permute-start.7 = (bf16[1024,256]{1,0:T(8,128)(2,1)S(1)}, bf16[1024,256]{1,0:T(8,128)(2,1)}, u32[]{:S(2)}, u32[]{:S(2)}) collective-permute-start(bf16[1024,256]{1,0:T(8,128)(2,1)S(1)} %collective-permute-done.6.refs_2_.refs_3_), channel_id=1, source_target_pairs={{0,1},{1,0},{2,3},{3,2},{4,5},{5,4},{6,7},{7,6},{8,9},{9,8},{10,11... | collective-permute-start | bytes 1572872 | tf_op jit(solution)/shard_map/ppermute | solution.py:264
  44.4 22.2 %collective-permute-start.10 = (bf16[1024,256]{1,0:T(8,128)(2,1)S(1)}, bf16[1024,256]{1,0:T(8,128)(2,1)S(1)}, u32[]{:S(2)}, u32[]{:S(2)}) collective-permute-start(bf16[1024,256]{1,0:T(8,128)(2,1)S(1)} %add.90.block_b.refs_2_), channel_id=1, source_target_pairs={{0,1},{1,0},{2,3},{3,2},{4,5},{5,4},{6,7},{7,6},{8,9},{9,8},{10,11... | collective-permute-start | bytes 1572872 | tf_op jit(solution)/shard_map/ppermute | solution.py:264
  44.6 3.0 %copy-start.28 = (s32[2]{0:T(128)}, s32[2]{0:T(128)S(1)}, u32[]{:S(2)}) copy-start(s32[2]{0:T(128)S(1)} %pad_add_fusion.3.ids) | copy-start | bytes 28
  44.7 16.3 %copy-start.34 = (s32[2]{0:T(128)}, s32[2]{0:T(128)S(1)}, u32[]{:S(2)}) copy-start(s32[2]{0:T(128)S(1)} %pad_add_fusion.2.ids) | copy-start | bytes 28
  44.7 16.3 %collective-permute-start.4 = (bf16[4,128,256]{2,1,0:T(8,128)(2,1)}, bf16[4,128,256]{2,1,0:T(8,128)(2,1)}, u32[]{:S(2)}, u32[]{:S(2)}) collective-permute-start(bf16[4,128,256]{2,1,0:T(8,128)(2,1)} %get-tuple-element.42), channel_id=1, source_target_pairs={{0,16},{8,24},{16,0},{24,8},{1,17},{9,25},{17,1},{25,9},{2,18},{10... | collective-permute-start | bytes 786440 | tf_op jit(solution)/shard_map/ppermute | solution.py:272
  46.0 15.1 %collective-permute-start.5 = (bf16[4,128,256]{2,1,0:T(8,128)(2,1)}, bf16[4,128,256]{2,1,0:T(8,128)(2,1)}, u32[]{:S(2)}, u32[]{:S(2)}) collective-permute-start(bf16[4,128,256]{2,1,0:T(8,128)(2,1)} %get-tuple-element.41), channel_id=1, source_target_pairs={{0,24},{8,16},{16,8},{24,0},{1,25},{9,17},{17,9},{25,1},{2,26},{10... | collective-permute-start | bytes 786440 | tf_op jit(solution)/shard_map/ppermute | solution.py:272
  47.5 16.1 %copy-start.36 = (s32[2]{0:T(128)}, s32[2]{0:T(128)S(1)}, u32[]{:S(2)}) copy-start(s32[2]{0:T(128)S(1)} %pad_add_fusion.1.ids) | copy-start | bytes 28
  47.5 19.1 %copy-start.30 = (s32[2]{0:T(128)}, s32[2]{0:T(128)S(1)}, u32[]{:S(2)}) copy-start(s32[2]{0:T(128)S(1)} %pad_add_fusion.ids) | copy-start | bytes 28
  47.5 3.4 %copy-start = (bf16[1,1,8,32,128,128]{5,4,3,2,1,0:T(8,128)(2,1)S(1)}, bf16[1,1,8,32,128,128]{5,4,3,2,1,0:T(8,128)(2,1)}, u32[]{:S(2)}) copy-start(bf16[1,1,8,32,128,128]{5,4,3,2,1,0:T(8,128)(2,1)} %param.16) | copy-start | bytes 25165828
  50.9 1.0 copy-start.4
  52.0 0.9 copy-start.7
  54.9 3.4 %copy-start.1 = (bf16[1,1,8,32,128,128]{5,4,3,2,1,0:T(8,128)(2,1)S(1)}, bf16[1,1,8,32,128,128]{5,4,3,2,1,0:T(8,128)(2,1)}, u32[]{:S(2)}) copy-start(bf16[1,1,8,32,128,128]{5,4,3,2,1,0:T(8,128)(2,1)} %param.16) | copy-start | bytes 25165828
  58.3 2.7 %copy-start.24 = (s32[4,1,16,1]{2,3,1,0:T(1,128)S(1)}, s32[4,1,16,1]{2,3,1,0:T(1,128)}, u32[]{:S(2)}) copy-start(s32[4,1,16,1]{2,3,1,0:T(1,128)} %param.22) | copy-start | bytes 772
  58.3 2.7 %copy-start.27 = (s32[4,1,16]{2,1,0:T(1,128)S(1)}, s32[4,1,16]{2,1,0:T(1,128)}, u32[]{:S(2)}) copy-start(s32[4,1,16]{2,1,0:T(1,128)} %param.23) | copy-start | bytes 772
  58.3 5.3 %copy-start.8 = (bf16[256,256]{1,0:T(8,128)(2,1)S(1)}, bf16[256,256]{1,0:T(8,128)(2,1)}, u32[]{:S(2)}) copy-start(bf16[256,256]{1,0:T(8,128)(2,1)} %refs_5_.1) | copy-start | bytes 393220
  66.6 10.0 %copy-start.22 = (s32[1,1,8,32]{3,2,1,0:T(8,128)S(1)}, s32[1,1,8,32]{3,2,1,0:T(8,128)}, u32[]{:S(2)}) copy-start(s32[1,1,8,32]{3,2,1,0:T(8,128)} %param.18) | copy-start | bytes 3076
  66.7 10.0 %copy-start.26 = (s32[1,1,8]{2,1,0:T(1,128)S(1)}, s32[1,1,8]{2,1,0:T(1,128)}, u32[]{:S(2)}) copy-start(s32[1,1,8]{2,1,0:T(1,128)} %param.19) | copy-start | bytes 100
  71.4 13.5 %copy-start.12 = (bf16[1024,256]{1,0:T(8,128)(2,1)S(1)}, bf16[1024,256]{1,0:T(8,128)(2,1)}, u32[]{:S(2)}) copy-start(bf16[1024,256]{1,0:T(8,128)(2,1)} %copy-done.11) | copy-start | bytes 1572868
  72.3 27.9 %collective-permute-start.11 = (bf16[4,128,256]{2,1,0:T(8,128)(2,1)}, bf16[4,128,256]{2,1,0:T(8,128)(2,1)}, u32[]{:S(2)}, u32[]{:S(2)}) collective-permute-start(bf16[4,128,256]{2,1,0:T(8,128)(2,1)} %get-tuple-element.39), channel_id=1, source_target_pairs={{0,8},{8,0},{16,24},{24,16},{1,9},{9,1},{17,25},{25,17},{2,10},{10... | collective-permute-start | bytes 786440 | tf_op jit(solution)/shard_map/ppermute | solution.py:272
  74.4 25.8 %collective-permute-start.12 = (bf16[4,128,256]{2,1,0:T(8,128)(2,1)}, bf16[4,128,256]{2,1,0:T(8,128)(2,1)}, u32[]{:S(2)}, u32[]{:S(2)}) collective-permute-start(bf16[4,128,256]{2,1,0:T(8,128)(2,1)} %get-tuple-element.38), channel_id=1, source_target_pairs={{0,16},{8,24},{16,0},{24,8},{1,17},{9,25},{17,1},{25,9},{2,18},{10... | collective-permute-start | bytes 786440 | tf_op jit(solution)/shard_map/ppermute | solution.py:272
  75.7 24.6 %collective-permute-start.13 = (bf16[4,128,256]{2,1,0:T(8,128)(2,1)}, bf16[4,128,256]{2,1,0:T(8,128)(2,1)}, u32[]{:S(2)}, u32[]{:S(2)}) collective-permute-start(bf16[4,128,256]{2,1,0:T(8,128)(2,1)} %get-tuple-element.37), channel_id=1, source_target_pairs={{0,24},{8,16},{16,8},{24,0},{1,25},{9,17},{17,9},{25,1},{2,26},{10... | collective-permute-start | bytes 786440 | tf_op jit(solution)/shard_map/ppermute | solution.py:272
  76.7 3.4 %copy-start.2 = (bf16[1,1,8,32,128,128]{5,4,3,2,1,0:T(8,128)(2,1)S(1)}, bf16[1,1,8,32,128,128]{5,4,3,2,1,0:T(8,128)(2,1)}, u32[]{:S(2)}) copy-start(bf16[1,1,8,32,128,128]{5,4,3,2,1,0:T(8,128)(2,1)} %param.16) | copy-start | bytes 25165828
  80.6 10.2 %copy-start.35 = (s32[2]{0:T(128)S(1)}, s32[2]{0:T(128)}, u32[]{:S(2)}) copy-start(s32[2]{0:T(128)} %copy-done.34) | copy-start | bytes 28
  83.9 1.0 copy-start.16
  83.9 23.9 %collective-permute-start.14 = (bf16[8,128,256]{2,1,0:T(8,128)(2,1)}, bf16[8,128,256]{2,1,0:T(8,128)(2,1)}, u32[]{:S(2)}, u32[]{:S(2)}) collective-permute-start(bf16[8,128,256]{2,1,0:T(8,128)(2,1)} %get-tuple-element.30), channel_id=1, source_target_pairs={{0,1},{1,0},{2,3},{3,2},{4,5},{5,4},{6,7},{7,6},{8,9},{9,8},{10,11... | collective-permute-start | bytes 1572872 | tf_op jit(solution)/shard_map/ppermute | solution.py:264
  85.5 10.2 %slice-start = ((s8[8388608]{0:T(1024)(128)(4,1)}), s8[4194304]{0:T(1024)(128)(4,1)S(1)}, s32[]{:S(2)}) async-start(s8[8388608]{0:T(1024)(128)(4,1)} %bitcast.48), calls=%async_computation | async-start | bytes 8388608
  85.5 10.3 %copy-start.5 = (bf16[1024,256]{1,0:T(8,128)(2,1)S(1)}, bf16[1024,256]{1,0:T(8,128)(2,1)}, u32[]{:S(2)}) copy-start(bf16[1024,256]{1,0:T(8,128)(2,1)} %feats.3) | copy-start | bytes 1572868
  85.5 10.3 %copy-start.29 = (s32[2]{0:T(128)S(1)}, s32[2]{0:T(128)}, u32[]{:S(2)}) copy-start(s32[2]{0:T(128)} %copy-done.28) | copy-start | bytes 28
  89.1 1.0 copy-start.13
  90.8 4.9 %slice-start.1 = ((s8[8388608]{0:T(1024)(128)(4,1)}), s8[4194304]{0:T(1024)(128)(4,1)S(1)}, s32[]{:S(2)}) async-start(s8[8388608]{0:T(1024)(128)(4,1)} %bitcast.48), calls=%async_computation.1 | async-start | bytes 8388608
  90.8 9.4 %copy-start.10 = (bf16[1,1,16,128,128]{4,3,2,1,0:T(8,128)(2,1)S(1)}, bf16[1,1,16,128,128]{4,3,2,1,0:T(8,128)(2,1)}, u32[]{:S(2)}) copy-start(bf16[1,1,16,128,128]{4,3,2,1,0:T(8,128)(2,1)} %param.20) | copy-start | bytes 1572868
  90.8 9.4 %copy-start.33 = (s32[1,1,16]{2,1,0:T(1,128)S(1)}, s32[1,1,16]{2,1,0:T(1,128)}, u32[]{:S(2)}) copy-start(s32[1,1,16]{2,1,0:T(1,128)} %param.21) | copy-start | bytes 196
  93.9 1.0 copy-start.15
  95.7 8.8 %copy-start.39 = (bf16[8,128,256]{2,1,0:T(8,128)(2,1)S(1)}, bf16[8,128,256]{2,1,0:T(8,128)(2,1)}, u32[]{:S(2)}) copy-start(bf16[8,128,256]{2,1,0:T(8,128)(2,1)} %copy-done.38) | copy-start | bytes 1572868
  95.8 30.3 %copy-start.14 = (f32[8,128,256]{2,1,0:T(8,128)S(1)}, f32[8,128,256]{2,1,0:T(8,128)}, u32[]{:S(2)}) copy-start(f32[8,128,256]{2,1,0:T(8,128)} %copy-done.13) | copy-start | bytes 3145732
  102.4 1.0 copy-start.17
  103.3 63.6 %copy-start.18 = (f32[8,128,256]{2,1,0:T(8,128)S(1)}, f32[8,128,256]{2,1,0:T(8,128)}, u32[]{:S(2)}) copy-start(f32[8,128,256]{2,1,0:T(8,128)} %copy-done.17) | copy-start | bytes 3145732
  103.4 2.0 %collective-permute-start.22 = (bf16[128,256]{1,0:T(8,128)(2,1)S(1)}, bf16[128,256]{1,0:T(8,128)(2,1)S(1)}, u32[]{:S(2)}, u32[]{:S(2)}) collective-permute-start(bf16[128,256]{1,0:T(8,128)(2,1)S(1)} %dynamic-slice_bitcast_fusion), channel_id=1, source_target_pairs={{0,1},{1,0},{2,3},{3,2},{4,5},{5,4},{6,7},{7,6},{8,9},{9,8},{10,11... | collective-permute-start | bytes 196616 | tf_op jit(solution)/shard_map/ppermute | solution.py:264
  104.5 8.6 %collective-permute-start.19 = (bf16[8,128,256]{2,1,0:T(8,128)(2,1)}, bf16[8,128,256]{2,1,0:T(8,128)(2,1)S(1)}, u32[]{:S(2)}, u32[]{:S(2)}) collective-permute-start(bf16[8,128,256]{2,1,0:T(8,128)(2,1)} %copy-done.40), channel_id=1, source_target_pairs={{0,1},{1,0},{2,3},{3,2},{4,5},{5,4},{6,7},{7,6},{8,9},{9,8},{10,11... | collective-permute-start | bytes 1572872 | tf_op jit(solution)/shard_map/ppermute | solution.py:264
  104.6 16.2 %collective-permute-start.16 = (bf16[8,128,256]{2,1,0:T(8,128)(2,1)S(1)}, bf16[8,128,256]{2,1,0:T(8,128)(2,1)S(1)}, u32[]{:S(2)}, u32[]{:S(2)}) collective-permute-start(bf16[8,128,256]{2,1,0:T(8,128)(2,1)S(1)} %copy-done.39), channel_id=1, source_target_pairs={{0,1},{1,0},{2,3},{3,2},{4,5},{5,4},{6,7},{7,6},{8,9},{9,8},{10,11... | collective-permute-start | bytes 1572872 | tf_op jit(solution)/shard_map/ppermute | solution.py:264
  105.4 5.8 %collective-permute-start.23 = (bf16[128,256]{1,0:T(8,128)(2,1)S(1)}, bf16[128,256]{1,0:T(8,128)(2,1)S(1)}, u32[]{:S(2)}, u32[]{:S(2)}) collective-permute-start(bf16[128,256]{1,0:T(8,128)(2,1)S(1)} %fusion), channel_id=1, source_target_pairs={{0,8},{8,0},{16,24},{24,16},{1,9},{9,1},{17,25},{25,17},{2,10},{10... | collective-permute-start | bytes 196616 | tf_op jit(solution)/shard_map/ppermute | solution.py:272
  106.5 6.2 %collective-permute-start.24 = (bf16[128,256]{1,0:T(8,128)(2,1)S(1)}, bf16[128,256]{1,0:T(8,128)(2,1)S(1)}, u32[]{:S(2)}, u32[]{:S(2)}) collective-permute-start(bf16[128,256]{1,0:T(8,128)(2,1)S(1)} %fusion), channel_id=1, source_target_pairs={{0,16},{8,24},{16,0},{24,8},{1,17},{9,25},{17,1},{25,9},{2,18},{10... | collective-permute-start | bytes 196616 | tf_op jit(solution)/shard_map/ppermute | solution.py:272
  107.8 5.2 %collective-permute-start.25 = (bf16[128,256]{1,0:T(8,128)(2,1)S(1)}, bf16[128,256]{1,0:T(8,128)(2,1)S(1)}, u32[]{:S(2)}, u32[]{:S(2)}) collective-permute-start(bf16[128,256]{1,0:T(8,128)(2,1)S(1)} %fusion), channel_id=1, source_target_pairs={{0,24},{8,16},{16,8},{24,0},{1,25},{9,17},{17,9},{25,1},{2,26},{10... | collective-permute-start | bytes 196616 | tf_op jit(solution)/shard_map/ppermute | solution.py:272
  111.2 14.1 %collective-permute-start.17 = (bf16[8,128,256]{2,1,0:T(8,128)(2,1)}, bf16[8,128,256]{2,1,0:T(8,128)(2,1)S(1)}, u32[]{:S(2)}, u32[]{:S(2)}) collective-permute-start(bf16[8,128,256]{2,1,0:T(8,128)(2,1)} %add_convert_fusion.2), channel_id=1, source_target_pairs={{0,2},{1,3},{6,4},{7,5},{8,10},{9,11},{14,12},{15,13},{16,18},{17,... | collective-permute-start | bytes 1572872 | tf_op jit(solution)/shard_map/ppermute | solution.py:269
  112.7 24.3 %collective-permute-start.21 = (bf16[8,128,256]{2,1,0:T(8,128)(2,1)}, bf16[8,128,256]{2,1,0:T(8,128)(2,1)S(1)}, u32[]{:S(2)}, u32[]{:S(2)}) collective-permute-start(bf16[8,128,256]{2,1,0:T(8,128)(2,1)} %get-tuple-element.35), channel_id=1, source_target_pairs={{0,1},{1,0},{2,3},{3,2},{4,5},{5,4},{6,7},{7,6},{8,9},{9,8},{10,11... | collective-permute-start | bytes 1572872 | tf_op jit(solution)/shard_map/ppermute | solution.py:264
  113.0 14.0 %collective-permute-start.26 = (bf16[128,256]{1,0:T(8,128)(2,1)S(1)}, bf16[128,256]{1,0:T(8,128)(2,1)S(1)}, u32[]{:S(2)}, u32[]{:S(2)}) collective-permute-start(bf16[128,256]{1,0:T(8,128)(2,1)S(1)} %add_convert_fusion.3), channel_id=1, source_target_pairs={{0,2},{1,3},{2,0},{3,1},{4,6},{5,7},{6,4},{7,5},{8,10},{9,11},{10,... | collective-permute-start | bytes 196616 | tf_op jit(solution)/shard_map/ppermute | solution.py:269
  113.1 21.7 %collective-permute-start.27 = (bf16[128,256]{1,0:T(8,128)(2,1)S(1)}, bf16[128,256]{1,0:T(8,128)(2,1)S(1)}, u32[]{:S(2)}, u32[]{:S(2)}) collective-permute-start(bf16[128,256]{1,0:T(8,128)(2,1)S(1)} %add_convert_fusion.3), channel_id=1, source_target_pairs={{0,4},{1,5},{2,6},{3,7},{4,0},{5,1},{6,2},{7,3},{8,12},{9,13},{10,... | collective-permute-start | bytes 196616 | tf_op jit(solution)/shard_map/ppermute | solution.py:269
  120.8 14.1 %collective-permute-start.28 = (bf16[128,256]{1,0:T(8,128)(2,1)S(1)}, bf16[128,256]{1,0:T(8,128)(2,1)S(1)}, u32[]{:S(2)}, u32[]{:S(2)}) collective-permute-start(bf16[128,256]{1,0:T(8,128)(2,1)S(1)} %add_convert_fusion.3), channel_id=1, source_target_pairs={{0,6},{1,7},{2,4},{3,5},{4,2},{5,3},{6,0},{7,1},{8,14},{9,15},{10,... | collective-permute-start | bytes 196616 | tf_op jit(solution)/shard_map/ppermute | solution.py:269
  125.3 22.2 %collective-permute-start.15 = (bf16[8,128,256]{2,1,0:T(8,128)(2,1)}, bf16[8,128,256]{2,1,0:T(8,128)(2,1)S(1)}, u32[]{:S(2)}, u32[]{:S(2)}) collective-permute-start(bf16[8,128,256]{2,1,0:T(8,128)(2,1)} %add_convert_fusion.2), channel_id=1, source_target_pairs={{2,4},{3,5},{4,2},{5,3},{10,12},{11,13},{12,10},{13,11},{18,20},{1... | collective-permute-start | bytes 1572872 | tf_op jit(solution)/shard_map/ppermute | solution.py:269
  127.0 20.5 %collective-permute-start.20 = (bf16[8,128,256]{2,1,0:T(8,128)(2,1)}, bf16[8,128,256]{2,1,0:T(8,128)(2,1)S(1)}, u32[]{:S(2)}, u32[]{:S(2)}) collective-permute-start(bf16[8,128,256]{2,1,0:T(8,128)(2,1)} %add_convert_fusion), channel_id=1, source_target_pairs={{0,2},{1,3},{2,0},{3,1},{4,6},{5,7},{6,4},{7,5},{8,10},{9,11},{10,... | collective-permute-start | bytes 1572872 | tf_op jit(solution)/shard_map/ppermute | solution.py:269
  134.8 32.1 %collective-permute-start.18 = (bf16[8,128,256]{2,1,0:T(8,128)(2,1)}, bf16[8,128,256]{2,1,0:T(8,128)(2,1)S(1)}, u32[]{:S(2)}, u32[]{:S(2)}) collective-permute-start(bf16[8,128,256]{2,1,0:T(8,128)(2,1)} %add_convert_fusion.1), channel_id=1, source_target_pairs={{0,4},{1,5},{2,6},{3,7},{4,0},{5,1},{6,2},{7,3},{8,12},{9,13},{10,... | collective-permute-start | bytes 1572872 | tf_op jit(solution)/shard_map/ppermute | solution.py:269
  134.9 1.4 collective-permute-start.29
  (9 other events, 6.1 us)

commit v2 on v1

v2 whole, which is shorter than its diff:
```python
import functools
import math

import jax
import jax.numpy as jnp
from jax import lax
from jax.experimental import pallas as pl
from jax.experimental.pallas import tpu as pltpu
from jax.sharding import PartitionSpec as P

F32 = jnp.float32
BF16 = jnp.bfloat16
UNROLL = 16
SMEM = pl.BlockSpec(memory_space=pltpu.SMEM)
VMEM = pl.BlockSpec(memory_space=pltpu.VMEM)
HBM = pl.BlockSpec(memory_space=pltpu.HBM)


def dot(a, b, dims):
    return lax.dot_general(a, b, (dims, ((), ())), preferred_element_type=F32)


def call(kernel, name, out_shape, in_specs, out_specs, scratch, flops, moved, vmem=14):
    return pl.pallas_call(
        kernel,
        out_shape=out_shape,
        in_specs=in_specs,
        out_specs=out_specs,
        scratch_shapes=scratch,
        compiler_params=pltpu.CompilerParams(vmem_limit_bytes=vmem << 20),
        cost_estimate=pl.CostEstimate(flops=flops, bytes_accessed=moved, transcendentals=0),
        name=name,
    )


class Meta:
    def __init__(self, blocks, slots):
        self.slots = slots
        starts = [0]
        for size in (3, blocks, blocks * slots, blocks * slots):
            starts.append(starts[-1] + size)
        self.at = starts

    def block(self, ref, mask, other):
        chip = ref[1] ^ mask
        return 2 * chip + (ref[2] ^ 1 if other else ref[2])

    def count(self, ref, block):
        return ref[self.at[1] + block]

    def row(self, ref, block, slot):
        return ref[self.at[2] + block * self.slots + slot]

    def col(self, ref, block, slot):
        return ref[self.at[3] + block * self.slots + slot]


def stage_tiles(meta, pos, vals, *refs):
    outs, sem = refs[:-1], refs[-1]
    copies = []
    for mask, out in enumerate(outs):
        for k, side in enumerate((1, 0)):
            block = vals.at[meta.block(pos, mask, side)]
            copies.append(pltpu.make_async_copy(block, out.at[k], sem.at[2 * mask + k]))
    for copy in copies:
        copy.start()
    for copy in copies:
        copy.wait()


def tile_loop(meta, ints, mask, sides, forward, tiles, sources, total):
    blocks = [meta.block(ints, mask, side) for side in sides]
    trash = total.shape[0] - 1
    row_tiles = trash // (1 if forward else len(blocks))
    first = meta.count(ints, blocks[0])
    used = first if len(blocks) == 1 else first + meta.count(ints, blocks[1])
    contract = ((1,), (0,)) if forward else ((0,), (0,))

    def body(step, carry):
        products = []
        for u in range(UNROLL):
            at = step * UNROLL + u
            live = at < used
            if len(blocks) == 1:
                block, late, shift, slot = blocks[0], 1 - sides[0], 0, jnp.where(live, at, 0)
            else:
                late = jnp.where(at >= first, 1, 0)
                block = jnp.where(late == 1, blocks[1], blocks[0])
                shift = late * row_tiles
                slot = jnp.where(live, at - late * first, 0)
            row, col = meta.row(ints, block, slot), meta.col(ints, block, slot)
            pick, place = (col + shift, row) if forward else (row, col + shift)
            place = jnp.where(live, place, trash)
            products.append((place, dot(tiles[late, slot], sources[pick], contract)))
        for place, product in products:
            total[place] += product
        return carry

    lax.fori_loop(0, (used + UNROLL - 1) // UNROLL, body, 0)


def gather_panels(parts, panel):
    start = 0
    for part in parts:
        panel[pl.ds(start, part.shape[0])] = part[...]
        start += part.shape[0]


def forward_blocks(meta, mask, sides, has_acc, ints, *refs):
    acc, refs = (refs[0], refs[1:]) if has_acc else (None, refs)
    feats, (tiles, out, panel, total) = refs[:-4], refs[-4:]
    row_tiles = out.shape[0]
    gather_panels(feats, panel)
    if has_acc:
        total[pl.ds(0, row_tiles)] = acc[...]
    else:
        total[...] = jnp.zeros_like(total)
    tile_loop(meta, ints, mask, sides, True, tiles, panel, total)
    out[...] = total[pl.ds(0, row_tiles)]


def hub_products(groups, pos, dest, cols, feats, tiles, send, tally):
    cap = send.shape[1]
    me = pos[0]
    for k in range(groups):
        tally[k] = 0
    for h in range(tiles.shape[0]):
        to = dest[me, h] ^ me
        rank = jnp.minimum(tally[to], cap - 1)
        tally[to] = rank + 1
        send[to, rank] = dot(tiles[h], feats[cols[h]], ((1,), (0,))).astype(BF16)


def each_hub(pos, dest, groups, cap, visit):
    me = pos[0]
    for k in range(groups):
        source = me ^ k

        def body(h, rank, k=k, source=source):
            mine = dest[source, h] == me

            @pl.when(mine)
            def _():
                visit(k, source, h, jnp.minimum(rank, cap - 1))

            return rank + mine.astype(jnp.int32)

        lax.fori_loop(0, dest.shape[1], body, jnp.int32(0))


def hub_add(pos, dest, rows, *refs):
    acc, parts, out = refs[0], refs[1:-1], refs[-1]
    out[...] = acc[...]

    def visit(k, source, h, rank):
        out[rows[source, h]] += parts[k][rank].astype(F32)

    each_hub(pos, dest, len(parts), parts[0].shape[0], visit)


def last_forward(meta, mask, ints, dest, rows, acc, *refs):
    feats, refs = refs[:-9], refs[-9:]
    weight, tiles, cot, layer_out, grad, back, gw, panel, total = refs
    row_tiles = grad.shape[0]
    gather_panels(feats, panel)
    total[pl.ds(0, row_tiles)] = acc[...]
    tile_loop(meta, ints, mask, (1,), True, tiles, panel, total)
    sums = jnp.zeros(gw.shape, F32)
    for r in range(row_tiles):
        neighbours = total[r].astype(BF16)
        agg = dot(neighbours, weight[...], ((1,), (0,)))
        sig = jax.nn.sigmoid(agg)
        layer_out[r] = (agg * sig).astype(BF16)
        slope = sig * (1.0 + agg * (1.0 - sig))
        grad[r] = (cot[r].astype(F32) * slope).astype(BF16)
        sums += dot(neighbours, grad[r], ((0,), (0,)))
    gw[...] = sums

    def visit(k, source, h, rank):
        back[k, rank] = grad[rows[source, h]]

    each_hub(ints, dest, back.shape[0], back.shape[1], visit)


def backward_blocks(meta, mask, sides, ints, grad, tiles, *refs):
    parts, total = refs[:-1], refs[-1]
    row_tiles = grad.shape[0]
    total[...] = jnp.zeros_like(total)
    tile_loop(meta, ints, mask, sides, False, tiles, grad, total)
    for k, part in enumerate(parts):
        part[...] = total[pl.ds(k * row_tiles, row_tiles)].astype(part.dtype)


def last_products(groups, meta, ints, dest, cols, grad, tiles, hub_tiles, *refs):
    parts, (other, out, total, slots, tally) = refs[:groups], refs[groups:]
    row_tiles, cap = out.shape[0], parts[0].shape[0]
    me = ints[0]
    total[...] = jnp.zeros_like(total)
    tile_loop(meta, ints, 0, (1, 0), False, tiles, grad, total)
    other[...] = total[pl.ds(0, row_tiles)].astype(BF16)
    for k in range(groups):
        slots[pl.ds(k * cap, cap)] = parts[k][...]
        tally[k] = 0
    products = []
    for h in range(hub_tiles.shape[0]):
        source = dest[me, h] ^ me
        rank = jnp.minimum(tally[source], cap - 1)
        tally[source] = rank + 1
        products.append((cols[h], dot(hub_tiles[h], slots[source * cap + rank], ((0,), (0,)))))
        if len(products) == 8 or h == hub_tiles.shape[0] - 1:
            for place, product in products:
                total[row_tiles + place] += product
            products = []
    out[...] = total[pl.ds(row_tiles, row_tiles)]


def last_backward(count, *refs):
    own, parts, weight, out = refs[0], refs[1 : 1 + count], refs[-2], refs[-1]
    sums = own[...]
    for part in parts:
        sums = sums + part[pl.ds(0, own.shape[0])].astype(F32)
    out[...] = dot(sums.astype(BF16).reshape(out.shape), weight[...], ((1,), (1,))).astype(BF16)


def after(value, *others):
    return lax.optimization_barrier((value, *others))[0]


def tree_sum(values):
    while len(values) > 1:
        values = [a + b for a, b in zip(values[::2], values[1::2])]
    return values[0]


def local(
    feats,
    weight,
    cotangent,
    labels,
    tile_vals,
    tile_row,
    tile_col,
    tile_count,
    hub_vals,
    hub_col,
    hub_dest,
    hub_row,
):
    n_blocks = lax.axis_size("blk")
    n_groups = lax.axis_size("grp")
    n_chips = n_blocks // 2
    my_block = lax.axis_index("blk").astype(jnp.int32)
    my_group = lax.axis_index("grp").astype(jnp.int32)
    core = my_block % 2
    rows_dev, width = feats.shape
    size = tile_vals.shape[-1]
    row_tiles = rows_dev // size
    slots = tile_vals.shape[3]
    hubs = hub_vals.shape[2]
    cap = max(2, hubs // 4)
    vals = tile_vals[0, 0]
    hub_tiles = hub_vals[0, 0]
    panel = (row_tiles, size, width)
    relay = n_chips == 4
    meta = Meta(n_blocks, slots)
    pos = jnp.stack([my_group, my_block // 2, core])
    ints = jnp.concatenate([pos] + [v.reshape(-1) for v in (tile_count, tile_row, tile_col)])
    dest, hub_rows, hub_cols = hub_dest[:, 0, :, 0], hub_row[:, 0, :], hub_col[0, 0]

    def swap(value):
        return lax.ppermute(value, "blk", [(i, i ^ 1) for i in range(n_blocks)])

    def across(value, mask, chips=None):
        chosen = range(n_chips) if chips is None else chips
        pairs = [(2 * c + k, 2 * (c ^ mask) + k) for c in chosen for k in range(2)]
        return lax.ppermute(value, "blk", pairs)

    def group(value, mask):
        return lax.ppermute(value, "grp", [(i, i ^ mask) for i in range(n_groups)])

    moved, tile_flops = 100 * (4 << 20), 100 * 2 * size * size * width
    block_flops = slots * tile_flops
    acc_shape = jax.ShapeDtypeStruct(panel, F32)
    tiles = call(
        functools.partial(stage_tiles, meta),
        "stage_tiles",
        (jax.ShapeDtypeStruct((2, slots, size, size), BF16),) * n_chips,
        [SMEM, HBM],
        (VMEM,) * n_chips,
        [pltpu.SemaphoreType.DMA((n_blocks,))],
        1,
        moved,
        48,
    )(pos, vals)

    def forward(mask, sides, acc, blocks):
        return call(
            functools.partial(forward_blocks, meta, mask, sides, acc is not None),
            "forward_blocks",
            acc_shape,
            [SMEM] + [VMEM] * (len(blocks) + (1 if acc is None else 2)),
            VMEM,
            [
                pltpu.VMEM((len(sides) * row_tiles, size, width), BF16),
                pltpu.VMEM((row_tiles + 1, size, width), F32),
            ],
            len(sides) * block_flops,
            moved,
        )(ints, *(() if acc is None else (acc,)), *blocks, tiles[mask])

    def backward(mask, sides, grad):
        return call(
            functools.partial(backward_blocks, meta, mask, sides),
            "backward_blocks",
            tuple(jax.ShapeDtypeStruct(panel, BF16 if side else F32) for side in sides),
            [SMEM, VMEM, VMEM],
            (VMEM,) * len(sides),
            [
                pltpu.VMEM((len(sides) * row_tiles + 1, size, width), F32),
            ],
            len(sides) * block_flops,
            moved,
        )(ints, grad, tiles[mask])

    last = n_chips - 1
    feats = feats.reshape(panel)
    got, pairs = {0: [feats]}, {0: [swap(feats)]}
    if relay:
        got[2] = [across(feats, 2)]
        got[1] = [across(feats, 1)]
    else:
        for mask in range(1, n_chips):
            got[mask] = [across(feats, mask)]

    send = call(
        functools.partial(hub_products, n_groups),
        "hub_products",
        jax.ShapeDtypeStruct((n_groups, cap, size, width), BF16),
        [SMEM, SMEM, SMEM, VMEM, VMEM],
        VMEM,
        [pltpu.SMEM((n_groups,), jnp.int32)],
        hubs * tile_flops,
        moved,
    )(pos, dest, hub_cols, after(feats, *pairs[0]), hub_tiles)
    hub_parts = [send[0]] + [group(send[k], k) for k in range(1, n_groups)]
    acc = forward(0, (1, 0), None, (*pairs[0], *got[0]))
    if relay:
        passed = across(after(got[2][0], acc), 1, (1, 2))
        direct = across(after(feats, acc, got[2][0]), 3, (1, 2))
    acc = call(
        hub_add,
        "hub_add",
        acc_shape,
        [SMEM] * 3 + [VMEM] * (1 + n_groups),
        VMEM,
        [],
        1 << 20,
        moved,
    )(pos, dest, hub_rows, acc, *hub_parts)
    for mask in range(1, last):
        pairs[mask] = [swap(part) for part in got[mask]]
        acc = forward(mask, (1, 0), acc, (*pairs[mask], *got[mask]))
    if relay:
        got[last] = [after(passed, acc) + direct]
    pairs[last] = [swap(part) for part in got[last]]
    acc = forward(last, (0,), acc, got[last])

    cot = jnp.where(labels[:, None] >= 0, cotangent, jnp.zeros_like(cotangent)).reshape(panel)
    layer_out, grad, back, gw = call(
        functools.partial(last_forward, meta, last),
        "last_forward",
        (
            jax.ShapeDtypeStruct(panel, BF16),
            jax.ShapeDtypeStruct(panel, BF16),
            jax.ShapeDtypeStruct((n_groups, cap, size, width), BF16),
            jax.ShapeDtypeStruct((width, width), F32),
        ),
        [SMEM] * 3 + [VMEM] * (4 + len(pairs[last])),
        (VMEM,) * 4,
        [
            pltpu.VMEM(panel, BF16),
            pltpu.VMEM((row_tiles + 1, size, width), F32),
        ],
        block_flops,
        moved,
    )(ints, dest, hub_rows, acc, *pairs[last], weight, tiles[last], cot)

    (part_other,) = backward(last, (1,), grad)
    theirs = swap(part_other)
    (part_own,) = backward(last, (0,), grad)
    both = (part_own + theirs.astype(F32)).astype(BF16)
    grad = after(grad, both)

    owns, theirs = {}, {}
    for mask in reversed(range(1, last)):
        part_other, owns[mask] = backward(mask, (1, 0), grad)
        theirs[mask] = swap(part_other)
        if mask == last - 1:
            gw = after(gw, owns[mask])

    halves = gw.reshape(2, -1, size, width).astype(BF16)
    kept = lax.dynamic_index_in_dim(halves, core, 0, keepdims=False)
    given = lax.dynamic_index_in_dim(halves, 1 - core, 0, keepdims=False)
    share = (kept.astype(F32) + swap(given).astype(F32)).astype(BF16)
    step = 1
    while step < n_groups:
        share = (share.astype(F32) + group(share, step).astype(F32)).astype(BF16)
        step *= 2

    if relay:
        from_ends = across(both, 1, (0, 3))
        middle = across(both, 3, (1, 2))
        from_ends = after(from_ends, middle, share, owns[1])
        far = (owns[2] + theirs[2].astype(F32) + from_ends.astype(F32)).astype(BF16)
        near = (owns[1] + theirs[1].astype(F32)).astype(BF16)
        back = after(back, far)
        far = across(jnp.concatenate([far, share]), 2)
        near = across(jnp.concatenate([near, share]), 1)
        arrived = [middle, far, near]
        shares = [share, near[row_tiles:], far[row_tiles:], across(share, 3)]
    else:
        arrived = [across(both, last)]
        for mask in reversed(range(1, last)):
            arrived.append(across((owns[mask] + theirs[mask].astype(F32)).astype(BF16), mask))
        shares = [share] + [across(share, m) for m in range(1, n_chips)]

    back_parts = [back[0]] + [group(back[k], k) for k in range(1, n_groups)]
    part_other, own_sum = call(
        functools.partial(last_products, n_groups, meta),
        "last_products",
        (jax.ShapeDtypeStruct(panel, BF16), acc_shape),
        [SMEM] * 3 + [VMEM] * (3 + n_groups),
        (VMEM, VMEM),
        [
            pltpu.VMEM((2 * row_tiles + 1, size, width), F32),
            pltpu.VMEM((n_groups * cap, size, width), BF16),
            pltpu.SMEM((n_groups,), jnp.int32),
        ],
        hubs * tile_flops,
        moved,
    )(ints, dest, hub_cols, grad, tiles[0], hub_tiles, *back_parts)
    arrived.append(swap(part_other))

    share = tree_sum([t.astype(F32) for t in shares]) * (1.0 / math.sqrt(rows_dev * n_blocks * n_groups))
    other = swap(share)
    grad_weight = jnp.concatenate(
        [jnp.where(core == 0, share, other), jnp.where(core == 0, other, share)], axis=0
    ).reshape(width, width)

    grad_feats = call(
        functools.partial(last_backward, len(arrived)),
        "last_backward",
        jax.ShapeDtypeStruct((rows_dev, width), BF16),
        [VMEM] * (2 + len(arrived)),
        VMEM,
        [],
        moved,
        moved,
    )(own_sum, *arrived, weight)
    return (layer_out.reshape(rows_dev, width), grad_feats, grad_weight)


def solution(mesh):
    in_specs = (
        P(("grp", "blk"), None),
        P(),
        P(("grp", "blk"), None),
        P(("grp", "blk")),
        P("grp", "blk", None, None, None, None),
        P("grp", "blk", None, None),
        P("grp", "blk", None, None),
        P("grp", "blk", None),
        P("grp", "blk", None, None, None),
        P("grp", "blk", None),
        P(None, "blk", None, None),
        P(None, "blk", None),
    )
    out_specs = (P(("grp", "blk"), None), P(("grp", "blk"), None), P())
    return jax.shard_map(local, mesh=mesh, in_specs=in_specs, out_specs=out_specs, check_vma=False)
```

time: 169 us -> 121 us (0.72)
  waiting for transfers between devices: 60.2 us -> 36.8 us
  local copies, waits for them, and re-layouts: 23.6 us -> 5.86 us
  other arithmetic: 9.71 us -> 3.6 us
  Pallas kernels: 35.4 us -> 32.6 us
  starting transfers between devices: 38.1 us -> 40.8 us
    ppermute x11 -> x9, waiting for transfers between devices: 58.3 us -> 33.3 us  [across(): return lax.ppermute(value, 'blk', pairs)]
    unnamed x86 -> x52, local copies, waits for them, and re-layouts: 21.9 us -> 5.47 us
    convert_element_type x5 -> x6, other arithmetic: 5.5 us -> 1.37 us  [the longest x1 0.92 us: local(): both = (part_own + theirs.astype(F32)).astype(BF16)]
    pallas_call x11 -> x13, Pallas kernels: 34.1 us -> 31.3 us  [the longest x4 7.53 us: forward(): call(functools.partial(forward_blocks, meta, mask, sides, acc is not None...]
    ppermute x11 -> x9, starting transfers between devices: 23.1 us -> 25 us  [across(): return lax.ppermute(value, 'blk', pairs)]
    ppermute x10, waiting for transfers between devices: 1.74 us -> 3.51 us  [swap(): return lax.ppermute(value, 'blk', [(i, i ^ 1) for i in range(n_blocks)])]
    ppermute x9 -> x8, starting transfers between devices: 12.4 us -> 13 us  [group(): return lax.ppermute(value, 'grp', [(i, i ^ mask) for i in range(n_groups)])]
  transfers between devices with their start and end apart: 30 -> 27, of which waited for: 8 -> 9; matrix products, arithmetic and copies ran while one was open for 6% -> 2% of each run, Pallas kernels for 17% -> 20%
where the time goes in v2:
time: 121 us
  starting transfers between devices  40.8 us (34%)
  waiting for transfers between devices  36.8 us (30%)
  Pallas kernels  32.6 us (27%)
  local copies, waits for them, and re-layouts  5.86 us (5%)
  other arithmetic  3.6 us (3%)
    ppermute x9, waiting for transfers between devices, across(): return lax.ppermute(value, 'blk', pairs)  33.3 us
    ppermute x9, starting transfers between devices, across(): return lax.ppermute(value, 'blk', pairs)  25 us
    ppermute x8, starting transfers between devices, group(): return lax.ppermute(value, 'grp', [(i, i ^ mask) for i in range(n_groups)])  13 us
    pallas_call x4, Pallas kernels, forward(): call(functools.partial(forward_blocks, meta, mask, sides, acc is not None...  7.53 us
    pallas_call x4, Pallas kernels, backward(): call(functools.partial(backward_blocks, meta, mask, sides), 'backward_blo...  6.44 us
    pallas_call x1, Pallas kernels, local(): call(functools.partial(stage_tiles, meta), 'stage_tiles', (jax.ShapeDtype...  6.05 us
    unnamed x52, local copies, waits for them, and re-layouts  5.47 us
    pallas_call x1, Pallas kernels, local(): call(functools.partial(last_forward, meta, last), 'last_forward', (jax.Sh...  4.26 us
  transfers between devices with their start and end apart: 27, of which 9 were waited for; matrix products, arithmetic and copies ran while one was open for 2% of the time, Pallas kernels for 20%

profile of v2, /device:TPU:0, one launch (start us, length us, event | category | flops | bytes accessed | tf_op | source)
XLA Modules:
  0.0 120.8 jit_solution(9259358053845495001)
XLA Ops:
  0.6 0.5 collective-permute-start
  1.1 2.7 %collective-permute-start.4 = (bf16[8,128,256]{2,1,0:T(8,128)(2,1)}, bf16[8,128,256]{2,1,0:T(8,128)(2,1)S(1)}, u32[]{:S(2)}, u32[]{:S(2)}) collective-permute-start(bf16[8,128,256]{2,1,0:T(8,128)(2,1)} %bitcast.47), channel_id=1, source_target_pairs={{0,2},{1,3},{2,0},{3,1},{4,6},{5,7},{6,4},{7,5},{8,10},{9,11},{10,... | collective-permute-start | bytes 1572872 | tf_op jit(solution)/shard_map/ppermute | solution.py:276
  3.8 2.6 %collective-permute-start.6 = (bf16[8,128,256]{2,1,0:T(8,128)(2,1)}, bf16[8,128,256]{2,1,0:T(8,128)(2,1)S(1)}, u32[]{:S(2)}, u32[]{:S(2)}) collective-permute-start(bf16[8,128,256]{2,1,0:T(8,128)(2,1)} %bitcast.48), channel_id=1, source_target_pairs={{0,4},{1,5},{2,6},{3,7},{4,0},{5,1},{6,2},{7,3},{8,12},{9,13},{10,... | collective-permute-start | bytes 1572872 | tf_op jit(solution)/shard_map/ppermute | solution.py:276
  6.4 0.1 pad_add_fusion.pos
  6.5 6.1 %stage_tiles.1 = (bf16[2,32,128,128]{3,2,1,0:T(8,128)(2,1)S(1)}, bf16[2,32,128,128]{3,2,1,0:T(8,128)(2,1)S(1)}, bf16[2,32,128,128]{3,2,1,0:T(8,128)(2,1)}, bf16[2,32,128,128]{3,2,1,0:T(8,128)(2,1)}) custom-call(s32[3]{0:T(128)S(1)} %pad_add_fusion.pos, bf16[8,32,128,128]{3,2,1,0:T(8,128)(2,1)} %bitcast.56), custom_call_target="tpu_custom_call" | custom-call | flops 1 | bytes 419430400 | tf_op jit(solution)/shard_map/stage_tiles/pallas_call | solution.py:284
  12.6 1.4 %copy-done.5 = bf16[2,32,128,128]{3,2,1,0:T(8,128)(2,1)} copy-done((bf16[2,32,128,128]{3,2,1,0:T(8,128)(2,1)}, bf16[2,32,128,128]{3,2,1,0:T(8,128)(2,1)S(1)}, u32[]{:S(2)}) %copy-start.5) | copy-done | bytes 2097176
  14.0 1.4 %copy-done.8 = bf16[2,32,128,128]{3,2,1,0:T(8,128)(2,1)} copy-done((bf16[2,32,128,128]{3,2,1,0:T(8,128)(2,1)}, bf16[2,32,128,128]{3,2,1,0:T(8,128)(2,1)S(1)}, u32[]{:S(2)}) %copy-start.8) | copy-done | bytes 2097176
  15.3 0.1 reshape.58
  15.4 0.1 reshape.59
  15.5 0.1 concatenate.13.ints
  15.6 0.2 broadcast_select_fusion
  15.9 1.0 hub_products.1
  16.9 0.1 slice_bitcast_fusion
  17.0 1.6 %collective-permute-start.1 = (bf16[4,128,256]{2,1,0:T(8,128)(2,1)S(1)}, bf16[4,128,256]{2,1,0:T(8,128)(2,1)S(1)}, u32[]{:S(2)}, u32[]{:S(2)}) collective-permute-start(bf16[4,128,256]{2,1,0:T(8,128)(2,1)S(1)} %get-tuple-element.53), channel_id=1, source_target_pairs={{0,8},{8,0},{16,24},{24,16},{1,9},{9,1},{17,25},{25,17},{2,10},{10... | collective-permute-start | bytes 786440 | tf_op jit(solution)/shard_map/ppermute | solution.py:279
  18.5 1.5 %collective-permute-start.2 = (bf16[4,128,256]{2,1,0:T(8,128)(2,1)S(1)}, bf16[4,128,256]{2,1,0:T(8,128)(2,1)S(1)}, u32[]{:S(2)}, u32[]{:S(2)}) collective-permute-start(bf16[4,128,256]{2,1,0:T(8,128)(2,1)S(1)} %get-tuple-element.52), channel_id=1, source_target_pairs={{0,16},{8,24},{16,0},{24,8},{1,17},{9,25},{17,1},{25,9},{2,18},{10... | collective-permute-start | bytes 786440 | tf_op jit(solution)/shard_map/ppermute | solution.py:279
  20.1 0.5 collective-permute-start.3
  20.5 7.1 %collective-permute-done.4.refs_2_ = bf16[8,128,256]{2,1,0:T(8,128)(2,1)S(1)} collective-permute-done((bf16[8,128,256]{2,1,0:T(8,128)(2,1)}, bf16[8,128,256]{2,1,0:T(8,128)(2,1)S(1)}, u32[]{:S(2)}, u32[]{:S(2)}) %collective-permute-start.4) | collective-permute-done | bytes 524320 | tf_op jit(solution)/shard_map/ppermute | solution.py:276
  27.6 2.6 %forward_blocks.4.refs_0_ = f32[8,128,256]{2,1,0:T(8,128)S(1)} custom-call(s32[523]{0:T(1024)S(1)} %concatenate.13.ints, bf16[8,128,256]{2,1,0:T(8,128)(2,1)S(1)} %collective-permute-done.refs_0_, bf16[8,128,256]{2,1,0:T(8,128)(2,1)S(1)} %bitcast.50, bf16[2,32,128,128]{3,2,1,0:T(8,128)(2,1)S(1)} %copy-done.6), custom_call_target="tpu_custom_call" | custom-call | flops 53687091200 | bytes 419430400 | tf_op jit(solution)/shard_map/forward_blocks/pallas_call | solution.py:297
  30.2 1.4 %collective-permute-start.8 = (bf16[8,128,256]{2,1,0:T(8,128)(2,1)S(1)}, bf16[8,128,256]{2,1,0:T(8,128)(2,1)S(1)}, u32[]{:S(2)}, u32[]{:S(2)}) collective-permute-start(bf16[8,128,256]{2,1,0:T(8,128)(2,1)S(1)} %collective-permute-done.6.refs_2_), channel_id=1, source_target_pairs={{2,0},{3,1},{4,6},{5,7},{10,8},{11,9},{12,14},{13,15},{18,16},{19,... | collective-permute-start | bytes 1572872 | tf_op jit(solution)/shard_map/ppermute | solution.py:276
  31.7 0.7 collective-permute-start.9
  32.4 0.1 collective-permute-start.7
  32.5 1.9 %hub_add.1.refs_0_ = f32[8,128,256]{2,1,0:T(8,128)S(1)} custom-call(s32[3]{0:T(128)S(1)} %pad_add_fusion.pos, s32[4,16]{1,0:T(4,128)S(1)} %bitcast.43, s32[4,16]{1,0:T(4,128)S(1)} %bitcast.40, f32[8,128,256]{2,1,0:T(8,128)S(1)} %forward_blocks.4.refs_0_, bf16[4,128,256]{2,1,0:T(8,128)(2,1)S(1)} %get-tuple-element.54.refs_1_, ...), custom_call_target="tpu_custom_call" | custom-call | flops 1048576 | bytes 419430400 | tf_op jit(solution)/shard_map/hub_add/pallas_call | solution.py:350
  34.5 2.1 %forward_blocks.5.refs_0_ = f32[8,128,256]{2,1,0:T(8,128)S(1)} custom-call(s32[523]{0:T(1024)S(1)} %concatenate.13.ints, f32[8,128,256]{2,1,0:T(8,128)S(1)} %hub_add.1.refs_0_, bf16[8,128,256]{2,1,0:T(8,128)(2,1)S(1)} %collective-permute-done.5.refs_1_, bf16[8,128,256]{2,1,0:T(8,128)(2,1)S(1)} %collective-permute-done.4.refs_2_, ...), custom_call_target="tpu_custom_call" | custom-call | flops 53687091200 | bytes 419430400 | tf_op jit(solution)/shard_map/forward_blocks/pallas_call | solution.py:297
  36.6 1.7 %forward_blocks.6.refs_0_ = f32[8,128,256]{2,1,0:T(8,128)S(1)} custom-call(s32[523]{0:T(1024)S(1)} %concatenate.13.ints, f32[8,128,256]{2,1,0:T(8,128)S(1)} %forward_blocks.5.refs_0_, bf16[8,128,256]{2,1,0:T(8,128)(2,1)S(1)} %collective-permute-done.7.refs_1_, bf16[8,128,256]{2,1,0:T(8,128)(2,1)S(1)} %collective-permute-done.6.refs_2_, ...), custom_call_target="tpu_custom_call" | custom-call | flops 53687091200 | bytes 419430400 | tf_op jit(solution)/shard_map/forward_blocks/pallas_call | solution.py:297
  38.3 7.8 %collective-permute-done.8 = bf16[8,128,256]{2,1,0:T(8,128)(2,1)S(1)} collective-permute-done((bf16[8,128,256]{2,1,0:T(8,128)(2,1)S(1)}, bf16[8,128,256]{2,1,0:T(8,128)(2,1)S(1)}, u32[]{:S(2)}, u32[]{:S(2)}) %collective-permute-start.8) | collective-permute-done | bytes 524320 | tf_op jit(solution)/shard_map/ppermute | solution.py:276
  46.1 0.1 add.47.refs_1_
  46.4 1.2 forward_blocks.7.acc
  47.6 0.7 collective-permute-done.10.refs_0_
  48.3 4.3 %last_forward.1 = (bf16[8,128,256]{2,1,0:T(8,128)(2,1)}, bf16[8,128,256]{2,1,0:T(8,128)(2,1)S(1)}, bf16[4,4,128,256]{3,2,1,0:T(8,128)(2,1)S(1)}, f32[256,256]{1,0:T(8,128)S(1)}) custom-call(s32[523]{0:T(1024)S(1)} %concatenate.13.ints, s32[4,16]{1,0:T(4,128)S(1)} %bitcast.44, s32[4,16]{1,0:T(4,128)S(1)} %bitcast.41, f32[8,128,256]{2,1,0:T(8,128)S(1)} %forward_blocks.7.acc, ...), custom_call_target="tpu_custom_call" | custom-call | flops 26843545600 | bytes 419430400 | tf_op jit(solution)/shard_map/last_forward/pallas_call | solution.py:369
  52.5 1.2 backward_blocks.5
  53.7 0.3 collective-permute-start.11
  54.0 1.2 backward_blocks.4
  55.2 0.5 collective-permute-done.11
  55.7 0.9 add_convert_fusion.2
  56.6 1.8 %backward_blocks.6 = (bf16[8,128,256]{2,1,0:T(8,128)(2,1)S(1)}, f32[8,128,256]{2,1,0:T(8,128)S(1)}) custom-call(s32[523]{0:T(1024)S(1)} %concatenate.13.ints, bf16[8,128,256]{2,1,0:T(8,128)(2,1)S(1)} %get-tuple-element.35.grad, bf16[2,32,128,128]{3,2,1,0:T(8,128)(2,1)S(1)} %copy-done.11), custom_call_target="tpu_custom_call" | custom-call | flops 53687091200 | bytes 419430400 | tf_op jit(solution)/shard_map/backward_blocks/pallas_call | solution.py:312
  58.5 1.3 %collective-permute-start.15 = (bf16[1,128,256]{2,1,0:T(8,128)(2,1)S(1)}, bf16[1,128,256]{2,1,0:T(8,128)(2,1)S(1)}, u32[]{:S(2)}, u32[]{:S(2)}) collective-permute-start(bf16[1,128,256]{2,1,0:T(8,128)(2,1)S(1)} %dynamic-slice_bitcast_fusion), channel_id=1, source_target_pairs={{0,1},{1,0},{2,3},{3,2},{4,5},{5,4},{6,7},{7,6},{8,9},{9,8},{10,11... | collective-permute-start | bytes 196616 | tf_op jit(solution)/shard_map/ppermute | solution.py:271
  59.8 0.9 collective-permute-done.15
  60.7 2.2 %collective-permute-start.16 = (bf16[1,128,256]{2,1,0:T(8,128)(2,1)S(1)}, bf16[1,128,256]{2,1,0:T(8,128)(2,1)S(1)}, u32[]{:S(2)}, u32[]{:S(2)}) collective-permute-start(bf16[1,128,256]{2,1,0:T(8,128)(2,1)S(1)} %fusion), channel_id=1, source_target_pairs={{0,8},{8,0},{16,24},{24,16},{1,9},{9,1},{17,25},{25,17},{2,10},{10... | collective-permute-start | bytes 196616 | tf_op jit(solution)/shard_map/ppermute | solution.py:279
  62.9 4.7 %collective-permute-start.13 = (bf16[8,128,256]{2,1,0:T(8,128)(2,1)}, bf16[8,128,256]{2,1,0:T(8,128)(2,1)S(1)}, u32[]{:S(2)}, u32[]{:S(2)}) collective-permute-start(bf16[8,128,256]{2,1,0:T(8,128)(2,1)} %add_convert_fusion.2), channel_id=1, source_target_pairs={{0,2},{1,3},{6,4},{7,5},{8,10},{9,11},{14,12},{15,13},{16,18},{17,... | collective-permute-start | bytes 1572872 | tf_op jit(solution)/shard_map/ppermute | solution.py:276
  67.7 0.7 collective-permute-start.14
  68.5 2.5 %collective-permute-start.17 = (bf16[1,128,256]{2,1,0:T(8,128)(2,1)S(1)}, bf16[1,128,256]{2,1,0:T(8,128)(2,1)S(1)}, u32[]{:S(2)}, u32[]{:S(2)}) collective-permute-start(bf16[1,128,256]{2,1,0:T(8,128)(2,1)S(1)} %add_convert_fusion.4), channel_id=1, source_target_pairs={{0,16},{8,24},{16,0},{24,8},{1,17},{9,25},{17,1},{25,9},{2,18},{10... | collective-permute-start | bytes 196616 | tf_op jit(solution)/shard_map/ppermute | solution.py:279
  71.0 1.6 %copy-done.10 = bf16[2,32,128,128]{3,2,1,0:T(8,128)(2,1)S(1)} copy-done((bf16[2,32,128,128]{3,2,1,0:T(8,128)(2,1)S(1)}, bf16[2,32,128,128]{3,2,1,0:T(8,128)(2,1)}, u32[]{:S(2)}) %copy-start.10) | copy-done | bytes 2097176
  72.6 1.0 copy-done.19
  73.6 2.3 %backward_blocks.7 = (bf16[8,128,256]{2,1,0:T(8,128)(2,1)S(1)}, f32[8,128,256]{2,1,0:T(8,128)S(1)}) custom-call(s32[523]{0:T(1024)S(1)} %concatenate.13.ints, bf16[8,128,256]{2,1,0:T(8,128)(2,1)S(1)} %copy-done.19, bf16[2,32,128,128]{3,2,1,0:T(8,128)(2,1)S(1)} %copy-done.10), custom_call_target="tpu_custom_call" | custom-call | flops 53687091200 | bytes 419430400 | tf_op jit(solution)/shard_map/backward_blocks/pallas_call | solution.py:312
  75.9 0.3 collective-permute-start.22
  76.2 2.3 %collective-permute-start.25 = (bf16[1,128,256]{2,1,0:T(8,128)(2,1)S(1)}, bf16[1,128,256]{2,1,0:T(8,128)(2,1)S(1)}, u32[]{:S(2)}, u32[]{:S(2)}) collective-permute-start(bf16[1,128,256]{2,1,0:T(8,128)(2,1)S(1)} %add_convert_fusion.3), channel_id=1, source_target_pairs={{0,6},{1,7},{2,4},{3,5},{4,2},{5,3},{6,0},{7,1},{8,14},{9,15},{10,... | collective-permute-start | bytes 196616 | tf_op jit(solution)/shard_map/ppermute | solution.py:276
  78.5 0.7 collective-permute-done.13
  79.2 0.2 add_convert_fusion.1
  79.4 0.1 slice_bitcast_fusion.4
  79.5 0.9 collective-permute-start.18
  80.3 2.8 %collective-permute-start.19 = (bf16[4,128,256]{2,1,0:T(8,128)(2,1)S(1)}, bf16[4,128,256]{2,1,0:T(8,128)(2,1)S(1)}, u32[]{:S(2)}, u32[]{:S(2)}) collective-permute-start(bf16[4,128,256]{2,1,0:T(8,128)(2,1)S(1)} %get-tuple-element.48), channel_id=1, source_target_pairs={{0,16},{8,24},{16,0},{24,8},{1,17},{9,25},{17,1},{25,9},{2,18},{10... | collective-permute-start | bytes 786440 | tf_op jit(solution)/shard_map/ppermute | solution.py:279
  83.2 1.0 collective-permute-start.20
  84.2 0.2 add_convert_fusion
  84.4 0.1 pad_maximum_fusion
  84.5 6.6 %collective-permute-start.21 = (bf16[9,128,256]{2,1,0:T(8,128)(2,1)S(1)}, bf16[9,128,256]{2,1,0:T(8,128)(2,1)S(1)}, u32[]{:S(2)}, u32[]{:S(2)}) collective-permute-start(bf16[9,128,256]{2,1,0:T(8,128)(2,1)S(1)} %get-tuple-element.58), channel_id=1, source_target_pairs={{0,4},{1,5},{2,6},{3,7},{4,0},{5,1},{6,2},{7,3},{8,12},{9,13},{10,... | collective-permute-start | bytes 1769480 | tf_op jit(solution)/shard_map/ppermute | solution.py:276
  91.1 3.3 %collective-permute-start.23 = (bf16[9,128,256]{2,1,0:T(8,128)(2,1)S(1)}, bf16[9,128,256]{2,1,0:T(8,128)(2,1)S(1)}, u32[]{:S(2)}, u32[]{:S(2)}) collective-permute-start(bf16[9,128,256]{2,1,0:T(8,128)(2,1)S(1)} %get-tuple-element.57), channel_id=1, source_target_pairs={{0,2},{1,3},{2,0},{3,1},{4,6},{5,7},{6,4},{7,5},{8,10},{9,11},{10,... | collective-permute-start | bytes 1769480 | tf_op jit(solution)/shard_map/ppermute | solution.py:276
  94.5 4.1 %last_products.1 = (bf16[8,128,256]{2,1,0:T(8,128)(2,1)}, f32[8,128,256]{2,1,0:T(8,128)S(1)}) custom-call(s32[523]{0:T(1024)S(1)} %concatenate.13.ints, s32[4,16]{1,0:T(4,128)S(1)} %bitcast.45, s32[16]{0:T(128)S(1)} %bitcast.55, bf16[8,128,256]{2,1,0:T(8,128)(2,1)S(1)} %copy-done.20, bf16[2,32,128,128]{3,2,1,0:T(8,128)(2,1)S(1)} %copy-done.7, ...), custom_call_target="tpu_custom_call" | custom-call | flops 13421772800 | bytes 419430400 | tf_op jit(solution)/shard_map/last_products/pallas_call | solution.py:428
  98.6 16.7 %collective-permute-done.21.refs_2_ = bf16[9,128,256]{2,1,0:T(8,128)(2,1)S(1)} collective-permute-done((bf16[9,128,256]{2,1,0:T(8,128)(2,1)S(1)}, bf16[9,128,256]{2,1,0:T(8,128)(2,1)S(1)}, u32[]{:S(2)}, u32[]{:S(2)}) %collective-permute-start.21) | collective-permute-done | bytes 589856 | tf_op jit(solution)/shard_map/ppermute | solution.py:276
  115.4 1.0 collective-permute-done.23.refs_3_
  116.4 0.1 collective-permute-start.26
  116.5 1.5 %collective-permute-done.26 = f32[1,128,256]{2,1,0:T(8,128)} collective-permute-done((f32[1,128,256]{2,1,0:T(8,128)S(1)}, f32[1,128,256]{2,1,0:T(8,128)}, u32[]{:S(2)}, u32[]{:S(2)}) %collective-permute-start.26) | collective-permute-done | bytes 131104 | tf_op jit(solution)/shard_map/ppermute | solution.py:271
  117.9 0.9 broadcast_select_fusion.2
  118.9 0.7 pad_maximum_fusion.2
  119.6 1.2 %last_backward.1 = bf16[1024,256]{1,0:T(8,128)(2,1)} custom-call(f32[8,128,256]{2,1,0:T(8,128)S(1)} %get-tuple-element.44.refs_0_, bf16[8,128,256]{2,1,0:T(8,128)(2,1)S(1)} %collective-permute-done.14.refs_1_, bf16[9,128,256]{2,1,0:T(8,128)(2,1)S(1)} %collective-permute-done.21.refs_2_, bf16[9,128,256]{2,1,0:T(8,128)(2,1)S(1)} %collective-permute-done.23.refs_3_, ...), custom_call_target="tpu_custom_call" | custom-call | flops 419430400 | bytes 419430400 | tf_op jit(solution)/shard_map/last_backward/pallas_call | solution.py:450
  (77 shorter events, 0.4 us)
Async XLA Ops:
  0.6 15.2 %collective-permute-start = (bf16[8,128,256]{2,1,0:T(8,128)(2,1)}, bf16[8,128,256]{2,1,0:T(8,128)(2,1)S(1)}, u32[]{:S(2)}, u32[]{:S(2)}) collective-permute-start(bf16[8,128,256]{2,1,0:T(8,128)(2,1)} %bitcast.46), channel_id=1, source_target_pairs={{0,1},{1,0},{2,3},{3,2},{4,5},{5,4},{6,7},{7,6},{8,9},{9,8},{10,11... | collective-permute-start | bytes 1572872 | tf_op jit(solution)/shard_map/ppermute | solution.py:271
  1.1 26.5 %collective-permute-start.4 = (bf16[8,128,256]{2,1,0:T(8,128)(2,1)}, bf16[8,128,256]{2,1,0:T(8,128)(2,1)S(1)}, u32[]{:S(2)}, u32[]{:S(2)}) collective-permute-start(bf16[8,128,256]{2,1,0:T(8,128)(2,1)} %bitcast.47), channel_id=1, source_target_pairs={{0,2},{1,3},{2,0},{3,1},{4,6},{5,7},{6,4},{7,5},{8,10},{9,11},{10,... | collective-permute-start | bytes 1572872 | tf_op jit(solution)/shard_map/ppermute | solution.py:276
  3.8 26.4 %collective-permute-start.6 = (bf16[8,128,256]{2,1,0:T(8,128)(2,1)}, bf16[8,128,256]{2,1,0:T(8,128)(2,1)S(1)}, u32[]{:S(2)}, u32[]{:S(2)}) collective-permute-start(bf16[8,128,256]{2,1,0:T(8,128)(2,1)} %bitcast.48), channel_id=1, source_target_pairs={{0,4},{1,5},{2,6},{3,7},{4,0},{5,1},{6,2},{7,3},{8,12},{9,13},{10,... | collective-permute-start | bytes 1572872 | tf_op jit(solution)/shard_map/ppermute | solution.py:276
  6.5 8.9 %copy-start.22 = (s32[1,1,8,32]{3,2,1,0:T(8,128)S(1)}, s32[1,1,8,32]{3,2,1,0:T(8,128)}, u32[]{:S(2)}) copy-start(s32[1,1,8,32]{3,2,1,0:T(8,128)} %param.17) | copy-start | bytes 3076
  6.5 9.0 %copy-start.23 = (s32[1,1,8,32]{3,2,1,0:T(8,128)S(1)}, s32[1,1,8,32]{3,2,1,0:T(8,128)}, u32[]{:S(2)}) copy-start(s32[1,1,8,32]{3,2,1,0:T(8,128)} %param.18) | copy-start | bytes 3076
  6.5 9.0 %copy-start.25 = (s32[1,1,8]{2,1,0:T(1,128)S(1)}, s32[1,1,8]{2,1,0:T(1,128)}, u32[]{:S(2)}) copy-start(s32[1,1,8]{2,1,0:T(1,128)} %param.19) | copy-start | bytes 100
  6.5 9.1 %copy-start.24 = (s32[1024]{0:T(1024)S(1)}, s32[1024]{0:T(1024)}, u32[]{:S(2)}) copy-start(s32[1024]{0:T(1024)} %param.15) | copy-start | bytes 12292
  6.5 9.1 %copy-start.21 = (bf16[1024,256]{1,0:T(8,128)(2,1)S(1)}, bf16[1024,256]{1,0:T(8,128)(2,1)}, u32[]{:S(2)}) copy-start(bf16[1024,256]{1,0:T(8,128)(2,1)} %param.14) | copy-start | bytes 1572868
  6.5 9.3 %copy-start.3 = (s32[4,1,16,1]{2,3,1,0:T(1,128)S(1)}, s32[4,1,16,1]{2,3,1,0:T(1,128)}, u32[]{:S(2)}) copy-start(s32[4,1,16,1]{2,3,1,0:T(1,128)} %param.22) | copy-start | bytes 772
  6.5 9.3 %copy-start.13 = (bf16[1024,256]{1,0:T(8,128)(2,1)S(1)}, bf16[1024,256]{1,0:T(8,128)(2,1)}, u32[]{:S(2)}) copy-start(bf16[1024,256]{1,0:T(8,128)(2,1)} %param.12) | copy-start | bytes 1572868
  6.5 9.3 %copy-start.14 = (bf16[1,1,16,128,128]{4,3,2,1,0:T(8,128)(2,1)S(1)}, bf16[1,1,16,128,128]{4,3,2,1,0:T(8,128)(2,1)}, u32[]{:S(2)}) copy-start(bf16[1,1,16,128,128]{4,3,2,1,0:T(8,128)(2,1)} %param.20) | copy-start | bytes 1572868
  6.5 9.3 %copy-start.16 = (s32[1,1,16]{2,1,0:T(1,128)S(1)}, s32[1,1,16]{2,1,0:T(1,128)}, u32[]{:S(2)}) copy-start(s32[1,1,16]{2,1,0:T(1,128)} %param.21) | copy-start | bytes 196
  12.6 1.4 %copy-start.5 = (bf16[2,32,128,128]{3,2,1,0:T(8,128)(2,1)}, bf16[2,32,128,128]{3,2,1,0:T(8,128)(2,1)S(1)}, u32[]{:S(2)}) copy-start(bf16[2,32,128,128]{3,2,1,0:T(8,128)(2,1)S(1)} %get-tuple-element.25.refs_2_.tiles) | copy-start | bytes 6291460
  14.0 1.4 %copy-start.8 = (bf16[2,32,128,128]{3,2,1,0:T(8,128)(2,1)}, bf16[2,32,128,128]{3,2,1,0:T(8,128)(2,1)S(1)}, u32[]{:S(2)}) copy-start(bf16[2,32,128,128]{3,2,1,0:T(8,128)(2,1)S(1)} %get-tuple-element.27.refs_3_.tiles) | copy-start | bytes 6291460
  16.9 10.7 %copy-start.6 = (bf16[2,32,128,128]{3,2,1,0:T(8,128)(2,1)S(1)}, bf16[2,32,128,128]{3,2,1,0:T(8,128)(2,1)}, u32[]{:S(2)}) copy-start(bf16[2,32,128,128]{3,2,1,0:T(8,128)(2,1)} %copy-done.5) | copy-start | bytes 6291460
  17.0 14.7 %collective-permute-start.1 = (bf16[4,128,256]{2,1,0:T(8,128)(2,1)S(1)}, bf16[4,128,256]{2,1,0:T(8,128)(2,1)S(1)}, u32[]{:S(2)}, u32[]{:S(2)}) collective-permute-start(bf16[4,128,256]{2,1,0:T(8,128)(2,1)S(1)} %get-tuple-element.53), channel_id=1, source_target_pairs={{0,8},{8,0},{16,24},{24,16},{1,9},{9,1},{17,25},{25,17},{2,10},{10... | collective-permute-start | bytes 786440 | tf_op jit(solution)/shard_map/ppermute | solution.py:279
  18.5 13.8 %collective-permute-start.2 = (bf16[4,128,256]{2,1,0:T(8,128)(2,1)S(1)}, bf16[4,128,256]{2,1,0:T(8,128)(2,1)S(1)}, u32[]{:S(2)}, u32[]{:S(2)}) collective-permute-start(bf16[4,128,256]{2,1,0:T(8,128)(2,1)S(1)} %get-tuple-element.52), channel_id=1, source_target_pairs={{0,16},{8,24},{16,0},{24,8},{1,17},{9,25},{17,1},{25,9},{2,18},{10... | collective-permute-start | bytes 786440 | tf_op jit(solution)/shard_map/ppermute | solution.py:279
  20.1 12.5 %collective-permute-start.3 = (bf16[4,128,256]{2,1,0:T(8,128)(2,1)S(1)}, bf16[4,128,256]{2,1,0:T(8,128)(2,1)S(1)}, u32[]{:S(2)}, u32[]{:S(2)}) collective-permute-start(bf16[4,128,256]{2,1,0:T(8,128)(2,1)S(1)} %get-tuple-element.51), channel_id=1, source_target_pairs={{0,24},{8,16},{16,8},{24,0},{1,25},{9,17},{17,9},{25,1},{2,26},{10... | collective-permute-start | bytes 786440 | tf_op jit(solution)/shard_map/ppermute | solution.py:279
  27.6 6.8 %collective-permute-start.5 = (bf16[8,128,256]{2,1,0:T(8,128)(2,1)S(1)}, bf16[8,128,256]{2,1,0:T(8,128)(2,1)S(1)}, u32[]{:S(2)}, u32[]{:S(2)}) collective-permute-start(bf16[8,128,256]{2,1,0:T(8,128)(2,1)S(1)} %collective-permute-done.4.refs_2_), channel_id=1, source_target_pairs={{0,1},{1,0},{2,3},{3,2},{4,5},{5,4},{6,7},{7,6},{8,9},{9,8},{10,11... | collective-permute-start | bytes 1572872 | tf_op jit(solution)/shard_map/ppermute | solution.py:271
  27.6 4.9 %copy-start.2 = (s32[4,1,16]{2,1,0:T(1,128)S(1)}, s32[4,1,16]{2,1,0:T(1,128)}, u32[]{:S(2)}) copy-start(s32[4,1,16]{2,1,0:T(1,128)} %param.23) | copy-start | bytes 772
  30.2 4.3 %copy-start.9 = (bf16[2,32,128,128]{3,2,1,0:T(8,128)(2,1)S(1)}, bf16[2,32,128,128]{3,2,1,0:T(8,128)(2,1)}, u32[]{:S(2)}) copy-start(bf16[2,32,128,128]{3,2,1,0:T(8,128)(2,1)} %copy-done.8) | copy-start | bytes 6291460
  30.2 15.9 %collective-permute-start.8 = (bf16[8,128,256]{2,1,0:T(8,128)(2,1)S(1)}, bf16[8,128,256]{2,1,0:T(8,128)(2,1)S(1)}, u32[]{:S(2)}, u32[]{:S(2)}) collective-permute-start(bf16[8,128,256]{2,1,0:T(8,128)(2,1)S(1)} %collective-permute-done.6.refs_2_), channel_id=1, source_target_pairs={{2,0},{3,1},{4,6},{5,7},{10,8},{11,9},{12,14},{13,15},{18,16},{19,... | collective-permute-start | bytes 1572872 | tf_op jit(solution)/shard_map/ppermute | solution.py:276
  31.7 14.5 %collective-permute-start.9 = (bf16[8,128,256]{2,1,0:T(8,128)(2,1)S(1)}, bf16[8,128,256]{2,1,0:T(8,128)(2,1)S(1)}, u32[]{:S(2)}, u32[]{:S(2)}) collective-permute-start(bf16[8,128,256]{2,1,0:T(8,128)(2,1)S(1)} %bitcast.51), channel_id=1, source_target_pairs={{2,4},{3,5},{4,2},{5,3},{10,12},{11,13},{12,10},{13,11},{18,20},{1... | collective-permute-start | bytes 1572872 | tf_op jit(solution)/shard_map/ppermute | solution.py:276
  32.4 4.2 %collective-permute-start.7 = (bf16[8,128,256]{2,1,0:T(8,128)(2,1)S(1)}, bf16[8,128,256]{2,1,0:T(8,128)(2,1)S(1)}, u32[]{:S(2)}, u32[]{:S(2)}) collective-permute-start(bf16[8,128,256]{2,1,0:T(8,128)(2,1)S(1)} %collective-permute-done.6.refs_2_), channel_id=1, source_target_pairs={{0,1},{1,0},{2,3},{3,2},{4,5},{5,4},{6,7},{7,6},{8,9},{9,8},{10,11... | collective-permute-start | bytes 1572872 | tf_op jit(solution)/shard_map/ppermute | solution.py:271
  34.5 2.1 %copy-start.11 = (bf16[2,32,128,128]{3,2,1,0:T(8,128)(2,1)S(1)}, bf16[2,32,128,128]{3,2,1,0:T(8,128)(2,1)}, u32[]{:S(2)}) copy-start(bf16[2,32,128,128]{3,2,1,0:T(8,128)(2,1)} %get-tuple-element.28.refs_3_.tiles) | copy-start | bytes 6291460
  36.6 9.7 %copy-start.12 = (bf16[2,32,128,128]{3,2,1,0:T(8,128)(2,1)S(1)}, bf16[2,32,128,128]{3,2,1,0:T(8,128)(2,1)}, u32[]{:S(2)}) copy-start(bf16[2,32,128,128]{3,2,1,0:T(8,128)(2,1)} %get-tuple-element.32.refs_2_.tiles) | copy-start | bytes 6291460
  46.3 2.0 %collective-permute-start.10 = (bf16[8,128,256]{2,1,0:T(8,128)(2,1)S(1)}, bf16[8,128,256]{2,1,0:T(8,128)(2,1)S(1)}, u32[]{:S(2)}, u32[]{:S(2)}) collective-permute-start(bf16[8,128,256]{2,1,0:T(8,128)(2,1)S(1)} %add.47.refs_1_), channel_id=1, source_target_pairs={{0,1},{1,0},{2,3},{3,2},{4,5},{5,4},{6,7},{7,6},{8,9},{9,8},{10,11... | collective-permute-start | bytes 1572872 | tf_op jit(solution)/shard_map/ppermute | solution.py:271
  46.4 1.9 %copy-start = (bf16[256,256]{1,0:T(8,128)(2,1)S(1)}, bf16[256,256]{1,0:T(8,128)(2,1)}, u32[]{:S(2)}) copy-start(bf16[256,256]{1,0:T(8,128)(2,1)} %refs_5_.1) | copy-start | bytes 393220
  52.5 4.1 %copy-start.18 = (bf16[8,128,256]{2,1,0:T(8,128)(2,1)}, bf16[8,128,256]{2,1,0:T(8,128)(2,1)S(1)}, u32[]{:S(2)}) copy-start(bf16[8,128,256]{2,1,0:T(8,128)(2,1)S(1)} %get-tuple-element.35.grad) | copy-start | bytes 1572868
  53.7 2.0 %collective-permute-start.11 = (bf16[8,128,256]{2,1,0:T(8,128)(2,1)S(1)}, bf16[8,128,256]{2,1,0:T(8,128)(2,1)S(1)}, u32[]{:S(2)}, u32[]{:S(2)}) collective-permute-start(bf16[8,128,256]{2,1,0:T(8,128)(2,1)S(1)} %backward_blocks.5), channel_id=1, source_target_pairs={{0,1},{1,0},{2,3},{3,2},{4,5},{5,4},{6,7},{7,6},{8,9},{9,8},{10,11... | collective-permute-start | bytes 1572872 | tf_op jit(solution)/shard_map/ppermute | solution.py:271
  58.5 2.2 %collective-permute-start.15 = (bf16[1,128,256]{2,1,0:T(8,128)(2,1)S(1)}, bf16[1,128,256]{2,1,0:T(8,128)(2,1)S(1)}, u32[]{:S(2)}, u32[]{:S(2)}) collective-permute-start(bf16[1,128,256]{2,1,0:T(8,128)(2,1)S(1)} %dynamic-slice_bitcast_fusion), channel_id=1, source_target_pairs={{0,1},{1,0},{2,3},{3,2},{4,5},{5,4},{6,7},{7,6},{8,9},{9,8},{10,11... | collective-permute-start | bytes 196616 | tf_op jit(solution)/shard_map/ppermute | solution.py:271
  60.7 7.7 %collective-permute-start.16 = (bf16[1,128,256]{2,1,0:T(8,128)(2,1)S(1)}, bf16[1,128,256]{2,1,0:T(8,128)(2,1)S(1)}, u32[]{:S(2)}, u32[]{:S(2)}) collective-permute-start(bf16[1,128,256]{2,1,0:T(8,128)(2,1)S(1)} %fusion), channel_id=1, source_target_pairs={{0,8},{8,0},{16,24},{24,16},{1,9},{9,1},{17,25},{25,17},{2,10},{10... | collective-permute-start | bytes 196616 | tf_op jit(solution)/shard_map/ppermute | solution.py:279
  62.9 16.2 %collective-permute-start.13 = (bf16[8,128,256]{2,1,0:T(8,128)(2,1)}, bf16[8,128,256]{2,1,0:T(8,128)(2,1)S(1)}, u32[]{:S(2)}, u32[]{:S(2)}) collective-permute-start(bf16[8,128,256]{2,1,0:T(8,128)(2,1)} %add_convert_fusion.2), channel_id=1, source_target_pairs={{0,2},{1,3},{6,4},{7,5},{8,10},{9,11},{14,12},{15,13},{16,18},{17,... | collective-permute-start | bytes 1572872 | tf_op jit(solution)/shard_map/ppermute | solution.py:276
  67.7 11.5 %collective-permute-start.14 = (bf16[8,128,256]{2,1,0:T(8,128)(2,1)}, bf16[8,128,256]{2,1,0:T(8,128)(2,1)S(1)}, u32[]{:S(2)}, u32[]{:S(2)}) collective-permute-start(bf16[8,128,256]{2,1,0:T(8,128)(2,1)} %add_convert_fusion.2), channel_id=1, source_target_pairs={{2,4},{3,5},{4,2},{5,3},{10,12},{11,13},{12,10},{13,11},{18,20},{1... | collective-permute-start | bytes 1572872 | tf_op jit(solution)/shard_map/ppermute | solution.py:276
  68.4 10.8 %collective-permute-start.12 = (bf16[8,128,256]{2,1,0:T(8,128)(2,1)S(1)}, bf16[8,128,256]{2,1,0:T(8,128)(2,1)S(1)}, u32[]{:S(2)}, u32[]{:S(2)}) collective-permute-start(bf16[8,128,256]{2,1,0:T(8,128)(2,1)S(1)} %get-tuple-element.38), channel_id=1, source_target_pairs={{0,1},{1,0},{2,3},{3,2},{4,5},{5,4},{6,7},{7,6},{8,9},{9,8},{10,11... | collective-permute-start | bytes 1572872 | tf_op jit(solution)/shard_map/ppermute | solution.py:271
  68.5 7.7 %collective-permute-start.17 = (bf16[1,128,256]{2,1,0:T(8,128)(2,1)S(1)}, bf16[1,128,256]{2,1,0:T(8,128)(2,1)S(1)}, u32[]{:S(2)}, u32[]{:S(2)}) collective-permute-start(bf16[1,128,256]{2,1,0:T(8,128)(2,1)S(1)} %add_convert_fusion.4), channel_id=1, source_target_pairs={{0,16},{8,24},{16,0},{24,8},{1,17},{9,25},{17,1},{25,9},{2,18},{10... | collective-permute-start | bytes 196616 | tf_op jit(solution)/shard_map/ppermute | solution.py:279
  71.0 1.6 %copy-start.10 = (bf16[2,32,128,128]{3,2,1,0:T(8,128)(2,1)S(1)}, bf16[2,32,128,128]{3,2,1,0:T(8,128)(2,1)}, u32[]{:S(2)}) copy-start(bf16[2,32,128,128]{3,2,1,0:T(8,128)(2,1)} %copy-done.8) | copy-start | bytes 6291460
  72.6 1.0 copy-start.19
  75.9 8.3 %collective-permute-start.22 = (bf16[8,128,256]{2,1,0:T(8,128)(2,1)S(1)}, bf16[8,128,256]{2,1,0:T(8,128)(2,1)S(1)}, u32[]{:S(2)}, u32[]{:S(2)}) collective-permute-start(bf16[8,128,256]{2,1,0:T(8,128)(2,1)S(1)} %get-tuple-element.45), channel_id=1, source_target_pairs={{0,1},{1,0},{2,3},{3,2},{4,5},{5,4},{6,7},{7,6},{8,9},{9,8},{10,11... | collective-permute-start | bytes 1572872 | tf_op jit(solution)/shard_map/ppermute | solution.py:271
  76.2 22.4 %collective-permute-start.25 = (bf16[1,128,256]{2,1,0:T(8,128)(2,1)S(1)}, bf16[1,128,256]{2,1,0:T(8,128)(2,1)S(1)}, u32[]{:S(2)}, u32[]{:S(2)}) collective-permute-start(bf16[1,128,256]{2,1,0:T(8,128)(2,1)S(1)} %add_convert_fusion.3), channel_id=1, source_target_pairs={{0,6},{1,7},{2,4},{3,5},{4,2},{5,3},{6,0},{7,1},{8,14},{9,15},{10,... | collective-permute-start | bytes 196616 | tf_op jit(solution)/shard_map/ppermute | solution.py:276
  79.5 11.6 %collective-permute-start.18 = (bf16[4,128,256]{2,1,0:T(8,128)(2,1)S(1)}, bf16[4,128,256]{2,1,0:T(8,128)(2,1)S(1)}, u32[]{:S(2)}, u32[]{:S(2)}) collective-permute-start(bf16[4,128,256]{2,1,0:T(8,128)(2,1)S(1)} %get-tuple-element.49), channel_id=1, source_target_pairs={{0,8},{8,0},{16,24},{24,16},{1,9},{9,1},{17,25},{25,17},{2,10},{10... | collective-permute-start | bytes 786440 | tf_op jit(solution)/shard_map/ppermute | solution.py:279
  80.3 14.1 %collective-permute-start.19 = (bf16[4,128,256]{2,1,0:T(8,128)(2,1)S(1)}, bf16[4,128,256]{2,1,0:T(8,128)(2,1)S(1)}, u32[]{:S(2)}, u32[]{:S(2)}) collective-permute-start(bf16[4,128,256]{2,1,0:T(8,128)(2,1)S(1)} %get-tuple-element.48), channel_id=1, source_target_pairs={{0,16},{8,24},{16,0},{24,8},{1,17},{9,25},{17,1},{25,9},{2,18},{10... | collective-permute-start | bytes 786440 | tf_op jit(solution)/shard_map/ppermute | solution.py:279
  83.2 11.3 %copy-start.4 = (s32[4,1,16,1]{2,3,1,0:T(1,128)S(1)}, s32[4,1,16,1]{2,3,1,0:T(1,128)}, u32[]{:S(2)}) copy-start(s32[4,1,16,1]{2,3,1,0:T(1,128)} %param.22) | copy-start | bytes 772
  83.2 11.3 %copy-start.7 = (bf16[2,32,128,128]{3,2,1,0:T(8,128)(2,1)S(1)}, bf16[2,32,128,128]{3,2,1,0:T(8,128)(2,1)}, u32[]{:S(2)}) copy-start(bf16[2,32,128,128]{3,2,1,0:T(8,128)(2,1)} %copy-done.5) | copy-start | bytes 6291460
  83.2 11.3 %copy-start.15 = (bf16[1,1,16,128,128]{4,3,2,1,0:T(8,128)(2,1)S(1)}, bf16[1,1,16,128,128]{4,3,2,1,0:T(8,128)(2,1)}, u32[]{:S(2)}) copy-start(bf16[1,1,16,128,128]{4,3,2,1,0:T(8,128)(2,1)} %param.20) | copy-start | bytes 1572868
  83.2 11.3 %copy-start.17 = (s32[1,1,16]{2,1,0:T(1,128)S(1)}, s32[1,1,16]{2,1,0:T(1,128)}, u32[]{:S(2)}) copy-start(s32[1,1,16]{2,1,0:T(1,128)} %param.21) | copy-start | bytes 196
  83.2 11.3 %copy-start.20 = (bf16[8,128,256]{2,1,0:T(8,128)(2,1)S(1)}, bf16[8,128,256]{2,1,0:T(8,128)(2,1)}, u32[]{:S(2)}) copy-start(bf16[8,128,256]{2,1,0:T(8,128)(2,1)} %copy-done.18) | copy-start | bytes 1572868
  83.2 11.3 %collective-permute-start.20 = (bf16[4,128,256]{2,1,0:T(8,128)(2,1)S(1)}, bf16[4,128,256]{2,1,0:T(8,128)(2,1)S(1)}, u32[]{:S(2)}, u32[]{:S(2)}) collective-permute-start(bf16[4,128,256]{2,1,0:T(8,128)(2,1)S(1)} %get-tuple-element.47), channel_id=1, source_target_pairs={{0,24},{8,16},{16,8},{24,0},{1,25},{9,17},{17,9},{25,1},{2,26},{10... | collective-permute-start | bytes 786440 | tf_op jit(solution)/shard_map/ppermute | solution.py:279
  84.5 30.8 %collective-permute-start.21 = (bf16[9,128,256]{2,1,0:T(8,128)(2,1)S(1)}, bf16[9,128,256]{2,1,0:T(8,128)(2,1)S(1)}, u32[]{:S(2)}, u32[]{:S(2)}) collective-permute-start(bf16[9,128,256]{2,1,0:T(8,128)(2,1)S(1)} %get-tuple-element.58), channel_id=1, source_target_pairs={{0,4},{1,5},{2,6},{3,7},{4,0},{5,1},{6,2},{7,3},{8,12},{9,13},{10,... | collective-permute-start | bytes 1769480 | tf_op jit(solution)/shard_map/ppermute | solution.py:276
  91.1 25.2 %collective-permute-start.23 = (bf16[9,128,256]{2,1,0:T(8,128)(2,1)S(1)}, bf16[9,128,256]{2,1,0:T(8,128)(2,1)S(1)}, u32[]{:S(2)}, u32[]{:S(2)}) collective-permute-start(bf16[9,128,256]{2,1,0:T(8,128)(2,1)S(1)} %get-tuple-element.57), channel_id=1, source_target_pairs={{0,2},{1,3},{2,0},{3,1},{4,6},{5,7},{6,4},{7,5},{8,10},{9,11},{10,... | collective-permute-start | bytes 1769480 | tf_op jit(solution)/shard_map/ppermute | solution.py:276
  94.5 25.1 %copy-start.1 = (bf16[256,256]{1,0:T(8,128)(2,1)S(1)}, bf16[256,256]{1,0:T(8,128)(2,1)}, u32[]{:S(2)}) copy-start(bf16[256,256]{1,0:T(8,128)(2,1)} %refs_5_.1) | copy-start | bytes 393220
  98.6 21.0 %collective-permute-start.24 = (bf16[8,128,256]{2,1,0:T(8,128)(2,1)}, bf16[8,128,256]{2,1,0:T(8,128)(2,1)S(1)}, u32[]{:S(2)}, u32[]{:S(2)}) collective-permute-start(bf16[8,128,256]{2,1,0:T(8,128)(2,1)} %get-tuple-element.46), channel_id=1, source_target_pairs={{0,1},{1,0},{2,3},{3,2},{4,5},{5,4},{6,7},{7,6},{8,9},{9,8},{10,11... | collective-permute-start | bytes 1572872 | tf_op jit(solution)/shard_map/ppermute | solution.py:271
  116.4 1.5 %collective-permute-start.26 = (f32[1,128,256]{2,1,0:T(8,128)S(1)}, f32[1,128,256]{2,1,0:T(8,128)}, u32[]{:S(2)}, u32[]{:S(2)}) collective-permute-start(f32[1,128,256]{2,1,0:T(8,128)S(1)} %add_multiply_fusion), channel_id=1, source_target_pairs={{0,1},{1,0},{2,3},{3,2},{4,5},{5,4},{6,7},{7,6},{8,9},{9,8},{10,11... | collective-permute-start | bytes 393224 | tf_op jit(solution)/shard_map/ppermute | solution.py:271

commit v3 on v2

--- a/solution.py
+++ b/solution.py
@@ -226,10 +226,8 @@
     return lax.optimization_barrier((value, *others))[0]
 
 
-def tree_sum(values):
-    while len(values) > 1:
-        values = [a + b for a, b in zip(values[::2], values[1::2])]
-    return values[0]
+def both_sum(mine, theirs):
+    return (mine.astype(F32) + theirs.astype(F32)).astype(BF16)
 
 
 def local(
@@ -391,40 +389,48 @@
     both = (part_own + theirs.astype(F32)).astype(BF16)
     grad = after(grad, both)
 
+    gw = after(gw, both)
+    halves = gw.reshape(2, -1, size, width).astype(BF16)
+    kept = lax.dynamic_index_in_dim(halves, core, 0, keepdims=False)
+    given = lax.dynamic_index_in_dim(halves, 1 - core, 0, keepdims=False)
+    share = both_sum(kept, swap(given))
+    step = 1
+    while step < n_groups:
+        share = both_sum(share, group(share, step))
+        step *= 2
+
     owns, theirs = {}, {}
     for mask in reversed(range(1, last)):
         part_other, owns[mask] = backward(mask, (1, 0), grad)
         theirs[mask] = swap(part_other)
-        if mask == last - 1:
-            gw = after(gw, owns[mask])
-
-    halves = gw.reshape(2, -1, size, width).astype(BF16)
-    kept = lax.dynamic_index_in_dim(halves, core, 0, keepdims=False)
-    given = lax.dynamic_index_in_dim(halves, 1 - core, 0, keepdims=False)
-    share = (kept.astype(F32) + swap(given).astype(F32)).astype(BF16)
-    step = 1
-    while step < n_groups:
-        share = (share.astype(F32) + group(share, step).astype(F32)).astype(BF16)
-        step *= 2
-
     if relay:
         from_ends = across(both, 1, (0, 3))
         middle = across(both, 3, (1, 2))
-        from_ends = after(from_ends, middle, share, owns[1])
+        from_ends = after(from_ends, middle, owns[1])
         far = (owns[2] + theirs[2].astype(F32) + from_ends.astype(F32)).astype(BF16)
         near = (owns[1] + theirs[1].astype(F32)).astype(BF16)
-        back = after(back, far)
-        far = across(jnp.concatenate([far, share]), 2)
-        near = across(jnp.concatenate([near, share]), 1)
-        arrived = [middle, far, near]
-        shares = [share, near[row_tiles:], far[row_tiles:], across(share, 3)]
+        near = after(near, far)
+        arrived = [middle, across(far, 2), across(near, 1)]
     else:
         arrived = [across(both, last)]
         for mask in reversed(range(1, last)):
             arrived.append(across((owns[mask] + theirs[mask].astype(F32)).astype(BF16), mask))
-        shares = [share] + [across(share, m) for m in range(1, n_chips)]
-
-    back_parts = [back[0]] + [group(back[k], k) for k in range(1, n_groups)]
+    for step in tuple(m for m in (2, 1) if m < n_chips) + tuple(1 << i for i in range(2, 8) if 1 << i < n_chips):
+        share = both_sum(share, across(share, step))
+
+    parts = [back[k] for k in range(n_groups)]
+    step = 1
+    while step < n_groups:
+        chosen = [k for k in range(n_groups) if k & step]
+        sent = jnp.concatenate([parts[k] for k in chosen])
+        if step == 1:
+            sent = after(sent, both)
+        elif relay and step == 2:
+            sent = after(sent, far)
+        moved_parts = group(sent, step)
+        for i, k in enumerate(chosen):
+            parts[k] = moved_parts[i * cap : (i + 1) * cap]
+        step *= 2
     part_other, own_sum = call(
         functools.partial(last_products, n_groups, meta),
         "last_products",
@@ -438,10 +444,10 @@
         ],
         hubs * tile_flops,
         moved,
-    )(ints, dest, hub_cols, grad, tiles[0], hub_tiles, *back_parts)
+    )(ints, dest, hub_cols, grad, tiles[0], hub_tiles, *parts)
     arrived.append(swap(part_other))
 
-    share = tree_sum([t.astype(F32) for t in shares]) * (1.0 / math.sqrt(rows_dev * n_blocks * n_groups))
+    share = share.astype(F32) * (1.0 / math.sqrt(rows_dev * n_blocks * n_groups))
     other = swap(share)
     grad_weight = jnp.concatenate(
         [jnp.where(core == 0, share, other), jnp.where(core == 0, other, share)], axis=0

time: 121 us -> 114 us (0.942)
  starting transfers between devices: 40.8 us -> 33.9 us
  local copies, waits for them, and re-layouts: 5.86 us -> 3.16 us
  Pallas kernels: 32.6 us -> 35.3 us
    ppermute x8 -> x7, waiting for transfers between devices: 0.02 us -> 11.8 us  [group(): return lax.ppermute(value, 'grp', [(i, i ^ mask) for i in range(n_groups)])]
    ppermute x9 -> x10, waiting for transfers between devices: 33.3 us -> 22.3 us  [across(): return lax.ppermute(value, 'blk', pairs)]
    ppermute x8 -> x7, starting transfers between devices: 13 us -> 9 us  [group(): return lax.ppermute(value, 'grp', [(i, i ^ mask) for i in range(n_groups)])]
    ppermute x9 -> x10, starting transfers between devices: 25 us -> 21.6 us  [across(): return lax.ppermute(value, 'blk', pairs)]
    unnamed x52 -> x44, local copies, waits for them, and re-layouts: 5.47 us -> 2.68 us
    pallas_call x4, Pallas kernels: 7.53 us -> 9.73 us  [forward(): call(functools.partial(forward_blocks, meta, mask, sides, acc is not None...]
    ppermute x10, waiting for transfers between devices: 3.51 us -> 2.13 us  [swap(): return lax.ppermute(value, 'blk', [(i, i ^ 1) for i in range(n_blocks)])]
  transfers between devices with their start and end apart: 27 -> 27, of which waited for: 9 -> 10; matrix products, arithmetic and copies ran while one was open for 2% -> 4% of each run, Pallas kernels for 20% -> 25%
where the time goes in v3:
time: 114 us
  waiting for transfers between devices  36.2 us (32%)
  Pallas kernels  35.3 us (31%)
  starting transfers between devices  33.9 us (30%)
  other arithmetic  4.05 us (4%)
  local copies, waits for them, and re-layouts  3.16 us (3%)
  between operations  1.19 us (1%)
    ppermute x10, waiting for transfers between devices, across(): return lax.ppermute(value, 'blk', pairs)  22.3 us
    ppermute x10, starting transfers between devices, across(): return lax.ppermute(value, 'blk', pairs)  21.6 us
    ppermute x7, waiting for transfers between devices, group(): return lax.ppermute(value, 'grp', [(i, i ^ mask) for i in range(n_groups)])  11.8 us
    pallas_call x4, Pallas kernels, forward(): call(functools.partial(forward_blocks, meta, mask, sides, acc is not None...  9.73 us
    ppermute x7, starting transfers between devices, group(): return lax.ppermute(value, 'grp', [(i, i ^ mask) for i in range(n_groups)])  9 us
    pallas_call x4, Pallas kernels, backward(): call(functools.partial(backward_blocks, meta, mask, sides), 'backward_blo...  7.39 us
    pallas_call x1, Pallas kernels, local(): call(functools.partial(stage_tiles, meta), 'stage_tiles', (jax.ShapeDtype...  6.15 us
    pallas_call x1, Pallas kernels, local(): call(functools.partial(last_forward, meta, last), 'last_forward', (jax.Sh...  4.26 us
  transfers between devices with their start and end apart: 27, of which 10 were waited for; matrix products, arithmetic and copies ran while one was open for 4% of the time, Pallas kernels for 25%

profile of v3, /device:TPU:0, one launch (start us, length us, event | category | flops | bytes accessed | tf_op | source)
XLA Modules:
  0.0 113.8 jit_solution(3567468380690488195)
XLA Ops:
  0.6 0.5 collective-permute-start
  1.1 2.7 %collective-permute-start.4 = (bf16[8,128,256]{2,1,0:T(8,128)(2,1)}, bf16[8,128,256]{2,1,0:T(8,128)(2,1)}, u32[]{:S(2)}, u32[]{:S(2)}) collective-permute-start(bf16[8,128,256]{2,1,0:T(8,128)(2,1)} %bitcast.47), channel_id=1, source_target_pairs={{0,2},{1,3},{2,0},{3,1},{4,6},{5,7},{6,4},{7,5},{8,10},{9,11},{10,... | collective-permute-start | bytes 1572872 | tf_op jit(solution)/shard_map/ppermute | solution.py:274
  3.8 2.6 %collective-permute-start.6 = (bf16[8,128,256]{2,1,0:T(8,128)(2,1)}, bf16[8,128,256]{2,1,0:T(8,128)(2,1)}, u32[]{:S(2)}, u32[]{:S(2)}) collective-permute-start(bf16[8,128,256]{2,1,0:T(8,128)(2,1)} %bitcast.48), channel_id=1, source_target_pairs={{0,4},{1,5},{2,6},{3,7},{4,0},{5,1},{6,2},{7,3},{8,12},{9,13},{10,... | collective-permute-start | bytes 1572872 | tf_op jit(solution)/shard_map/ppermute | solution.py:274
  6.4 0.1 pad_add_fusion.pos
  6.5 0.0 copy-start.12
  6.5 6.1 %stage_tiles.1 = (bf16[2,32,128,128]{3,2,1,0:T(8,128)(2,1)S(1)}, bf16[2,32,128,128]{3,2,1,0:T(8,128)(2,1)S(1)}, bf16[2,32,128,128]{3,2,1,0:T(8,128)(2,1)}, bf16[2,32,128,128]{3,2,1,0:T(8,128)(2,1)}) custom-call(s32[3]{0:T(128)S(1)} %pad_add_fusion.pos, bf16[8,32,128,128]{3,2,1,0:T(8,128)(2,1)} %bitcast.56), custom_call_target="tpu_custom_call" | custom-call | flops 1 | bytes 419430400 | tf_op jit(solution)/shard_map/stage_tiles/pallas_call | solution.py:282
  12.7 1.3 %copy-done.7 = bf16[2,32,128,128]{3,2,1,0:T(8,128)(2,1)} copy-done((bf16[2,32,128,128]{3,2,1,0:T(8,128)(2,1)}, bf16[2,32,128,128]{3,2,1,0:T(8,128)(2,1)S(1)}, u32[]{:S(2)}) %copy-start.7) | copy-done | bytes 2097176
  14.0 0.1 reshape.58
  14.1 0.1 reshape.59
  14.2 0.1 concatenate.13.ints
  14.3 0.2 broadcast_select_fusion
  14.6 1.2 %copy-done.13 = bf16[1,1,16,128,128]{4,3,2,1,0:T(8,128)(2,1)S(1)} copy-done((bf16[1,1,16,128,128]{4,3,2,1,0:T(8,128)(2,1)S(1)}, bf16[1,1,16,128,128]{4,3,2,1,0:T(8,128)(2,1)}, u32[]{:S(2)}) %copy-start.13) | copy-done | bytes 524312
  15.8 1.0 hub_products.1
  16.8 0.1 slice_bitcast_fusion
  16.9 1.6 %collective-permute-start.1 = (bf16[4,128,256]{2,1,0:T(8,128)(2,1)S(1)}, bf16[4,128,256]{2,1,0:T(8,128)(2,1)S(1)}, u32[]{:S(2)}, u32[]{:S(2)}) collective-permute-start(bf16[4,128,256]{2,1,0:T(8,128)(2,1)S(1)} %get-tuple-element.57), channel_id=1, source_target_pairs={{0,8},{8,0},{16,24},{24,16},{1,9},{9,1},{17,25},{25,17},{2,10},{10... | collective-permute-start | bytes 786440 | tf_op jit(solution)/shard_map/ppermute | solution.py:277
  18.5 1.5 %collective-permute-start.2 = (bf16[4,128,256]{2,1,0:T(8,128)(2,1)S(1)}, bf16[4,128,256]{2,1,0:T(8,128)(2,1)S(1)}, u32[]{:S(2)}, u32[]{:S(2)}) collective-permute-start(bf16[4,128,256]{2,1,0:T(8,128)(2,1)S(1)} %get-tuple-element.56), channel_id=1, source_target_pairs={{0,16},{8,24},{16,0},{24,8},{1,17},{9,25},{17,1},{25,9},{2,18},{10... | collective-permute-start | bytes 786440 | tf_op jit(solution)/shard_map/ppermute | solution.py:277
  20.0 0.5 collective-permute-start.3
  20.5 7.3 %collective-permute-done.4.refs_2_ = bf16[8,128,256]{2,1,0:T(8,128)(2,1)} collective-permute-done((bf16[8,128,256]{2,1,0:T(8,128)(2,1)}, bf16[8,128,256]{2,1,0:T(8,128)(2,1)}, u32[]{:S(2)}, u32[]{:S(2)}) %collective-permute-start.4) | collective-permute-done | bytes 524320 | tf_op jit(solution)/shard_map/ppermute | solution.py:274
  27.7 2.6 %forward_blocks.4.refs_0_ = f32[8,128,256]{2,1,0:T(8,128)S(1)} custom-call(s32[523]{0:T(1024)S(1)} %concatenate.13.ints, bf16[8,128,256]{2,1,0:T(8,128)(2,1)} %collective-permute-done.refs_0_, bf16[8,128,256]{2,1,0:T(8,128)(2,1)S(1)} %bitcast.50, bf16[2,32,128,128]{3,2,1,0:T(8,128)(2,1)S(1)} %get-tuple-element.27.refs_2_.tiles), custom_call_target="tpu_custom_call" | custom-call | flops 53687091200 | bytes 419430400 | tf_op jit(solution)/shard_map/forward_blocks/pallas_call | solution.py:295
  30.4 1.4 %collective-permute-start.8 = (bf16[8,128,256]{2,1,0:T(8,128)(2,1)}, bf16[8,128,256]{2,1,0:T(8,128)(2,1)S(1)}, u32[]{:S(2)}, u32[]{:S(2)}) collective-permute-start(bf16[8,128,256]{2,1,0:T(8,128)(2,1)} %collective-permute-done.6.refs_2_), channel_id=1, source_target_pairs={{2,0},{3,1},{4,6},{5,7},{10,8},{11,9},{12,14},{13,15},{18,16},{19,... | collective-permute-start | bytes 1572872 | tf_op jit(solution)/shard_map/ppermute | solution.py:274
  31.8 0.7 collective-permute-start.9
  32.6 0.6 collective-permute-start.7
  33.1 1.9 %hub_add.1.refs_0_ = f32[8,128,256]{2,1,0:T(8,128)S(1)} custom-call(s32[3]{0:T(128)S(1)} %pad_add_fusion.pos, s32[4,16]{1,0:T(4,128)S(1)} %bitcast.43, s32[4,16]{1,0:T(4,128)S(1)} %bitcast.40, f32[8,128,256]{2,1,0:T(8,128)S(1)} %forward_blocks.4.refs_0_, bf16[4,128,256]{2,1,0:T(8,128)(2,1)S(1)} %get-tuple-element.58.refs_1_, ...), custom_call_target="tpu_custom_call" | custom-call | flops 1048576 | bytes 419430400 | tf_op jit(solution)/shard_map/hub_add/pallas_call | solution.py:348
  35.1 2.7 %forward_blocks.5.refs_0_ = f32[8,128,256]{2,1,0:T(8,128)S(1)} custom-call(s32[523]{0:T(1024)S(1)} %concatenate.13.ints, f32[8,128,256]{2,1,0:T(8,128)S(1)} %hub_add.1.refs_0_, bf16[8,128,256]{2,1,0:T(8,128)(2,1)S(1)} %collective-permute-done.5.refs_1_, bf16[8,128,256]{2,1,0:T(8,128)(2,1)} %collective-permute-done.4.refs_2_, ...), custom_call_target="tpu_custom_call" | custom-call | flops 53687091200 | bytes 419430400 | tf_op jit(solution)/shard_map/forward_blocks/pallas_call | solution.py:295
  37.9 3.2 %forward_blocks.6.refs_0_ = f32[8,128,256]{2,1,0:T(8,128)S(1)} custom-call(s32[523]{0:T(1024)S(1)} %concatenate.13.ints, f32[8,128,256]{2,1,0:T(8,128)S(1)} %forward_blocks.5.refs_0_, bf16[8,128,256]{2,1,0:T(8,128)(2,1)S(1)} %collective-permute-done.7.refs_1_, bf16[8,128,256]{2,1,0:T(8,128)(2,1)} %collective-permute-done.6.refs_2_, ...), custom_call_target="tpu_custom_call" | custom-call | flops 53687091200 | bytes 419430400 | tf_op jit(solution)/shard_map/forward_blocks/pallas_call | solution.py:295
  41.1 5.9 %collective-permute-done.8 = bf16[8,128,256]{2,1,0:T(8,128)(2,1)S(1)} collective-permute-done((bf16[8,128,256]{2,1,0:T(8,128)(2,1)}, bf16[8,128,256]{2,1,0:T(8,128)(2,1)S(1)}, u32[]{:S(2)}, u32[]{:S(2)}) %collective-permute-start.8) | collective-permute-done | bytes 524320 | tf_op jit(solution)/shard_map/ppermute | solution.py:274
  47.0 0.1 add.44.refs_1_
  47.1 0.1 collective-permute-start.10
  47.2 1.2 %forward_blocks.7.acc = f32[8,128,256]{2,1,0:T(8,128)S(1)} custom-call(s32[523]{0:T(1024)S(1)} %concatenate.13.ints, f32[8,128,256]{2,1,0:T(8,128)S(1)} %forward_blocks.6.refs_0_, bf16[8,128,256]{2,1,0:T(8,128)(2,1)S(1)} %add.44.refs_1_, bf16[2,32,128,128]{3,2,1,0:T(8,128)(2,1)S(1)} %copy-done.11), custom_call_target="tpu_custom_call" | custom-call | flops 26843545600 | bytes 419430400 | tf_op jit(solution)/shard_map/forward_blocks/pallas_call | solution.py:295
  48.4 0.7 collective-permute-done.10.refs_0_
  49.1 4.3 %last_forward.1 = (bf16[8,128,256]{2,1,0:T(8,128)(2,1)}, bf16[8,128,256]{2,1,0:T(8,128)(2,1)S(1)}, bf16[4,4,128,256]{3,2,1,0:T(8,128)(2,1)S(1)}, f32[256,256]{1,0:T(8,128)S(1)}) custom-call(s32[523]{0:T(1024)S(1)} %concatenate.13.ints, s32[4,16]{1,0:T(4,128)S(1)} %bitcast.44, s32[4,16]{1,0:T(4,128)S(1)} %bitcast.41, f32[8,128,256]{2,1,0:T(8,128)S(1)} %forward_blocks.7.acc, ...), custom_call_target="tpu_custom_call" | custom-call | flops 26843545600 | bytes 419430400 | tf_op jit(solution)/shard_map/last_forward/pallas_call | solution.py:367
  53.3 1.2 %backward_blocks.5 = bf16[8,128,256]{2,1,0:T(8,128)(2,1)S(1)} custom-call(s32[523]{0:T(1024)S(1)} %concatenate.13.ints, bf16[8,128,256]{2,1,0:T(8,128)(2,1)S(1)} %get-tuple-element.37.grad, bf16[2,32,128,128]{3,2,1,0:T(8,128)(2,1)S(1)} %copy-done.11), custom_call_target="tpu_custom_call" | custom-call | flops 26843545600 | bytes 419430400 | tf_op jit(solution)/shard_map/backward_blocks/pallas_call | solution.py:310
  54.5 1.1 collective-permute-start.11
  55.6 1.2 %backward_blocks.4 = f32[8,128,256]{2,1,0:T(8,128)S(1)} custom-call(s32[523]{0:T(1024)S(1)} %concatenate.13.ints, bf16[8,128,256]{2,1,0:T(8,128)(2,1)S(1)} %get-tuple-element.37.grad, bf16[2,32,128,128]{3,2,1,0:T(8,128)(2,1)S(1)} %copy-done.11), custom_call_target="tpu_custom_call" | custom-call | flops 26843545600 | bytes 419430400 | tf_op jit(solution)/shard_map/backward_blocks/pallas_call | solution.py:310
  56.8 0.1 slice_bitcast_fusion.4
  56.9 0.2 collective-permute-done.11
  57.2 0.1 add_convert_fusion.2
  57.3 0.4 collective-permute-start.21
  57.8 4.8 %collective-permute-start.14 = (bf16[8,128,256]{2,1,0:T(8,128)(2,1)S(1)}, bf16[8,128,256]{2,1,0:T(8,128)(2,1)S(1)}, u32[]{:S(2)}, u32[]{:S(2)}) collective-permute-start(bf16[8,128,256]{2,1,0:T(8,128)(2,1)S(1)} %add_convert_fusion.2), channel_id=1, source_target_pairs={{0,2},{1,3},{6,4},{7,5},{8,10},{9,11},{14,12},{15,13},{16,18},{17,... | collective-permute-start | bytes 1572872 | tf_op jit(solution)/shard_map/ppermute | solution.py:274
  62.6 0.7 collective-permute-start.15
  63.4 2.9 %collective-permute-start.22 = (bf16[1,128,256]{2,1,0:T(8,128)(2,1)S(1)}, bf16[1,128,256]{2,1,0:T(8,128)(2,1)S(1)}, u32[]{:S(2)}, u32[]{:S(2)}) collective-permute-start(bf16[1,128,256]{2,1,0:T(8,128)(2,1)S(1)} %fusion), channel_id=1, source_target_pairs={{0,8},{8,0},{16,24},{24,16},{1,9},{9,1},{17,25},{25,17},{2,10},{10... | collective-permute-start | bytes 196616 | tf_op jit(solution)/shard_map/ppermute | solution.py:277
  66.2 2.7 %backward_blocks.6 = (bf16[8,128,256]{2,1,0:T(8,128)(2,1)S(1)}, f32[8,128,256]{2,1,0:T(8,128)S(1)}) custom-call(s32[523]{0:T(1024)S(1)} %concatenate.13.ints, bf16[8,128,256]{2,1,0:T(8,128)(2,1)S(1)} %get-tuple-element.37.grad, bf16[2,32,128,128]{3,2,1,0:T(8,128)(2,1)S(1)} %copy-done.10), custom_call_target="tpu_custom_call" | custom-call | flops 53687091200 | bytes 419430400 | tf_op jit(solution)/shard_map/backward_blocks/pallas_call | solution.py:310
  69.0 0.1 collective-permute-start.13
  69.1 0.1 collective-permute-start.12
  69.2 1.3 %collective-permute-start.23 = (bf16[1,128,256]{2,1,0:T(8,128)(2,1)S(1)}, bf16[1,128,256]{2,1,0:T(8,128)(2,1)S(1)}, u32[]{:S(2)}, u32[]{:S(2)}) collective-permute-start(bf16[1,128,256]{2,1,0:T(8,128)(2,1)S(1)} %add_convert_fusion.6), channel_id=1, source_target_pairs={{0,16},{8,24},{16,0},{24,8},{1,17},{9,25},{17,1},{25,9},{2,18},{10... | collective-permute-start | bytes 196616 | tf_op jit(solution)/shard_map/ppermute | solution.py:277
  70.4 2.3 %backward_blocks.7 = (bf16[8,128,256]{2,1,0:T(8,128)(2,1)S(1)}, f32[8,128,256]{2,1,0:T(8,128)S(1)}) custom-call(s32[523]{0:T(1024)S(1)} %concatenate.13.ints, bf16[8,128,256]{2,1,0:T(8,128)(2,1)S(1)} %get-tuple-element.37.grad, bf16[2,32,128,128]{3,2,1,0:T(8,128)(2,1)S(1)} %copy-done.9), custom_call_target="tpu_custom_call" | custom-call | flops 53687091200 | bytes 419430400 | tf_op jit(solution)/shard_map/backward_blocks/pallas_call | solution.py:310
  72.7 1.0 collective-permute-done.23
  73.7 0.5 collective-permute-done.14
  74.2 4.2 %collective-permute-start.24 = (bf16[1,128,256]{2,1,0:T(8,128)(2,1)S(1)}, bf16[1,128,256]{2,1,0:T(8,128)(2,1)S(1)}, u32[]{:S(2)}, u32[]{:S(2)}) collective-permute-start(bf16[1,128,256]{2,1,0:T(8,128)(2,1)S(1)} %add_convert_fusion.5), channel_id=1, source_target_pairs={{0,4},{1,5},{2,6},{3,7},{4,0},{5,1},{6,2},{7,3},{8,12},{9,13},{10,... | collective-permute-start | bytes 196616 | tf_op jit(solution)/shard_map/ppermute | solution.py:274
  78.3 1.0 add_convert_fusion.1
  79.3 4.1 %collective-permute-done.12 = bf16[8,128,256]{2,1,0:T(8,128)(2,1)S(1)} collective-permute-done((bf16[8,128,256]{2,1,0:T(8,128)(2,1)S(1)}, bf16[8,128,256]{2,1,0:T(8,128)(2,1)S(1)}, u32[]{:S(2)}, u32[]{:S(2)}) %collective-permute-start.12) | collective-permute-done | bytes 524320 | tf_op jit(solution)/shard_map/ppermute | solution.py:277
  83.5 1.3 %collective-permute-start.16 = (bf16[8,128,256]{2,1,0:T(8,128)(2,1)S(1)}, bf16[8,128,256]{2,1,0:T(8,128)(2,1)S(1)}, u32[]{:S(2)}, u32[]{:S(2)}) collective-permute-start(bf16[8,128,256]{2,1,0:T(8,128)(2,1)S(1)} %pad_maximum_fusion.1), channel_id=1, source_target_pairs={{0,16},{8,24},{16,0},{24,8},{1,17},{9,25},{17,1},{25,9},{2,18},{10... | collective-permute-start | bytes 1572872 | tf_op jit(solution)/shard_map/ppermute | solution.py:277
  84.8 1.8 %collective-permute-start.25 = (bf16[1,128,256]{2,1,0:T(8,128)(2,1)S(1)}, bf16[1,128,256]{2,1,0:T(8,128)(2,1)S(1)}, u32[]{:S(2)}, u32[]{:S(2)}) collective-permute-start(bf16[1,128,256]{2,1,0:T(8,128)(2,1)S(1)} %add_convert_fusion.4), channel_id=1, source_target_pairs={{0,2},{1,3},{2,0},{3,1},{4,6},{5,7},{6,4},{7,5},{8,10},{9,11},{10,... | collective-permute-start | bytes 196616 | tf_op jit(solution)/shard_map/ppermute | solution.py:274
  86.6 0.9 collective-permute-start.17
  87.5 0.9 add_convert_fusion
  88.4 1.9 %collective-permute-start.19 = (bf16[8,128,256]{2,1,0:T(8,128)(2,1)}, bf16[8,128,256]{2,1,0:T(8,128)(2,1)S(1)}, u32[]{:S(2)}, u32[]{:S(2)}) collective-permute-start(bf16[8,128,256]{2,1,0:T(8,128)(2,1)} %add_convert_fusion), channel_id=1, source_target_pairs={{0,2},{1,3},{2,0},{3,1},{4,6},{5,7},{6,4},{7,5},{8,10},{9,11},{10,... | collective-permute-start | bytes 1572872 | tf_op jit(solution)/shard_map/ppermute | solution.py:274
  90.3 6.7 %collective-permute-done.16 = bf16[8,128,256]{2,1,0:T(8,128)(2,1)S(1)} collective-permute-done((bf16[8,128,256]{2,1,0:T(8,128)(2,1)S(1)}, bf16[8,128,256]{2,1,0:T(8,128)(2,1)S(1)}, u32[]{:S(2)}, u32[]{:S(2)}) %collective-permute-start.16) | collective-permute-done | bytes 524320 | tf_op jit(solution)/shard_map/ppermute | solution.py:277
  97.2 3.6 %last_products.1 = (bf16[8,128,256]{2,1,0:T(8,128)(2,1)}, f32[8,128,256]{2,1,0:T(8,128)S(1)}) custom-call(s32[523]{0:T(1024)S(1)} %concatenate.13.ints, s32[4,16]{1,0:T(4,128)S(1)} %bitcast.45, s32[16]{0:T(128)S(1)} %bitcast.55, bf16[8,128,256]{2,1,0:T(8,128)(2,1)S(1)} %get-tuple-element.37.grad, bf16[2,32,128,128]{3,2,1,0:T(8,128)(2,1)S(1)} %copy-done.6, ...), custom_call_target="tpu_custom_call" | custom-call | flops 13421772800 | bytes 419430400 | tf_op jit(solution)/shard_map/last_products/pallas_call | solution.py:434
  100.8 0.7 convert_multiply_fusion
  101.5 0.5 collective-permute-start.26
  102.0 1.2 %collective-permute-done.26 = f32[1,128,256]{2,1,0:T(8,128)S(1)} collective-permute-done((f32[1,128,256]{2,1,0:T(8,128)}, f32[1,128,256]{2,1,0:T(8,128)S(1)}, u32[]{:S(2)}, u32[]{:S(2)}) %collective-permute-start.26) | collective-permute-done | bytes 131104 | tf_op jit(solution)/shard_map/ppermute | solution.py:269
  103.2 0.7 pad_maximum_fusion.2
  103.9 8.6 %collective-permute-done.19.refs_3_ = bf16[8,128,256]{2,1,0:T(8,128)(2,1)S(1)} collective-permute-done((bf16[8,128,256]{2,1,0:T(8,128)(2,1)}, bf16[8,128,256]{2,1,0:T(8,128)(2,1)S(1)}, u32[]{:S(2)}, u32[]{:S(2)}) %collective-permute-start.19) | collective-permute-done | bytes 524320 | tf_op jit(solution)/shard_map/ppermute | solution.py:274
  112.6 1.2 %last_backward.1 = bf16[1024,256]{1,0:T(8,128)(2,1)} custom-call(f32[8,128,256]{2,1,0:T(8,128)S(1)} %get-tuple-element.45.refs_0_, bf16[8,128,256]{2,1,0:T(8,128)(2,1)S(1)} %collective-permute-done.15.refs_1_, bf16[8,128,256]{2,1,0:T(8,128)(2,1)S(1)} %collective-permute-done.17.refs_2_, bf16[8,128,256]{2,1,0:T(8,128)(2,1)S(1)} %collective-permute-done.19.refs_3_, ...), custom_call_target="tpu_custom_call" | custom-call | flops 419430400 | bytes 419430400 | tf_op jit(solution)/shard_map/last_backward/pallas_call | solution.py:456
  (73 shorter events, 0.5 us)
Async XLA Ops:
  0.6 13.9 %collective-permute-start = (bf16[8,128,256]{2,1,0:T(8,128)(2,1)}, bf16[8,128,256]{2,1,0:T(8,128)(2,1)}, u32[]{:S(2)}, u32[]{:S(2)}) collective-permute-start(bf16[8,128,256]{2,1,0:T(8,128)(2,1)} %bitcast.46), channel_id=1, source_target_pairs={{0,1},{1,0},{2,3},{3,2},{4,5},{5,4},{6,7},{7,6},{8,9},{9,8},{10,11... | collective-permute-start | bytes 1572872 | tf_op jit(solution)/shard_map/ppermute | solution.py:269
  1.1 26.6 %collective-permute-start.4 = (bf16[8,128,256]{2,1,0:T(8,128)(2,1)}, bf16[8,128,256]{2,1,0:T(8,128)(2,1)}, u32[]{:S(2)}, u32[]{:S(2)}) collective-permute-start(bf16[8,128,256]{2,1,0:T(8,128)(2,1)} %bitcast.47), channel_id=1, source_target_pairs={{0,2},{1,3},{2,0},{3,1},{4,6},{5,7},{6,4},{7,5},{8,10},{9,11},{10,... | collective-permute-start | bytes 1572872 | tf_op jit(solution)/shard_map/ppermute | solution.py:274
  3.8 26.6 %collective-permute-start.6 = (bf16[8,128,256]{2,1,0:T(8,128)(2,1)}, bf16[8,128,256]{2,1,0:T(8,128)(2,1)}, u32[]{:S(2)}, u32[]{:S(2)}) collective-permute-start(bf16[8,128,256]{2,1,0:T(8,128)(2,1)} %bitcast.48), channel_id=1, source_target_pairs={{0,4},{1,5},{2,6},{3,7},{4,0},{5,1},{6,2},{7,3},{8,12},{9,13},{10,... | collective-permute-start | bytes 1572872 | tf_op jit(solution)/shard_map/ppermute | solution.py:274
  6.5 7.6 %copy-start.18 = (s32[1,1,8,32]{3,2,1,0:T(8,128)S(1)}, s32[1,1,8,32]{3,2,1,0:T(8,128)}, u32[]{:S(2)}) copy-start(s32[1,1,8,32]{3,2,1,0:T(8,128)} %param.17) | copy-start | bytes 3076
  6.5 7.7 %copy-start.19 = (s32[1,1,8,32]{3,2,1,0:T(8,128)S(1)}, s32[1,1,8,32]{3,2,1,0:T(8,128)}, u32[]{:S(2)}) copy-start(s32[1,1,8,32]{3,2,1,0:T(8,128)} %param.18) | copy-start | bytes 3076
  6.5 7.7 %copy-start.21 = (s32[1,1,8]{2,1,0:T(1,128)S(1)}, s32[1,1,8]{2,1,0:T(1,128)}, u32[]{:S(2)}) copy-start(s32[1,1,8]{2,1,0:T(1,128)} %param.19) | copy-start | bytes 100
  6.5 7.8 %copy-start.20 = (s32[1024]{0:T(1024)S(1)}, s32[1024]{0:T(1024)}, u32[]{:S(2)}) copy-start(s32[1024]{0:T(1024)} %param.15) | copy-start | bytes 12292
  6.5 7.8 %copy-start.17 = (bf16[1024,256]{1,0:T(8,128)(2,1)S(1)}, bf16[1024,256]{1,0:T(8,128)(2,1)}, u32[]{:S(2)}) copy-start(bf16[1024,256]{1,0:T(8,128)(2,1)} %param.14) | copy-start | bytes 1572868
  6.5 8.0 %copy-start.3 = (s32[4,1,16,1]{2,3,1,0:T(1,128)S(1)}, s32[4,1,16,1]{2,3,1,0:T(1,128)}, u32[]{:S(2)}) copy-start(s32[4,1,16,1]{2,3,1,0:T(1,128)} %param.22) | copy-start | bytes 772
  6.5 8.0 %copy-start.12 = (bf16[1024,256]{1,0:T(8,128)(2,1)S(1)}, bf16[1024,256]{1,0:T(8,128)(2,1)}, u32[]{:S(2)}) copy-start(bf16[1024,256]{1,0:T(8,128)(2,1)} %param.12) | copy-start | bytes 1572868
  6.5 8.0 %copy-start.15 = (s32[1,1,16]{2,1,0:T(1,128)S(1)}, s32[1,1,16]{2,1,0:T(1,128)}, u32[]{:S(2)}) copy-start(s32[1,1,16]{2,1,0:T(1,128)} %param.21) | copy-start | bytes 196
  12.7 1.4 %copy-start.7 = (bf16[2,32,128,128]{3,2,1,0:T(8,128)(2,1)}, bf16[2,32,128,128]{3,2,1,0:T(8,128)(2,1)S(1)}, u32[]{:S(2)}) copy-start(bf16[2,32,128,128]{3,2,1,0:T(8,128)(2,1)S(1)} %get-tuple-element.29.refs_3_.tiles) | copy-start | bytes 6291460
  14.0 13.7 %copy-start.5 = (bf16[2,32,128,128]{3,2,1,0:T(8,128)(2,1)}, bf16[2,32,128,128]{3,2,1,0:T(8,128)(2,1)S(1)}, u32[]{:S(2)}) copy-start(bf16[2,32,128,128]{3,2,1,0:T(8,128)(2,1)S(1)} %get-tuple-element.27.refs_2_.tiles) | copy-start | bytes 6291460
  14.6 1.2 %copy-start.13 = (bf16[1,1,16,128,128]{4,3,2,1,0:T(8,128)(2,1)S(1)}, bf16[1,1,16,128,128]{4,3,2,1,0:T(8,128)(2,1)}, u32[]{:S(2)}) copy-start(bf16[1,1,16,128,128]{4,3,2,1,0:T(8,128)(2,1)} %param.20) | copy-start | bytes 1572868
  16.9 14.9 %collective-permute-start.1 = (bf16[4,128,256]{2,1,0:T(8,128)(2,1)S(1)}, bf16[4,128,256]{2,1,0:T(8,128)(2,1)S(1)}, u32[]{:S(2)}, u32[]{:S(2)}) collective-permute-start(bf16[4,128,256]{2,1,0:T(8,128)(2,1)S(1)} %get-tuple-element.57), channel_id=1, source_target_pairs={{0,8},{8,0},{16,24},{24,16},{1,9},{9,1},{17,25},{25,17},{2,10},{10... | collective-permute-start | bytes 786440 | tf_op jit(solution)/shard_map/ppermute | solution.py:277
  18.5 14.1 %collective-permute-start.2 = (bf16[4,128,256]{2,1,0:T(8,128)(2,1)S(1)}, bf16[4,128,256]{2,1,0:T(8,128)(2,1)S(1)}, u32[]{:S(2)}, u32[]{:S(2)}) collective-permute-start(bf16[4,128,256]{2,1,0:T(8,128)(2,1)S(1)} %get-tuple-element.56), channel_id=1, source_target_pairs={{0,16},{8,24},{16,0},{24,8},{1,17},{9,25},{17,1},{25,9},{2,18},{10... | collective-permute-start | bytes 786440 | tf_op jit(solution)/shard_map/ppermute | solution.py:277
  20.0 13.1 %collective-permute-start.3 = (bf16[4,128,256]{2,1,0:T(8,128)(2,1)S(1)}, bf16[4,128,256]{2,1,0:T(8,128)(2,1)S(1)}, u32[]{:S(2)}, u32[]{:S(2)}) collective-permute-start(bf16[4,128,256]{2,1,0:T(8,128)(2,1)S(1)} %get-tuple-element.55), channel_id=1, source_target_pairs={{0,24},{8,16},{16,8},{24,0},{1,25},{9,17},{17,9},{25,1},{2,26},{10... | collective-permute-start | bytes 786440 | tf_op jit(solution)/shard_map/ppermute | solution.py:277
  27.7 7.3 %collective-permute-start.5 = (bf16[8,128,256]{2,1,0:T(8,128)(2,1)}, bf16[8,128,256]{2,1,0:T(8,128)(2,1)S(1)}, u32[]{:S(2)}, u32[]{:S(2)}) collective-permute-start(bf16[8,128,256]{2,1,0:T(8,128)(2,1)} %collective-permute-done.4.refs_2_), channel_id=1, source_target_pairs={{0,1},{1,0},{2,3},{3,2},{4,5},{5,4},{6,7},{7,6},{8,9},{9,8},{10,11... | collective-permute-start | bytes 1572872 | tf_op jit(solution)/shard_map/ppermute | solution.py:269
  27.7 5.4 %copy-start.2 = (s32[4,1,16]{2,1,0:T(1,128)S(1)}, s32[4,1,16]{2,1,0:T(1,128)}, u32[]{:S(2)}) copy-start(s32[4,1,16]{2,1,0:T(1,128)} %param.23) | copy-start | bytes 772
  30.4 4.7 %copy-start.8 = (bf16[2,32,128,128]{3,2,1,0:T(8,128)(2,1)S(1)}, bf16[2,32,128,128]{3,2,1,0:T(8,128)(2,1)}, u32[]{:S(2)}) copy-start(bf16[2,32,128,128]{3,2,1,0:T(8,128)(2,1)} %copy-done.7) | copy-start | bytes 6291460
  30.4 16.6 %collective-permute-start.8 = (bf16[8,128,256]{2,1,0:T(8,128)(2,1)}, bf16[8,128,256]{2,1,0:T(8,128)(2,1)S(1)}, u32[]{:S(2)}, u32[]{:S(2)}) collective-permute-start(bf16[8,128,256]{2,1,0:T(8,128)(2,1)} %collective-permute-done.6.refs_2_), channel_id=1, source_target_pairs={{2,0},{3,1},{4,6},{5,7},{10,8},{11,9},{12,14},{13,15},{18,16},{19,... | collective-permute-start | bytes 1572872 | tf_op jit(solution)/shard_map/ppermute | solution.py:274
  31.8 15.1 %collective-permute-start.9 = (bf16[8,128,256]{2,1,0:T(8,128)(2,1)S(1)}, bf16[8,128,256]{2,1,0:T(8,128)(2,1)S(1)}, u32[]{:S(2)}, u32[]{:S(2)}) collective-permute-start(bf16[8,128,256]{2,1,0:T(8,128)(2,1)S(1)} %bitcast.51), channel_id=1, source_target_pairs={{2,4},{3,5},{4,2},{5,3},{10,12},{11,13},{12,10},{13,11},{18,20},{1... | collective-permute-start | bytes 1572872 | tf_op jit(solution)/shard_map/ppermute | solution.py:274
  32.6 5.3 %collective-permute-start.7 = (bf16[8,128,256]{2,1,0:T(8,128)(2,1)}, bf16[8,128,256]{2,1,0:T(8,128)(2,1)S(1)}, u32[]{:S(2)}, u32[]{:S(2)}) collective-permute-start(bf16[8,128,256]{2,1,0:T(8,128)(2,1)} %collective-permute-done.6.refs_2_), channel_id=1, source_target_pairs={{0,1},{1,0},{2,3},{3,2},{4,5},{5,4},{6,7},{7,6},{8,9},{9,8},{10,11... | collective-permute-start | bytes 1572872 | tf_op jit(solution)/shard_map/ppermute | solution.py:269
  35.1 2.8 %copy-start.10 = (bf16[2,32,128,128]{3,2,1,0:T(8,128)(2,1)S(1)}, bf16[2,32,128,128]{3,2,1,0:T(8,128)(2,1)}, u32[]{:S(2)}) copy-start(bf16[2,32,128,128]{3,2,1,0:T(8,128)(2,1)} %get-tuple-element.30.refs_3_.tiles) | copy-start | bytes 6291460
  37.9 9.3 %copy-start.11 = (bf16[2,32,128,128]{3,2,1,0:T(8,128)(2,1)S(1)}, bf16[2,32,128,128]{3,2,1,0:T(8,128)(2,1)}, u32[]{:S(2)}) copy-start(bf16[2,32,128,128]{3,2,1,0:T(8,128)(2,1)} %get-tuple-element.34.refs_2_.tiles) | copy-start | bytes 6291460
  47.1 2.0 %collective-permute-start.10 = (bf16[8,128,256]{2,1,0:T(8,128)(2,1)S(1)}, bf16[8,128,256]{2,1,0:T(8,128)(2,1)S(1)}, u32[]{:S(2)}, u32[]{:S(2)}) collective-permute-start(bf16[8,128,256]{2,1,0:T(8,128)(2,1)S(1)} %add.44.refs_1_), channel_id=1, source_target_pairs={{0,1},{1,0},{2,3},{3,2},{4,5},{5,4},{6,7},{7,6},{8,9},{9,8},{10,11... | collective-permute-start | bytes 1572872 | tf_op jit(solution)/shard_map/ppermute | solution.py:269
  47.2 1.9 %copy-start = (bf16[256,256]{1,0:T(8,128)(2,1)S(1)}, bf16[256,256]{1,0:T(8,128)(2,1)}, u32[]{:S(2)}) copy-start(bf16[256,256]{1,0:T(8,128)(2,1)} %refs_5_.1) | copy-start | bytes 393220
  54.5 2.7 %collective-permute-start.11 = (bf16[8,128,256]{2,1,0:T(8,128)(2,1)S(1)}, bf16[8,128,256]{2,1,0:T(8,128)(2,1)S(1)}, u32[]{:S(2)}, u32[]{:S(2)}) collective-permute-start(bf16[8,128,256]{2,1,0:T(8,128)(2,1)S(1)} %backward_blocks.5), channel_id=1, source_target_pairs={{0,1},{1,0},{2,3},{3,2},{4,5},{5,4},{6,7},{7,6},{8,9},{9,8},{10,11... | collective-permute-start | bytes 1572872 | tf_op jit(solution)/shard_map/ppermute | solution.py:269
  57.3 6.0 %collective-permute-start.21 = (bf16[1,128,256]{2,1,0:T(8,128)(2,1)S(1)}, bf16[1,128,256]{2,1,0:T(8,128)(2,1)S(1)}, u32[]{:S(2)}, u32[]{:S(2)}) collective-permute-start(bf16[1,128,256]{2,1,0:T(8,128)(2,1)S(1)} %dynamic-slice_bitcast_fusion), channel_id=1, source_target_pairs={{0,1},{1,0},{2,3},{3,2},{4,5},{5,4},{6,7},{7,6},{8,9},{9,8},{10,11... | collective-permute-start | bytes 196616 | tf_op jit(solution)/shard_map/ppermute | solution.py:269
  57.8 16.3 %collective-permute-start.14 = (bf16[8,128,256]{2,1,0:T(8,128)(2,1)S(1)}, bf16[8,128,256]{2,1,0:T(8,128)(2,1)S(1)}, u32[]{:S(2)}, u32[]{:S(2)}) collective-permute-start(bf16[8,128,256]{2,1,0:T(8,128)(2,1)S(1)} %add_convert_fusion.2), channel_id=1, source_target_pairs={{0,2},{1,3},{6,4},{7,5},{8,10},{9,11},{14,12},{15,13},{16,18},{17,... | collective-permute-start | bytes 1572872 | tf_op jit(solution)/shard_map/ppermute | solution.py:274
  62.6 15.7 %collective-permute-start.15 = (bf16[8,128,256]{2,1,0:T(8,128)(2,1)S(1)}, bf16[8,128,256]{2,1,0:T(8,128)(2,1)S(1)}, u32[]{:S(2)}, u32[]{:S(2)}) collective-permute-start(bf16[8,128,256]{2,1,0:T(8,128)(2,1)S(1)} %add_convert_fusion.2), channel_id=1, source_target_pairs={{2,4},{3,5},{4,2},{5,3},{10,12},{11,13},{12,10},{13,11},{18,20},{1... | collective-permute-start | bytes 1572872 | tf_op jit(solution)/shard_map/ppermute | solution.py:274
  63.4 7.1 %copy-start.9 = (bf16[2,32,128,128]{3,2,1,0:T(8,128)(2,1)S(1)}, bf16[2,32,128,128]{3,2,1,0:T(8,128)(2,1)}, u32[]{:S(2)}) copy-start(bf16[2,32,128,128]{3,2,1,0:T(8,128)(2,1)} %copy-done.7) | copy-start | bytes 6291460
  63.4 5.8 %collective-permute-start.22 = (bf16[1,128,256]{2,1,0:T(8,128)(2,1)S(1)}, bf16[1,128,256]{2,1,0:T(8,128)(2,1)S(1)}, u32[]{:S(2)}, u32[]{:S(2)}) collective-permute-start(bf16[1,128,256]{2,1,0:T(8,128)(2,1)S(1)} %fusion), channel_id=1, source_target_pairs={{0,8},{8,0},{16,24},{24,16},{1,9},{9,1},{17,25},{25,17},{2,10},{10... | collective-permute-start | bytes 196616 | tf_op jit(solution)/shard_map/ppermute | solution.py:277
  69.0 9.3 %collective-permute-start.13 = (bf16[8,128,256]{2,1,0:T(8,128)(2,1)S(1)}, bf16[8,128,256]{2,1,0:T(8,128)(2,1)S(1)}, u32[]{:S(2)}, u32[]{:S(2)}) collective-permute-start(bf16[8,128,256]{2,1,0:T(8,128)(2,1)S(1)} %get-tuple-element.41), channel_id=1, source_target_pairs={{0,1},{1,0},{2,3},{3,2},{4,5},{5,4},{6,7},{7,6},{8,9},{9,8},{10,11... | collective-permute-start | bytes 1572872 | tf_op jit(solution)/shard_map/ppermute | solution.py:269
  69.1 14.3 %collective-permute-start.12 = (bf16[8,128,256]{2,1,0:T(8,128)(2,1)S(1)}, bf16[8,128,256]{2,1,0:T(8,128)(2,1)S(1)}, u32[]{:S(2)}, u32[]{:S(2)}) collective-permute-start(bf16[8,128,256]{2,1,0:T(8,128)(2,1)S(1)} %pad_maximum_fusion), channel_id=1, source_target_pairs={{0,8},{8,0},{16,24},{24,16},{1,9},{9,1},{17,25},{25,17},{2,10},{10... | collective-permute-start | bytes 1572872 | tf_op jit(solution)/shard_map/ppermute | solution.py:277
  69.2 4.5 %collective-permute-start.23 = (bf16[1,128,256]{2,1,0:T(8,128)(2,1)S(1)}, bf16[1,128,256]{2,1,0:T(8,128)(2,1)S(1)}, u32[]{:S(2)}, u32[]{:S(2)}) collective-permute-start(bf16[1,128,256]{2,1,0:T(8,128)(2,1)S(1)} %add_convert_fusion.6), channel_id=1, source_target_pairs={{0,16},{8,24},{16,0},{24,8},{1,17},{9,25},{17,1},{25,9},{2,18},{10... | collective-permute-start | bytes 196616 | tf_op jit(solution)/shard_map/ppermute | solution.py:277
  73.7 13.8 %collective-permute-start.18 = (bf16[8,128,256]{2,1,0:T(8,128)(2,1)S(1)}, bf16[8,128,256]{2,1,0:T(8,128)(2,1)S(1)}, u32[]{:S(2)}, u32[]{:S(2)}) collective-permute-start(bf16[8,128,256]{2,1,0:T(8,128)(2,1)S(1)} %get-tuple-element.46), channel_id=1, source_target_pairs={{0,1},{1,0},{2,3},{3,2},{4,5},{5,4},{6,7},{7,6},{8,9},{9,8},{10,11... | collective-permute-start | bytes 1572872 | tf_op jit(solution)/shard_map/ppermute | solution.py:269
  74.2 10.6 %collective-permute-start.24 = (bf16[1,128,256]{2,1,0:T(8,128)(2,1)S(1)}, bf16[1,128,256]{2,1,0:T(8,128)(2,1)S(1)}, u32[]{:S(2)}, u32[]{:S(2)}) collective-permute-start(bf16[1,128,256]{2,1,0:T(8,128)(2,1)S(1)} %add_convert_fusion.5), channel_id=1, source_target_pairs={{0,4},{1,5},{2,6},{3,7},{4,0},{5,1},{6,2},{7,3},{8,12},{9,13},{10,... | collective-permute-start | bytes 196616 | tf_op jit(solution)/shard_map/ppermute | solution.py:274
  83.4 13.7 %copy-start.4 = (s32[4,1,16,1]{2,3,1,0:T(1,128)S(1)}, s32[4,1,16,1]{2,3,1,0:T(1,128)}, u32[]{:S(2)}) copy-start(s32[4,1,16,1]{2,3,1,0:T(1,128)} %param.22) | copy-start | bytes 772
  83.4 13.7 %copy-start.6 = (bf16[2,32,128,128]{3,2,1,0:T(8,128)(2,1)S(1)}, bf16[2,32,128,128]{3,2,1,0:T(8,128)(2,1)}, u32[]{:S(2)}) copy-start(bf16[2,32,128,128]{3,2,1,0:T(8,128)(2,1)} %copy-done.5) | copy-start | bytes 6291460
  83.5 13.7 %copy-start.14 = (bf16[1,1,16,128,128]{4,3,2,1,0:T(8,128)(2,1)S(1)}, bf16[1,1,16,128,128]{4,3,2,1,0:T(8,128)(2,1)}, u32[]{:S(2)}) copy-start(bf16[1,1,16,128,128]{4,3,2,1,0:T(8,128)(2,1)} %param.20) | copy-start | bytes 1572868
  83.5 13.7 %copy-start.16 = (s32[1,1,16]{2,1,0:T(1,128)S(1)}, s32[1,1,16]{2,1,0:T(1,128)}, u32[]{:S(2)}) copy-start(s32[1,1,16]{2,1,0:T(1,128)} %param.21) | copy-start | bytes 196
  83.5 13.6 %collective-permute-start.16 = (bf16[8,128,256]{2,1,0:T(8,128)(2,1)S(1)}, bf16[8,128,256]{2,1,0:T(8,128)(2,1)S(1)}, u32[]{:S(2)}, u32[]{:S(2)}) collective-permute-start(bf16[8,128,256]{2,1,0:T(8,128)(2,1)S(1)} %pad_maximum_fusion.1), channel_id=1, source_target_pairs={{0,16},{8,24},{16,0},{24,8},{1,17},{9,25},{17,1},{25,9},{2,18},{10... | collective-permute-start | bytes 1572872 | tf_op jit(solution)/shard_map/ppermute | solution.py:277
  84.8 16.0 %collective-permute-start.25 = (bf16[1,128,256]{2,1,0:T(8,128)(2,1)S(1)}, bf16[1,128,256]{2,1,0:T(8,128)(2,1)S(1)}, u32[]{:S(2)}, u32[]{:S(2)}) collective-permute-start(bf16[1,128,256]{2,1,0:T(8,128)(2,1)S(1)} %add_convert_fusion.4), channel_id=1, source_target_pairs={{0,2},{1,3},{2,0},{3,1},{4,6},{5,7},{6,4},{7,5},{8,10},{9,11},{10,... | collective-permute-start | bytes 196616 | tf_op jit(solution)/shard_map/ppermute | solution.py:274
  86.6 26.0 %collective-permute-start.17 = (bf16[8,128,256]{2,1,0:T(8,128)(2,1)}, bf16[8,128,256]{2,1,0:T(8,128)(2,1)S(1)}, u32[]{:S(2)}, u32[]{:S(2)}) collective-permute-start(bf16[8,128,256]{2,1,0:T(8,128)(2,1)} %add_convert_fusion.1), channel_id=1, source_target_pairs={{0,4},{1,5},{2,6},{3,7},{4,0},{5,1},{6,2},{7,3},{8,12},{9,13},{10,... | collective-permute-start | bytes 1572872 | tf_op jit(solution)/shard_map/ppermute | solution.py:274
  88.4 24.2 %collective-permute-start.19 = (bf16[8,128,256]{2,1,0:T(8,128)(2,1)}, bf16[8,128,256]{2,1,0:T(8,128)(2,1)S(1)}, u32[]{:S(2)}, u32[]{:S(2)}) collective-permute-start(bf16[8,128,256]{2,1,0:T(8,128)(2,1)} %add_convert_fusion), channel_id=1, source_target_pairs={{0,2},{1,3},{2,0},{3,1},{4,6},{5,7},{6,4},{7,5},{8,10},{9,11},{10,... | collective-permute-start | bytes 1572872 | tf_op jit(solution)/shard_map/ppermute | solution.py:274
  97.2 15.4 %copy-start.1 = (bf16[256,256]{1,0:T(8,128)(2,1)S(1)}, bf16[256,256]{1,0:T(8,128)(2,1)}, u32[]{:S(2)}) copy-start(bf16[256,256]{1,0:T(8,128)(2,1)} %refs_5_.1) | copy-start | bytes 393220
  100.8 11.8 %collective-permute-start.20 = (bf16[8,128,256]{2,1,0:T(8,128)(2,1)}, bf16[8,128,256]{2,1,0:T(8,128)(2,1)S(1)}, u32[]{:S(2)}, u32[]{:S(2)}) collective-permute-start(bf16[8,128,256]{2,1,0:T(8,128)(2,1)} %get-tuple-element.48), channel_id=1, source_target_pairs={{0,1},{1,0},{2,3},{3,2},{4,5},{5,4},{6,7},{7,6},{8,9},{9,8},{10,11... | collective-permute-start | bytes 1572872 | tf_op jit(solution)/shard_map/ppermute | solution.py:269
  101.5 1.7 %collective-permute-start.26 = (f32[1,128,256]{2,1,0:T(8,128)}, f32[1,128,256]{2,1,0:T(8,128)S(1)}, u32[]{:S(2)}, u32[]{:S(2)}) collective-permute-start(f32[1,128,256]{2,1,0:T(8,128)} %convert_multiply_fusion), channel_id=1, source_target_pairs={{0,1},{1,0},{2,3},{3,2},{4,5},{5,4},{6,7},{7,6},{8,9},{9,8},{10,11... | collective-permute-start | bytes 393224 | tf_op jit(solution)/shard_map/ppermute | solution.py:269

commit v4 on v3

--- a/solution.py
+++ b/solution.py
@@ -409,7 +409,6 @@
         from_ends = after(from_ends, middle, owns[1])
         far = (owns[2] + theirs[2].astype(F32) + from_ends.astype(F32)).astype(BF16)
         near = (owns[1] + theirs[1].astype(F32)).astype(BF16)
-        near = after(near, far)
         arrived = [middle, across(far, 2), across(near, 1)]
     else:
         arrived = [across(both, last)]
@@ -423,8 +422,8 @@
     while step < n_groups:
         chosen = [k for k in range(n_groups) if k & step]
         sent = jnp.concatenate([parts[k] for k in chosen])
-        if step == 1:
-            sent = after(sent, both)
+        if relay and step == 1:
+            sent = after(sent, theirs[2])
         elif relay and step == 2:
             sent = after(sent, far)
         moved_parts = group(sent, step)

time: 114 us -> 114 us (level); the launches traced: 114 us -> 112 us
  starting transfers between devices: 33.9 us -> 32.2 us
    ppermute x7, waiting for transfers between devices: 11.8 us -> 6.69 us  [group(): return lax.ppermute(value, 'grp', [(i, i ^ mask) for i in range(n_groups)])]
    ppermute x10, waiting for transfers between devices: 22.3 us -> 27.4 us  [across(): return lax.ppermute(value, 'blk', pairs)]
  transfers between devices with their start and end apart: 27 -> 27, of which waited for: 10 -> 9; matrix products, arithmetic and copies ran while one was open for 4% -> 4% of each run, Pallas kernels for 25% -> 25%
where the time goes in v4:
time: 114 us; the launch traced here: 112 us
  Pallas kernels  36.2 us (32%)
  waiting for transfers between devices  35.5 us (31%)
  starting transfers between devices  32.2 us (28%)
  other arithmetic  4.08 us (4%)
  local copies, waits for them, and re-layouts  3.16 us (3%)
  between operations  1.23 us (1%)
    ppermute x10, waiting for transfers between devices, across(): return lax.ppermute(value, 'blk', pairs)  27.4 us
    ppermute x10, starting transfers between devices, across(): return lax.ppermute(value, 'blk', pairs)  20.5 us
    pallas_call x4, Pallas kernels, forward(): call(functools.partial(forward_blocks, meta, mask, sides, acc is not None...  9.73 us
    ppermute x7, starting transfers between devices, group(): return lax.ppermute(value, 'grp', [(i, i ^ mask) for i in range(n_groups)])  9 us
    pallas_call x4, Pallas kernels, backward(): call(functools.partial(backward_blocks, meta, mask, sides), 'backward_blo...  7.38 us
    ppermute x7, waiting for transfers between devices, group(): return lax.ppermute(value, 'grp', [(i, i ^ mask) for i in range(n_groups)])  6.69 us
    pallas_call x1, Pallas kernels, local(): call(functools.partial(stage_tiles, meta), 'stage_tiles', (jax.ShapeDtype...  6.15 us
    pallas_call x1, Pallas kernels, local(): call(functools.partial(last_forward, meta, last), 'last_forward', (jax.Sh...  4.7 us
  transfers between devices with their start and end apart: 27, of which 9 were waited for; matrix products, arithmetic and copies ran while one was open for 4% of the time, Pallas kernels for 25%

profile of v4, /device:TPU:0, one launch (start us, length us, event | category | flops | bytes accessed | tf_op | source)
XLA Modules:
  0.0 112.4 jit_solution(12579431147029555545)
XLA Ops:
  0.6 0.5 collective-permute-start
  1.1 2.7 %collective-permute-start.4 = (bf16[8,128,256]{2,1,0:T(8,128)(2,1)}, bf16[8,128,256]{2,1,0:T(8,128)(2,1)}, u32[]{:S(2)}, u32[]{:S(2)}) collective-permute-start(bf16[8,128,256]{2,1,0:T(8,128)(2,1)} %bitcast.47), channel_id=1, source_target_pairs={{0,2},{1,3},{2,0},{3,1},{4,6},{5,7},{6,4},{7,5},{8,10},{9,11},{10,... | collective-permute-start | bytes 1572872 | tf_op jit(solution)/shard_map/ppermute | solution.py:274
  3.8 2.6 %collective-permute-start.6 = (bf16[8,128,256]{2,1,0:T(8,128)(2,1)}, bf16[8,128,256]{2,1,0:T(8,128)(2,1)}, u32[]{:S(2)}, u32[]{:S(2)}) collective-permute-start(bf16[8,128,256]{2,1,0:T(8,128)(2,1)} %bitcast.48), channel_id=1, source_target_pairs={{0,4},{1,5},{2,6},{3,7},{4,0},{5,1},{6,2},{7,3},{8,12},{9,13},{10,... | collective-permute-start | bytes 1572872 | tf_op jit(solution)/shard_map/ppermute | solution.py:274
  6.4 0.1 pad_add_fusion.pos
  6.5 0.0 copy-start.3
  6.5 6.1 %stage_tiles.1 = (bf16[2,32,128,128]{3,2,1,0:T(8,128)(2,1)S(1)}, bf16[2,32,128,128]{3,2,1,0:T(8,128)(2,1)S(1)}, bf16[2,32,128,128]{3,2,1,0:T(8,128)(2,1)}, bf16[2,32,128,128]{3,2,1,0:T(8,128)(2,1)}) custom-call(s32[3]{0:T(128)S(1)} %pad_add_fusion.pos, bf16[8,32,128,128]{3,2,1,0:T(8,128)(2,1)} %bitcast.56), custom_call_target="tpu_custom_call" | custom-call | flops 1 | bytes 419430400 | tf_op jit(solution)/shard_map/stage_tiles/pallas_call | solution.py:282
  12.7 1.3 %copy-done.7 = bf16[2,32,128,128]{3,2,1,0:T(8,128)(2,1)} copy-done((bf16[2,32,128,128]{3,2,1,0:T(8,128)(2,1)}, bf16[2,32,128,128]{3,2,1,0:T(8,128)(2,1)S(1)}, u32[]{:S(2)}) %copy-start.7) | copy-done | bytes 2097176
  14.0 0.1 reshape.58
  14.1 0.1 reshape.59
  14.2 0.1 concatenate.13.ints
  14.3 0.2 broadcast_select_fusion
  14.6 1.2 %copy-done.13 = bf16[1,1,16,128,128]{4,3,2,1,0:T(8,128)(2,1)S(1)} copy-done((bf16[1,1,16,128,128]{4,3,2,1,0:T(8,128)(2,1)S(1)}, bf16[1,1,16,128,128]{4,3,2,1,0:T(8,128)(2,1)}, u32[]{:S(2)}) %copy-start.13) | copy-done | bytes 524312
  15.8 1.0 hub_products.1
  16.8 0.1 slice_bitcast_fusion
  16.9 1.6 %collective-permute-start.1 = (bf16[4,128,256]{2,1,0:T(8,128)(2,1)S(1)}, bf16[4,128,256]{2,1,0:T(8,128)(2,1)S(1)}, u32[]{:S(2)}, u32[]{:S(2)}) collective-permute-start(bf16[4,128,256]{2,1,0:T(8,128)(2,1)S(1)} %get-tuple-element.55), channel_id=1, source_target_pairs={{0,8},{8,0},{16,24},{24,16},{1,9},{9,1},{17,25},{25,17},{2,10},{10... | collective-permute-start | bytes 786440 | tf_op jit(solution)/shard_map/ppermute | solution.py:277
  18.5 1.5 %collective-permute-start.2 = (bf16[4,128,256]{2,1,0:T(8,128)(2,1)S(1)}, bf16[4,128,256]{2,1,0:T(8,128)(2,1)S(1)}, u32[]{:S(2)}, u32[]{:S(2)}) collective-permute-start(bf16[4,128,256]{2,1,0:T(8,128)(2,1)S(1)} %get-tuple-element.54), channel_id=1, source_target_pairs={{0,16},{8,24},{16,0},{24,8},{1,17},{9,25},{17,1},{25,9},{2,18},{10... | collective-permute-start | bytes 786440 | tf_op jit(solution)/shard_map/ppermute | solution.py:277
  20.0 0.5 collective-permute-start.3
  20.5 7.3 %collective-permute-done.4.refs_2_ = bf16[8,128,256]{2,1,0:T(8,128)(2,1)} collective-permute-done((bf16[8,128,256]{2,1,0:T(8,128)(2,1)}, bf16[8,128,256]{2,1,0:T(8,128)(2,1)}, u32[]{:S(2)}, u32[]{:S(2)}) %collective-permute-start.4) | collective-permute-done | bytes 524320 | tf_op jit(solution)/shard_map/ppermute | solution.py:274
  27.7 3.1 %forward_blocks.4.refs_0_ = f32[8,128,256]{2,1,0:T(8,128)S(1)} custom-call(s32[523]{0:T(1024)S(1)} %concatenate.13.ints, bf16[8,128,256]{2,1,0:T(8,128)(2,1)} %collective-permute-done.refs_0_, bf16[8,128,256]{2,1,0:T(8,128)(2,1)S(1)} %bitcast.50, bf16[2,32,128,128]{3,2,1,0:T(8,128)(2,1)S(1)} %get-tuple-element.26.refs_2_.tiles), custom_call_target="tpu_custom_call" | custom-call | flops 53687091200 | bytes 419430400 | tf_op jit(solution)/shard_map/forward_blocks/pallas_call | solution.py:295
  30.9 1.4 %collective-permute-start.8 = (bf16[8,128,256]{2,1,0:T(8,128)(2,1)}, bf16[8,128,256]{2,1,0:T(8,128)(2,1)S(1)}, u32[]{:S(2)}, u32[]{:S(2)}) collective-permute-start(bf16[8,128,256]{2,1,0:T(8,128)(2,1)} %collective-permute-done.6.refs_2_), channel_id=1, source_target_pairs={{2,0},{3,1},{4,6},{5,7},{10,8},{11,9},{12,14},{13,15},{18,16},{19,... | collective-permute-start | bytes 1572872 | tf_op jit(solution)/shard_map/ppermute | solution.py:274
  32.3 0.7 collective-permute-start.9
  33.0 0.1 collective-permute-start.7
  33.1 1.9 %hub_add.1.refs_0_ = f32[8,128,256]{2,1,0:T(8,128)S(1)} custom-call(s32[3]{0:T(128)S(1)} %pad_add_fusion.pos, s32[4,16]{1,0:T(4,128)S(1)} %bitcast.43, s32[4,16]{1,0:T(4,128)S(1)} %bitcast.40, f32[8,128,256]{2,1,0:T(8,128)S(1)} %forward_blocks.4.refs_0_, bf16[4,128,256]{2,1,0:T(8,128)(2,1)S(1)} %get-tuple-element.56.refs_1_, ...), custom_call_target="tpu_custom_call" | custom-call | flops 1048576 | bytes 419430400 | tf_op jit(solution)/shard_map/hub_add/pallas_call | solution.py:348
  35.1 2.7 %forward_blocks.5.refs_0_ = f32[8,128,256]{2,1,0:T(8,128)S(1)} custom-call(s32[523]{0:T(1024)S(1)} %concatenate.13.ints, f32[8,128,256]{2,1,0:T(8,128)S(1)} %hub_add.1.refs_0_, bf16[8,128,256]{2,1,0:T(8,128)(2,1)S(1)} %collective-permute-done.5.refs_1_, bf16[8,128,256]{2,1,0:T(8,128)(2,1)} %collective-permute-done.4.refs_2_, ...), custom_call_target="tpu_custom_call" | custom-call | flops 53687091200 | bytes 419430400 | tf_op jit(solution)/shard_map/forward_blocks/pallas_call | solution.py:295
  37.9 2.3 %forward_blocks.6.refs_0_ = f32[8,128,256]{2,1,0:T(8,128)S(1)} custom-call(s32[523]{0:T(1024)S(1)} %concatenate.13.ints, f32[8,128,256]{2,1,0:T(8,128)S(1)} %forward_blocks.5.refs_0_, bf16[8,128,256]{2,1,0:T(8,128)(2,1)S(1)} %collective-permute-done.7.refs_1_, bf16[8,128,256]{2,1,0:T(8,128)(2,1)} %collective-permute-done.6.refs_2_, ...), custom_call_target="tpu_custom_call" | custom-call | flops 53687091200 | bytes 419430400 | tf_op jit(solution)/shard_map/forward_blocks/pallas_call | solution.py:295
  40.2 6.4 %collective-permute-done.8 = bf16[8,128,256]{2,1,0:T(8,128)(2,1)S(1)} collective-permute-done((bf16[8,128,256]{2,1,0:T(8,128)(2,1)}, bf16[8,128,256]{2,1,0:T(8,128)(2,1)S(1)}, u32[]{:S(2)}, u32[]{:S(2)}) %collective-permute-start.8) | collective-permute-done | bytes 524320 | tf_op jit(solution)/shard_map/ppermute | solution.py:274
  46.5 0.1 add.44.refs_1_
  46.7 0.1 collective-permute-start.10
  46.8 1.6 %forward_blocks.7.acc = f32[8,128,256]{2,1,0:T(8,128)S(1)} custom-call(s32[523]{0:T(1024)S(1)} %concatenate.13.ints, f32[8,128,256]{2,1,0:T(8,128)S(1)} %forward_blocks.6.refs_0_, bf16[8,128,256]{2,1,0:T(8,128)(2,1)S(1)} %add.44.refs_1_, bf16[2,32,128,128]{3,2,1,0:T(8,128)(2,1)S(1)} %copy-done.11), custom_call_target="tpu_custom_call" | custom-call | flops 26843545600 | bytes 419430400 | tf_op jit(solution)/shard_map/forward_blocks/pallas_call | solution.py:295
  48.4 0.2 collective-permute-done.10.refs_0_
  48.6 4.7 %last_forward.1 = (bf16[8,128,256]{2,1,0:T(8,128)(2,1)}, bf16[8,128,256]{2,1,0:T(8,128)(2,1)S(1)}, bf16[4,4,128,256]{3,2,1,0:T(8,128)(2,1)S(1)}, f32[256,256]{1,0:T(8,128)S(1)}) custom-call(s32[523]{0:T(1024)S(1)} %concatenate.13.ints, s32[4,16]{1,0:T(4,128)S(1)} %bitcast.44, s32[4,16]{1,0:T(4,128)S(1)} %bitcast.41, f32[8,128,256]{2,1,0:T(8,128)S(1)} %forward_blocks.7.acc, ...), custom_call_target="tpu_custom_call" | custom-call | flops 26843545600 | bytes 419430400 | tf_op jit(solution)/shard_map/last_forward/pallas_call | solution.py:367
  53.3 1.6 %backward_blocks.5 = bf16[8,128,256]{2,1,0:T(8,128)(2,1)S(1)} custom-call(s32[523]{0:T(1024)S(1)} %concatenate.13.ints, bf16[8,128,256]{2,1,0:T(8,128)(2,1)S(1)} %get-tuple-element.36.grad, bf16[2,32,128,128]{3,2,1,0:T(8,128)(2,1)S(1)} %copy-done.11), custom_call_target="tpu_custom_call" | custom-call | flops 26843545600 | bytes 419430400 | tf_op jit(solution)/shard_map/backward_blocks/pallas_call | solution.py:310
  55.0 0.3 collective-permute-start.11
  55.3 1.7 %backward_blocks.4 = f32[8,128,256]{2,1,0:T(8,128)S(1)} custom-call(s32[523]{0:T(1024)S(1)} %concatenate.13.ints, bf16[8,128,256]{2,1,0:T(8,128)(2,1)S(1)} %get-tuple-element.36.grad, bf16[2,32,128,128]{3,2,1,0:T(8,128)(2,1)S(1)} %copy-done.11), custom_call_target="tpu_custom_call" | custom-call | flops 26843545600 | bytes 419430400 | tf_op jit(solution)/shard_map/backward_blocks/pallas_call | solution.py:310
  57.0 0.1 slice_bitcast_fusion.4
  57.1 0.1 add_convert_fusion.2
  57.3 0.3 collective-permute-start.21
  57.6 1.8 %backward_blocks.6 = (bf16[8,128,256]{2,1,0:T(8,128)(2,1)S(1)}, f32[8,128,256]{2,1,0:T(8,128)S(1)}) custom-call(s32[523]{0:T(1024)S(1)} %concatenate.13.ints, bf16[8,128,256]{2,1,0:T(8,128)(2,1)S(1)} %get-tuple-element.36.grad, bf16[2,32,128,128]{3,2,1,0:T(8,128)(2,1)S(1)} %copy-done.10), custom_call_target="tpu_custom_call" | custom-call | flops 53687091200 | bytes 419430400 | tf_op jit(solution)/shard_map/backward_blocks/pallas_call | solution.py:310
  59.4 0.8 collective-permute-start.12
  60.2 2.4 %collective-permute-start.22 = (bf16[1,128,256]{2,1,0:T(8,128)(2,1)S(1)}, bf16[1,128,256]{2,1,0:T(8,128)(2,1)S(1)}, u32[]{:S(2)}, u32[]{:S(2)}) collective-permute-start(bf16[1,128,256]{2,1,0:T(8,128)(2,1)S(1)} %fusion), channel_id=1, source_target_pairs={{0,8},{8,0},{16,24},{24,16},{1,9},{9,1},{17,25},{25,17},{2,10},{10... | collective-permute-start | bytes 196616 | tf_op jit(solution)/shard_map/ppermute | solution.py:277
  62.7 4.7 %collective-permute-start.14 = (bf16[8,128,256]{2,1,0:T(8,128)(2,1)S(1)}, bf16[8,128,256]{2,1,0:T(8,128)(2,1)S(1)}, u32[]{:S(2)}, u32[]{:S(2)}) collective-permute-start(bf16[8,128,256]{2,1,0:T(8,128)(2,1)S(1)} %add_convert_fusion.2), channel_id=1, source_target_pairs={{0,2},{1,3},{6,4},{7,5},{8,10},{9,11},{14,12},{15,13},{16,18},{17,... | collective-permute-start | bytes 1572872 | tf_op jit(solution)/shard_map/ppermute | solution.py:274
  67.4 0.7 collective-permute-start.15
  68.2 2.1 %collective-permute-start.23 = (bf16[1,128,256]{2,1,0:T(8,128)(2,1)S(1)}, bf16[1,128,256]{2,1,0:T(8,128)(2,1)S(1)}, u32[]{:S(2)}, u32[]{:S(2)}) collective-permute-start(bf16[1,128,256]{2,1,0:T(8,128)(2,1)S(1)} %add_convert_fusion.6), channel_id=1, source_target_pairs={{0,16},{8,24},{16,0},{24,8},{1,17},{9,25},{17,1},{25,9},{2,18},{10... | collective-permute-start | bytes 196616 | tf_op jit(solution)/shard_map/ppermute | solution.py:277
  70.2 0.5 collective-permute-start.13
  70.7 2.3 %backward_blocks.7 = (bf16[8,128,256]{2,1,0:T(8,128)(2,1)S(1)}, f32[8,128,256]{2,1,0:T(8,128)S(1)}) custom-call(s32[523]{0:T(1024)S(1)} %concatenate.13.ints, bf16[8,128,256]{2,1,0:T(8,128)(2,1)S(1)} %get-tuple-element.36.grad, bf16[2,32,128,128]{3,2,1,0:T(8,128)(2,1)S(1)} %copy-done.9), custom_call_target="tpu_custom_call" | custom-call | flops 53687091200 | bytes 419430400 | tf_op jit(solution)/shard_map/backward_blocks/pallas_call | solution.py:310
  73.0 0.1 collective-permute-start.18
  73.1 2.2 %collective-permute-start.24 = (bf16[1,128,256]{2,1,0:T(8,128)(2,1)S(1)}, bf16[1,128,256]{2,1,0:T(8,128)(2,1)S(1)}, u32[]{:S(2)}, u32[]{:S(2)}) collective-permute-start(bf16[1,128,256]{2,1,0:T(8,128)(2,1)S(1)} %add_convert_fusion.5), channel_id=1, source_target_pairs={{0,4},{1,5},{2,6},{3,7},{4,0},{5,1},{6,2},{7,3},{8,12},{9,13},{10,... | collective-permute-start | bytes 196616 | tf_op jit(solution)/shard_map/ppermute | solution.py:274
  75.3 4.4 %collective-permute-done.14 = bf16[8,128,256]{2,1,0:T(8,128)(2,1)S(1)} collective-permute-done((bf16[8,128,256]{2,1,0:T(8,128)(2,1)S(1)}, bf16[8,128,256]{2,1,0:T(8,128)(2,1)S(1)}, u32[]{:S(2)}, u32[]{:S(2)}) %collective-permute-start.14) | collective-permute-done | bytes 524320 | tf_op jit(solution)/shard_map/ppermute | solution.py:274
  79.7 1.0 add_convert_fusion.1
  80.6 2.7 %collective-permute-done.13 = bf16[8,128,256]{2,1,0:T(8,128)(2,1)S(1)} collective-permute-done((bf16[8,128,256]{2,1,0:T(8,128)(2,1)S(1)}, bf16[8,128,256]{2,1,0:T(8,128)(2,1)S(1)}, u32[]{:S(2)}, u32[]{:S(2)}) %collective-permute-start.13) | collective-permute-done | bytes 524320 | tf_op jit(solution)/shard_map/ppermute | solution.py:277
  83.5 0.5 collective-permute-start.16
  83.9 1.3 %collective-permute-done.24 = bf16[1,128,256]{2,1,0:T(8,128)(2,1)S(1)} collective-permute-done((bf16[1,128,256]{2,1,0:T(8,128)(2,1)S(1)}, bf16[1,128,256]{2,1,0:T(8,128)(2,1)S(1)}, u32[]{:S(2)}, u32[]{:S(2)}) %collective-permute-start.24) | collective-permute-done | bytes 65568 | tf_op jit(solution)/shard_map/ppermute | solution.py:274
  85.2 2.5 %collective-permute-start.25 = (bf16[1,128,256]{2,1,0:T(8,128)(2,1)S(1)}, bf16[1,128,256]{2,1,0:T(8,128)(2,1)S(1)}, u32[]{:S(2)}, u32[]{:S(2)}) collective-permute-start(bf16[1,128,256]{2,1,0:T(8,128)(2,1)S(1)} %add_convert_fusion.4), channel_id=1, source_target_pairs={{0,2},{1,3},{2,0},{3,1},{4,6},{5,7},{6,4},{7,5},{8,10},{9,11},{10,... | collective-permute-start | bytes 196616 | tf_op jit(solution)/shard_map/ppermute | solution.py:274
  87.7 1.1 %collective-permute-start.17 = (bf16[8,128,256]{2,1,0:T(8,128)(2,1)}, bf16[8,128,256]{2,1,0:T(8,128)(2,1)S(1)}, u32[]{:S(2)}, u32[]{:S(2)}) collective-permute-start(bf16[8,128,256]{2,1,0:T(8,128)(2,1)} %add_convert_fusion.1), channel_id=1, source_target_pairs={{0,4},{1,5},{2,6},{3,7},{4,0},{5,1},{6,2},{7,3},{8,12},{9,13},{10,... | collective-permute-start | bytes 1572872 | tf_op jit(solution)/shard_map/ppermute | solution.py:274
  88.9 1.0 add_convert_fusion
  89.8 1.9 %collective-permute-start.19 = (bf16[8,128,256]{2,1,0:T(8,128)(2,1)}, bf16[8,128,256]{2,1,0:T(8,128)(2,1)S(1)}, u32[]{:S(2)}, u32[]{:S(2)}) collective-permute-start(bf16[8,128,256]{2,1,0:T(8,128)(2,1)} %add_convert_fusion), channel_id=1, source_target_pairs={{0,2},{1,3},{2,0},{3,1},{4,6},{5,7},{6,4},{7,5},{8,10},{9,11},{10,... | collective-permute-start | bytes 1572872 | tf_op jit(solution)/shard_map/ppermute | solution.py:274
  91.8 4.0 %collective-permute-done.16 = bf16[8,128,256]{2,1,0:T(8,128)(2,1)S(1)} collective-permute-done((bf16[8,128,256]{2,1,0:T(8,128)(2,1)S(1)}, bf16[8,128,256]{2,1,0:T(8,128)(2,1)S(1)}, u32[]{:S(2)}, u32[]{:S(2)}) %collective-permute-start.16) | collective-permute-done | bytes 524320 | tf_op jit(solution)/shard_map/ppermute | solution.py:277
  95.8 4.1 %last_products.1 = (bf16[8,128,256]{2,1,0:T(8,128)(2,1)}, f32[8,128,256]{2,1,0:T(8,128)S(1)}) custom-call(s32[523]{0:T(1024)S(1)} %concatenate.13.ints, s32[4,16]{1,0:T(4,128)S(1)} %bitcast.45, s32[16]{0:T(128)S(1)} %bitcast.55, bf16[8,128,256]{2,1,0:T(8,128)(2,1)S(1)} %get-tuple-element.36.grad, bf16[2,32,128,128]{3,2,1,0:T(8,128)(2,1)S(1)} %copy-done.6, ...), custom_call_target="tpu_custom_call" | custom-call | flops 13421772800 | bytes 419430400 | tf_op jit(solution)/shard_map/last_products/pallas_call | solution.py:433
  99.9 0.7 convert_multiply_fusion
  100.6 0.5 collective-permute-start.26
  101.1 1.2 %collective-permute-done.26 = f32[1,128,256]{2,1,0:T(8,128)S(1)} collective-permute-done((f32[1,128,256]{2,1,0:T(8,128)}, f32[1,128,256]{2,1,0:T(8,128)S(1)}, u32[]{:S(2)}, u32[]{:S(2)}) %collective-permute-start.26) | collective-permute-done | bytes 131104 | tf_op jit(solution)/shard_map/ppermute | solution.py:269
  102.3 0.7 pad_maximum_fusion.2
  103.0 8.1 %collective-permute-done.19.refs_3_ = bf16[8,128,256]{2,1,0:T(8,128)(2,1)S(1)} collective-permute-done((bf16[8,128,256]{2,1,0:T(8,128)(2,1)}, bf16[8,128,256]{2,1,0:T(8,128)(2,1)S(1)}, u32[]{:S(2)}, u32[]{:S(2)}) %collective-permute-start.19) | collective-permute-done | bytes 524320 | tf_op jit(solution)/shard_map/ppermute | solution.py:274
  111.2 1.2 %last_backward.1 = bf16[1024,256]{1,0:T(8,128)(2,1)} custom-call(f32[8,128,256]{2,1,0:T(8,128)S(1)} %get-tuple-element.44.refs_0_, bf16[8,128,256]{2,1,0:T(8,128)(2,1)S(1)} %collective-permute-done.15.refs_1_, bf16[8,128,256]{2,1,0:T(8,128)(2,1)S(1)} %collective-permute-done.17.refs_2_, bf16[8,128,256]{2,1,0:T(8,128)(2,1)S(1)} %collective-permute-done.19.refs_3_, ...), custom_call_target="tpu_custom_call" | custom-call | flops 419430400 | bytes 419430400 | tf_op jit(solution)/shard_map/last_backward/pallas_call | solution.py:455
  (73 shorter events, 0.5 us)
Async XLA Ops:
  0.6 13.9 %collective-permute-start = (bf16[8,128,256]{2,1,0:T(8,128)(2,1)}, bf16[8,128,256]{2,1,0:T(8,128)(2,1)}, u32[]{:S(2)}, u32[]{:S(2)}) collective-permute-start(bf16[8,128,256]{2,1,0:T(8,128)(2,1)} %bitcast.46), channel_id=1, source_target_pairs={{0,1},{1,0},{2,3},{3,2},{4,5},{5,4},{6,7},{7,6},{8,9},{9,8},{10,11... | collective-permute-start | bytes 1572872 | tf_op jit(solution)/shard_map/ppermute | solution.py:269
  1.1 26.6 %collective-permute-start.4 = (bf16[8,128,256]{2,1,0:T(8,128)(2,1)}, bf16[8,128,256]{2,1,0:T(8,128)(2,1)}, u32[]{:S(2)}, u32[]{:S(2)}) collective-permute-start(bf16[8,128,256]{2,1,0:T(8,128)(2,1)} %bitcast.47), channel_id=1, source_target_pairs={{0,2},{1,3},{2,0},{3,1},{4,6},{5,7},{6,4},{7,5},{8,10},{9,11},{10,... | collective-permute-start | bytes 1572872 | tf_op jit(solution)/shard_map/ppermute | solution.py:274
  3.8 27.0 %collective-permute-start.6 = (bf16[8,128,256]{2,1,0:T(8,128)(2,1)}, bf16[8,128,256]{2,1,0:T(8,128)(2,1)}, u32[]{:S(2)}, u32[]{:S(2)}) collective-permute-start(bf16[8,128,256]{2,1,0:T(8,128)(2,1)} %bitcast.48), channel_id=1, source_target_pairs={{0,4},{1,5},{2,6},{3,7},{4,0},{5,1},{6,2},{7,3},{8,12},{9,13},{10,... | collective-permute-start | bytes 1572872 | tf_op jit(solution)/shard_map/ppermute | solution.py:274
  6.5 7.6 %copy-start.18 = (s32[1,1,8,32]{3,2,1,0:T(8,128)S(1)}, s32[1,1,8,32]{3,2,1,0:T(8,128)}, u32[]{:S(2)}) copy-start(s32[1,1,8,32]{3,2,1,0:T(8,128)} %param.17) | copy-start | bytes 3076
  6.5 7.7 %copy-start.19 = (s32[1,1,8,32]{3,2,1,0:T(8,128)S(1)}, s32[1,1,8,32]{3,2,1,0:T(8,128)}, u32[]{:S(2)}) copy-start(s32[1,1,8,32]{3,2,1,0:T(8,128)} %param.18) | copy-start | bytes 3076
  6.5 7.7 %copy-start.21 = (s32[1,1,8]{2,1,0:T(1,128)S(1)}, s32[1,1,8]{2,1,0:T(1,128)}, u32[]{:S(2)}) copy-start(s32[1,1,8]{2,1,0:T(1,128)} %param.19) | copy-start | bytes 100
  6.5 7.8 %copy-start.20 = (s32[1024]{0:T(1024)S(1)}, s32[1024]{0:T(1024)}, u32[]{:S(2)}) copy-start(s32[1024]{0:T(1024)} %param.15) | copy-start | bytes 12292
  6.5 7.8 %copy-start.17 = (bf16[1024,256]{1,0:T(8,128)(2,1)S(1)}, bf16[1024,256]{1,0:T(8,128)(2,1)}, u32[]{:S(2)}) copy-start(bf16[1024,256]{1,0:T(8,128)(2,1)} %param.14) | copy-start | bytes 1572868
  6.5 8.0 %copy-start.3 = (s32[4,1,16,1]{2,3,1,0:T(1,128)S(1)}, s32[4,1,16,1]{2,3,1,0:T(1,128)}, u32[]{:S(2)}) copy-start(s32[4,1,16,1]{2,3,1,0:T(1,128)} %param.22) | copy-start | bytes 772
  6.5 8.0 %copy-start.12 = (bf16[1024,256]{1,0:T(8,128)(2,1)S(1)}, bf16[1024,256]{1,0:T(8,128)(2,1)}, u32[]{:S(2)}) copy-start(bf16[1024,256]{1,0:T(8,128)(2,1)} %param.12) | copy-start | bytes 1572868
  6.5 8.0 %copy-start.15 = (s32[1,1,16]{2,1,0:T(1,128)S(1)}, s32[1,1,16]{2,1,0:T(1,128)}, u32[]{:S(2)}) copy-start(s32[1,1,16]{2,1,0:T(1,128)} %param.21) | copy-start | bytes 196
  12.7 1.4 %copy-start.7 = (bf16[2,32,128,128]{3,2,1,0:T(8,128)(2,1)}, bf16[2,32,128,128]{3,2,1,0:T(8,128)(2,1)S(1)}, u32[]{:S(2)}) copy-start(bf16[2,32,128,128]{3,2,1,0:T(8,128)(2,1)S(1)} %get-tuple-element.28.refs_3_.tiles) | copy-start | bytes 6291460
  14.0 13.7 %copy-start.5 = (bf16[2,32,128,128]{3,2,1,0:T(8,128)(2,1)}, bf16[2,32,128,128]{3,2,1,0:T(8,128)(2,1)S(1)}, u32[]{:S(2)}) copy-start(bf16[2,32,128,128]{3,2,1,0:T(8,128)(2,1)S(1)} %get-tuple-element.26.refs_2_.tiles) | copy-start | bytes 6291460
  14.6 1.2 %copy-start.13 = (bf16[1,1,16,128,128]{4,3,2,1,0:T(8,128)(2,1)S(1)}, bf16[1,1,16,128,128]{4,3,2,1,0:T(8,128)(2,1)}, u32[]{:S(2)}) copy-start(bf16[1,1,16,128,128]{4,3,2,1,0:T(8,128)(2,1)} %param.20) | copy-start | bytes 1572868
  16.9 15.4 %collective-permute-start.1 = (bf16[4,128,256]{2,1,0:T(8,128)(2,1)S(1)}, bf16[4,128,256]{2,1,0:T(8,128)(2,1)S(1)}, u32[]{:S(2)}, u32[]{:S(2)}) collective-permute-start(bf16[4,128,256]{2,1,0:T(8,128)(2,1)S(1)} %get-tuple-element.55), channel_id=1, source_target_pairs={{0,8},{8,0},{16,24},{24,16},{1,9},{9,1},{17,25},{25,17},{2,10},{10... | collective-permute-start | bytes 786440 | tf_op jit(solution)/shard_map/ppermute | solution.py:277
  18.5 14.5 %collective-permute-start.2 = (bf16[4,128,256]{2,1,0:T(8,128)(2,1)S(1)}, bf16[4,128,256]{2,1,0:T(8,128)(2,1)S(1)}, u32[]{:S(2)}, u32[]{:S(2)}) collective-permute-start(bf16[4,128,256]{2,1,0:T(8,128)(2,1)S(1)} %get-tuple-element.54), channel_id=1, source_target_pairs={{0,16},{8,24},{16,0},{24,8},{1,17},{9,25},{17,1},{25,9},{2,18},{10... | collective-permute-start | bytes 786440 | tf_op jit(solution)/shard_map/ppermute | solution.py:277
  20.0 13.1 %collective-permute-start.3 = (bf16[4,128,256]{2,1,0:T(8,128)(2,1)S(1)}, bf16[4,128,256]{2,1,0:T(8,128)(2,1)S(1)}, u32[]{:S(2)}, u32[]{:S(2)}) collective-permute-start(bf16[4,128,256]{2,1,0:T(8,128)(2,1)S(1)} %get-tuple-element.53), channel_id=1, source_target_pairs={{0,24},{8,16},{16,8},{24,0},{1,25},{9,17},{17,9},{25,1},{2,26},{10... | collective-permute-start | bytes 786440 | tf_op jit(solution)/shard_map/ppermute | solution.py:277
  27.7 7.3 %collective-permute-start.5 = (bf16[8,128,256]{2,1,0:T(8,128)(2,1)}, bf16[8,128,256]{2,1,0:T(8,128)(2,1)S(1)}, u32[]{:S(2)}, u32[]{:S(2)}) collective-permute-start(bf16[8,128,256]{2,1,0:T(8,128)(2,1)} %collective-permute-done.4.refs_2_), channel_id=1, source_target_pairs={{0,1},{1,0},{2,3},{3,2},{4,5},{5,4},{6,7},{7,6},{8,9},{9,8},{10,11... | collective-permute-start | bytes 1572872 | tf_op jit(solution)/shard_map/ppermute | solution.py:269
  27.7 5.4 %copy-start.2 = (s32[4,1,16]{2,1,0:T(1,128)S(1)}, s32[4,1,16]{2,1,0:T(1,128)}, u32[]{:S(2)}) copy-start(s32[4,1,16]{2,1,0:T(1,128)} %param.23) | copy-start | bytes 772
  30.8 4.2 %copy-start.8 = (bf16[2,32,128,128]{3,2,1,0:T(8,128)(2,1)S(1)}, bf16[2,32,128,128]{3,2,1,0:T(8,128)(2,1)}, u32[]{:S(2)}) copy-start(bf16[2,32,128,128]{3,2,1,0:T(8,128)(2,1)} %copy-done.7) | copy-start | bytes 6291460
  30.9 15.7 %collective-permute-start.8 = (bf16[8,128,256]{2,1,0:T(8,128)(2,1)}, bf16[8,128,256]{2,1,0:T(8,128)(2,1)S(1)}, u32[]{:S(2)}, u32[]{:S(2)}) collective-permute-start(bf16[8,128,256]{2,1,0:T(8,128)(2,1)} %collective-permute-done.6.refs_2_), channel_id=1, source_target_pairs={{2,0},{3,1},{4,6},{5,7},{10,8},{11,9},{12,14},{13,15},{18,16},{19,... | collective-permute-start | bytes 1572872 | tf_op jit(solution)/shard_map/ppermute | solution.py:274
  32.3 14.2 %collective-permute-start.9 = (bf16[8,128,256]{2,1,0:T(8,128)(2,1)S(1)}, bf16[8,128,256]{2,1,0:T(8,128)(2,1)S(1)}, u32[]{:S(2)}, u32[]{:S(2)}) collective-permute-start(bf16[8,128,256]{2,1,0:T(8,128)(2,1)S(1)} %bitcast.51), channel_id=1, source_target_pairs={{2,4},{3,5},{4,2},{5,3},{10,12},{11,13},{12,10},{13,11},{18,20},{1... | collective-permute-start | bytes 1572872 | tf_op jit(solution)/shard_map/ppermute | solution.py:274
  33.0 4.8 %collective-permute-start.7 = (bf16[8,128,256]{2,1,0:T(8,128)(2,1)}, bf16[8,128,256]{2,1,0:T(8,128)(2,1)S(1)}, u32[]{:S(2)}, u32[]{:S(2)}) collective-permute-start(bf16[8,128,256]{2,1,0:T(8,128)(2,1)} %collective-permute-done.6.refs_2_), channel_id=1, source_target_pairs={{0,1},{1,0},{2,3},{3,2},{4,5},{5,4},{6,7},{7,6},{8,9},{9,8},{10,11... | collective-permute-start | bytes 1572872 | tf_op jit(solution)/shard_map/ppermute | solution.py:269
  35.1 2.8 %copy-start.10 = (bf16[2,32,128,128]{3,2,1,0:T(8,128)(2,1)S(1)}, bf16[2,32,128,128]{3,2,1,0:T(8,128)(2,1)}, u32[]{:S(2)}) copy-start(bf16[2,32,128,128]{3,2,1,0:T(8,128)(2,1)} %get-tuple-element.29.refs_3_.tiles) | copy-start | bytes 6291460
  37.9 8.9 %copy-start.11 = (bf16[2,32,128,128]{3,2,1,0:T(8,128)(2,1)S(1)}, bf16[2,32,128,128]{3,2,1,0:T(8,128)(2,1)}, u32[]{:S(2)}) copy-start(bf16[2,32,128,128]{3,2,1,0:T(8,128)(2,1)} %get-tuple-element.33.refs_2_.tiles) | copy-start | bytes 6291460
  46.7 2.0 %collective-permute-start.10 = (bf16[8,128,256]{2,1,0:T(8,128)(2,1)S(1)}, bf16[8,128,256]{2,1,0:T(8,128)(2,1)S(1)}, u32[]{:S(2)}, u32[]{:S(2)}) collective-permute-start(bf16[8,128,256]{2,1,0:T(8,128)(2,1)S(1)} %add.44.refs_1_), channel_id=1, source_target_pairs={{0,1},{1,0},{2,3},{3,2},{4,5},{5,4},{6,7},{7,6},{8,9},{9,8},{10,11... | collective-permute-start | bytes 1572872 | tf_op jit(solution)/shard_map/ppermute | solution.py:269
  46.7 1.9 %copy-start = (bf16[256,256]{1,0:T(8,128)(2,1)S(1)}, bf16[256,256]{1,0:T(8,128)(2,1)}, u32[]{:S(2)}) copy-start(bf16[256,256]{1,0:T(8,128)(2,1)} %refs_5_.1) | copy-start | bytes 393220
  55.0 2.1 %collective-permute-start.11 = (bf16[8,128,256]{2,1,0:T(8,128)(2,1)S(1)}, bf16[8,128,256]{2,1,0:T(8,128)(2,1)S(1)}, u32[]{:S(2)}, u32[]{:S(2)}) collective-permute-start(bf16[8,128,256]{2,1,0:T(8,128)(2,1)S(1)} %backward_blocks.5), channel_id=1, source_target_pairs={{0,1},{1,0},{2,3},{3,2},{4,5},{5,4},{6,7},{7,6},{8,9},{9,8},{10,11... | collective-permute-start | bytes 1572872 | tf_op jit(solution)/shard_map/ppermute | solution.py:269
  57.3 13.5 %copy-start.9 = (bf16[2,32,128,128]{3,2,1,0:T(8,128)(2,1)S(1)}, bf16[2,32,128,128]{3,2,1,0:T(8,128)(2,1)}, u32[]{:S(2)}) copy-start(bf16[2,32,128,128]{3,2,1,0:T(8,128)(2,1)} %copy-done.7) | copy-start | bytes 6291460
  57.3 2.9 %collective-permute-start.21 = (bf16[1,128,256]{2,1,0:T(8,128)(2,1)S(1)}, bf16[1,128,256]{2,1,0:T(8,128)(2,1)S(1)}, u32[]{:S(2)}, u32[]{:S(2)}) collective-permute-start(bf16[1,128,256]{2,1,0:T(8,128)(2,1)S(1)} %dynamic-slice_bitcast_fusion), channel_id=1, source_target_pairs={{0,1},{1,0},{2,3},{3,2},{4,5},{5,4},{6,7},{7,6},{8,9},{9,8},{10,11... | collective-permute-start | bytes 196616 | tf_op jit(solution)/shard_map/ppermute | solution.py:269
  59.4 10.8 %collective-permute-start.12 = (bf16[8,128,256]{2,1,0:T(8,128)(2,1)S(1)}, bf16[8,128,256]{2,1,0:T(8,128)(2,1)S(1)}, u32[]{:S(2)}, u32[]{:S(2)}) collective-permute-start(bf16[8,128,256]{2,1,0:T(8,128)(2,1)S(1)} %get-tuple-element.38), channel_id=1, source_target_pairs={{0,1},{1,0},{2,3},{3,2},{4,5},{5,4},{6,7},{7,6},{8,9},{9,8},{10,11... | collective-permute-start | bytes 1572872 | tf_op jit(solution)/shard_map/ppermute | solution.py:269
  60.2 7.9 %collective-permute-start.22 = (bf16[1,128,256]{2,1,0:T(8,128)(2,1)S(1)}, bf16[1,128,256]{2,1,0:T(8,128)(2,1)S(1)}, u32[]{:S(2)}, u32[]{:S(2)}) collective-permute-start(bf16[1,128,256]{2,1,0:T(8,128)(2,1)S(1)} %fusion), channel_id=1, source_target_pairs={{0,8},{8,0},{16,24},{24,16},{1,9},{9,1},{17,25},{25,17},{2,10},{10... | collective-permute-start | bytes 196616 | tf_op jit(solution)/shard_map/ppermute | solution.py:277
  62.7 16.9 %collective-permute-start.14 = (bf16[8,128,256]{2,1,0:T(8,128)(2,1)S(1)}, bf16[8,128,256]{2,1,0:T(8,128)(2,1)S(1)}, u32[]{:S(2)}, u32[]{:S(2)}) collective-permute-start(bf16[8,128,256]{2,1,0:T(8,128)(2,1)S(1)} %add_convert_fusion.2), channel_id=1, source_target_pairs={{0,2},{1,3},{6,4},{7,5},{8,10},{9,11},{14,12},{15,13},{16,18},{17,... | collective-permute-start | bytes 1572872 | tf_op jit(solution)/shard_map/ppermute | solution.py:274
  67.4 12.2 %collective-permute-start.15 = (bf16[8,128,256]{2,1,0:T(8,128)(2,1)S(1)}, bf16[8,128,256]{2,1,0:T(8,128)(2,1)S(1)}, u32[]{:S(2)}, u32[]{:S(2)}) collective-permute-start(bf16[8,128,256]{2,1,0:T(8,128)(2,1)S(1)} %add_convert_fusion.2), channel_id=1, source_target_pairs={{2,4},{3,5},{4,2},{5,3},{10,12},{11,13},{12,10},{13,11},{18,20},{1... | collective-permute-start | bytes 1572872 | tf_op jit(solution)/shard_map/ppermute | solution.py:274
  68.2 4.9 %collective-permute-start.23 = (bf16[1,128,256]{2,1,0:T(8,128)(2,1)S(1)}, bf16[1,128,256]{2,1,0:T(8,128)(2,1)S(1)}, u32[]{:S(2)}, u32[]{:S(2)}) collective-permute-start(bf16[1,128,256]{2,1,0:T(8,128)(2,1)S(1)} %add_convert_fusion.6), channel_id=1, source_target_pairs={{0,16},{8,24},{16,0},{24,8},{1,17},{9,25},{17,1},{25,9},{2,18},{10... | collective-permute-start | bytes 196616 | tf_op jit(solution)/shard_map/ppermute | solution.py:277
  70.2 13.1 %collective-permute-start.13 = (bf16[8,128,256]{2,1,0:T(8,128)(2,1)S(1)}, bf16[8,128,256]{2,1,0:T(8,128)(2,1)S(1)}, u32[]{:S(2)}, u32[]{:S(2)}) collective-permute-start(bf16[8,128,256]{2,1,0:T(8,128)(2,1)S(1)} %pad_maximum_fusion), channel_id=1, source_target_pairs={{0,8},{8,0},{16,24},{24,16},{1,9},{9,1},{17,25},{25,17},{2,10},{10... | collective-permute-start | bytes 1572872 | tf_op jit(solution)/shard_map/ppermute | solution.py:277
  73.0 15.8 %collective-permute-start.18 = (bf16[8,128,256]{2,1,0:T(8,128)(2,1)S(1)}, bf16[8,128,256]{2,1,0:T(8,128)(2,1)S(1)}, u32[]{:S(2)}, u32[]{:S(2)}) collective-permute-start(bf16[8,128,256]{2,1,0:T(8,128)(2,1)S(1)} %get-tuple-element.45), channel_id=1, source_target_pairs={{0,1},{1,0},{2,3},{3,2},{4,5},{5,4},{6,7},{7,6},{8,9},{9,8},{10,11... | collective-permute-start | bytes 1572872 | tf_op jit(solution)/shard_map/ppermute | solution.py:269
  73.1 12.1 %collective-permute-start.24 = (bf16[1,128,256]{2,1,0:T(8,128)(2,1)S(1)}, bf16[1,128,256]{2,1,0:T(8,128)(2,1)S(1)}, u32[]{:S(2)}, u32[]{:S(2)}) collective-permute-start(bf16[1,128,256]{2,1,0:T(8,128)(2,1)S(1)} %add_convert_fusion.5), channel_id=1, source_target_pairs={{0,4},{1,5},{2,6},{3,7},{4,0},{5,1},{6,2},{7,3},{8,12},{9,13},{10,... | collective-permute-start | bytes 196616 | tf_op jit(solution)/shard_map/ppermute | solution.py:274
  83.4 12.4 %copy-start.4 = (s32[4,1,16,1]{2,3,1,0:T(1,128)S(1)}, s32[4,1,16,1]{2,3,1,0:T(1,128)}, u32[]{:S(2)}) copy-start(s32[4,1,16,1]{2,3,1,0:T(1,128)} %param.22) | copy-start | bytes 772
  83.4 12.4 %copy-start.6 = (bf16[2,32,128,128]{3,2,1,0:T(8,128)(2,1)S(1)}, bf16[2,32,128,128]{3,2,1,0:T(8,128)(2,1)}, u32[]{:S(2)}) copy-start(bf16[2,32,128,128]{3,2,1,0:T(8,128)(2,1)} %copy-done.5) | copy-start | bytes 6291460
  83.4 12.4 %copy-start.14 = (bf16[1,1,16,128,128]{4,3,2,1,0:T(8,128)(2,1)S(1)}, bf16[1,1,16,128,128]{4,3,2,1,0:T(8,128)(2,1)}, u32[]{:S(2)}) copy-start(bf16[1,1,16,128,128]{4,3,2,1,0:T(8,128)(2,1)} %param.20) | copy-start | bytes 1572868
  83.4 12.4 %copy-start.16 = (s32[1,1,16]{2,1,0:T(1,128)S(1)}, s32[1,1,16]{2,1,0:T(1,128)}, u32[]{:S(2)}) copy-start(s32[1,1,16]{2,1,0:T(1,128)} %param.21) | copy-start | bytes 196
  83.5 12.2 %collective-permute-start.16 = (bf16[8,128,256]{2,1,0:T(8,128)(2,1)S(1)}, bf16[8,128,256]{2,1,0:T(8,128)(2,1)S(1)}, u32[]{:S(2)}, u32[]{:S(2)}) collective-permute-start(bf16[8,128,256]{2,1,0:T(8,128)(2,1)S(1)} %pad_maximum_fusion.1), channel_id=1, source_target_pairs={{0,16},{8,24},{16,0},{24,8},{1,17},{9,25},{17,1},{25,9},{2,18},{10... | collective-permute-start | bytes 1572872 | tf_op jit(solution)/shard_map/ppermute | solution.py:277
  85.2 14.7 %collective-permute-start.25 = (bf16[1,128,256]{2,1,0:T(8,128)(2,1)S(1)}, bf16[1,128,256]{2,1,0:T(8,128)(2,1)S(1)}, u32[]{:S(2)}, u32[]{:S(2)}) collective-permute-start(bf16[1,128,256]{2,1,0:T(8,128)(2,1)S(1)} %add_convert_fusion.4), channel_id=1, source_target_pairs={{0,2},{1,3},{2,0},{3,1},{4,6},{5,7},{6,4},{7,5},{8,10},{9,11},{10,... | collective-permute-start | bytes 196616 | tf_op jit(solution)/shard_map/ppermute | solution.py:274
  87.7 23.5 %collective-permute-start.17 = (bf16[8,128,256]{2,1,0:T(8,128)(2,1)}, bf16[8,128,256]{2,1,0:T(8,128)(2,1)S(1)}, u32[]{:S(2)}, u32[]{:S(2)}) collective-permute-start(bf16[8,128,256]{2,1,0:T(8,128)(2,1)} %add_convert_fusion.1), channel_id=1, source_target_pairs={{0,4},{1,5},{2,6},{3,7},{4,0},{5,1},{6,2},{7,3},{8,12},{9,13},{10,... | collective-permute-start | bytes 1572872 | tf_op jit(solution)/shard_map/ppermute | solution.py:274
  89.8 21.4 %collective-permute-start.19 = (bf16[8,128,256]{2,1,0:T(8,128)(2,1)}, bf16[8,128,256]{2,1,0:T(8,128)(2,1)S(1)}, u32[]{:S(2)}, u32[]{:S(2)}) collective-permute-start(bf16[8,128,256]{2,1,0:T(8,128)(2,1)} %add_convert_fusion), channel_id=1, source_target_pairs={{0,2},{1,3},{2,0},{3,1},{4,6},{5,7},{6,4},{7,5},{8,10},{9,11},{10,... | collective-permute-start | bytes 1572872 | tf_op jit(solution)/shard_map/ppermute | solution.py:274
  95.8 15.4 %copy-start.1 = (bf16[256,256]{1,0:T(8,128)(2,1)S(1)}, bf16[256,256]{1,0:T(8,128)(2,1)}, u32[]{:S(2)}) copy-start(bf16[256,256]{1,0:T(8,128)(2,1)} %refs_5_.1) | copy-start | bytes 393220
  99.9 11.3 %collective-permute-start.20 = (bf16[8,128,256]{2,1,0:T(8,128)(2,1)}, bf16[8,128,256]{2,1,0:T(8,128)(2,1)S(1)}, u32[]{:S(2)}, u32[]{:S(2)}) collective-permute-start(bf16[8,128,256]{2,1,0:T(8,128)(2,1)} %get-tuple-element.46), channel_id=1, source_target_pairs={{0,1},{1,0},{2,3},{3,2},{4,5},{5,4},{6,7},{7,6},{8,9},{9,8},{10,11... | collective-permute-start | bytes 1572872 | tf_op jit(solution)/shard_map/ppermute | solution.py:269
  100.6 1.7 %collective-permute-start.26 = (f32[1,128,256]{2,1,0:T(8,128)}, f32[1,128,256]{2,1,0:T(8,128)S(1)}, u32[]{:S(2)}, u32[]{:S(2)}) collective-permute-start(f32[1,128,256]{2,1,0:T(8,128)} %convert_multiply_fusion), channel_id=1, source_target_pairs={{0,1},{1,0},{2,3},{3,2},{4,5},{5,4},{6,7},{7,6},{8,9},{9,8},{10,11... | collective-permute-start | bytes 393224 | tf_op jit(solution)/shard_map/ppermute | solution.py:269
